TPU v7x, 256 devices: a whole 4x4x8 slice. The times are simulated.
256 devices in a mesh: dp: 32 (over x, z), seq: 8 (over y, core).
Axes of the slice: x: 4, y: 4, z: 8, core: 2. Of those that a mesh axis runs over, the one named last changes fastest.
Arguments:
- queries: bfloat16 [32768, 3072], P(('dp', 'seq')), may hold values from -150 to 150
- key_rows: bfloat16 [32768, 3072], P(('dp', 'seq')), may hold values from -5 to 5
- values: bfloat16 [32768, 3072], P(('dp', 'seq')), may hold values from -6 to 6
- target: bfloat16 [32768, 3072], P(('dp', 'seq')), may hold values from -18 to 18
- row_clip: int32 [32768], P(('dp', 'seq')), may hold values from -1 to 1, as said below
- ratios: float32 [32, 2], P('dp'), may hold values from 0.5 to 2
- ref_loss: float32 [32, 2], P('dp'), may hold values from 0.5 to 4
- noise_level: int32 [1], replicated, may hold values from 0 to 999
Outputs:
- grad_queries: bfloat16 [32768, 3072], P(('dp', 'seq'))
- grad_keys: bfloat16 [32768, 3072], P(('dp', 'seq'))
- grad_values: bfloat16 [32768, 3072], P(('dp', 'seq'))
- clip_loss: float32 [32, 2], P('dp')
Inputs may be any that keep to these rules, and one draw needn't show every extreme that they name: `row_clip`: the rows a device sends to group g are rows g * 4 to (g+1) * 4 - 1 of its block, used rows first, at least two fifths of them used; every clip of every group has rows.
All inputs are finite; a program needn't handle non-finite values.
Results may differ from a plain program's by a relative error of at most 0.0058.
Values may be sent and summed in bfloat16 or wider, within the bound.
No kernel may reach another device: no remote copies, remote signals or barrier semaphores. Data moves between devices by JAX's collectives and lax.ppermute only.
A program may use at most 64 MiB of HBM per device.

v0:
```python
import jax
import jax.numpy as jnp
from jax import lax
from jax.sharding import PartitionSpec as P

HEADS = 24
HD = 128
CLIPS_G = 2
LEVELS = 1000


NEG_FILL = -1e30
SHIFT_FACTOR = 5.0
LOSS_SCALE = 2.0**21


def level_weight(noise_level):
    fraction = 1.0 - noise_level[0].astype(jnp.float32) / LEVELS
    sigma = SHIFT_FACTOR * fraction / (1.0 + (SHIFT_FACTOR - 1.0) * fraction)
    return 1.0 / (sigma * sigma + (1.0 - sigma) * (1.0 - sigma))


def head_probs(query_head, key_head, allowed):
    scores = jnp.dot(query_head, key_head.T, preferred_element_type=jnp.float32) * HD ** (-0.5)
    scores = jnp.where(allowed, scores, NEG_FILL)
    largest = jnp.max(scores, axis=1, keepdims=True)
    expo = jnp.exp(scores - largest)
    return expo / jnp.sum(expo, axis=1, keepdims=True)


def head_forward(query_head, key_head, value_head, allowed):
    probs = head_probs(query_head, key_head, allowed)
    return jnp.dot(probs.astype(jnp.bfloat16), value_head, preferred_element_type=jnp.float32)


def head_backward(query_head, key_head, value_head, grad_head, allowed):
    probs = head_probs(query_head, key_head, allowed)
    probs_low = probs.astype(jnp.bfloat16)
    grad_probs = jnp.dot(grad_head, value_head.T, preferred_element_type=jnp.float32)
    grad_value = jnp.dot(probs_low.T, grad_head, preferred_element_type=jnp.float32)
    inner = jnp.sum(probs * grad_probs, axis=1, keepdims=True)
    grad_scores = (probs * (grad_probs - inner)).astype(jnp.bfloat16)
    grad_query = jnp.dot(grad_scores, key_head, preferred_element_type=jnp.float32) * HD ** (-0.5)
    grad_key = jnp.dot(grad_scores.T, query_head, preferred_element_type=jnp.float32) * HD ** (-0.5)
    return (
        grad_query.astype(jnp.bfloat16),
        grad_key.astype(jnp.bfloat16),
        grad_value.astype(jnp.bfloat16),
    )


def shards(queries, key_rows, values, target, row_clip, ratios, ref_loss, noise_level):
    groups = lax.axis_size("dp")
    seq_size = lax.axis_size("seq")
    tok_rows = queries.shape[0]
    cap_rows = tok_rows // groups
    local_heads = HEADS // seq_size
    layout = (groups, cap_rows, seq_size, local_heads, HD)
    query_in = queries.reshape(layout)
    key_in = key_rows.reshape(layout)
    value_in = values.reshape(layout)
    target_in = target.reshape(layout)
    labels = jnp.broadcast_to(
        row_clip.astype(jnp.bfloat16).reshape(groups, cap_rows, 1), (groups, cap_rows, seq_size)
    )
    arrived = (
        lax.all_to_all(query_in, "dp", split_axis=0, concat_axis=0, tiled=True),
        lax.all_to_all(key_in, "dp", split_axis=0, concat_axis=0, tiled=True),
        lax.all_to_all(value_in, "dp", split_axis=0, concat_axis=0, tiled=True),
        lax.all_to_all(target_in, "dp", split_axis=0, concat_axis=0, tiled=True),
        lax.all_to_all(labels, "dp", split_axis=0, concat_axis=0, tiled=True),
    )
    arrived = (
        lax.all_to_all(arrived[0], "seq", split_axis=2, concat_axis=0, tiled=True),
        lax.all_to_all(arrived[1], "seq", split_axis=2, concat_axis=0, tiled=True),
        lax.all_to_all(arrived[2], "seq", split_axis=2, concat_axis=0, tiled=True),
        lax.all_to_all(arrived[3], "seq", split_axis=2, concat_axis=0, tiled=True),
        lax.all_to_all(arrived[4], "seq", split_axis=2, concat_axis=0, tiled=True),
    )
    lead_dim = arrived[0].shape[0]
    mid_dim = arrived[0].shape[1]
    total_rows = lead_dim * mid_dim
    query_heads = jnp.swapaxes(arrived[0].reshape(total_rows, local_heads, HD), 0, 1)
    key_heads = jnp.swapaxes(arrived[1].reshape(total_rows, local_heads, HD), 0, 1)
    value_heads = jnp.swapaxes(arrived[2].reshape(total_rows, local_heads, HD), 0, 1)
    target_heads = jnp.swapaxes(arrived[3].reshape(total_rows, local_heads, HD), 0, 1)
    clip_ids = arrived[4].reshape(total_rows).astype(jnp.int32)
    allowed = (clip_ids[:, None] == clip_ids[None, :]) & (clip_ids[None, :] >= 0)

    def forward_one(trio):
        return head_forward(trio[0], trio[1], trio[2], allowed)

    output = lax.map(forward_one, (query_heads, key_heads, value_heads))
    error = output - target_heads.astype(jnp.float32)
    row_squares = jnp.sum(error * error, axis=(0, 2))
    onehot = (clip_ids[:, None] == jnp.arange(CLIPS_G, dtype=jnp.int32)[None, :]).astype(
        jnp.float32
    )
    partial_sums = jnp.sum(onehot * row_squares[:, None], axis=0)
    counts = jnp.sum(onehot, axis=0)
    sums = lax.psum(partial_sums, "seq")
    width = HEADS * HD
    weight_level = level_weight(noise_level)
    loss = weight_level * sums / (counts * width)
    weight = ratios[0] * loss / ref_loss[0]
    coef = weight_level * weight * 2.0 * LOSS_SCALE / (counts * width)
    coef_row = jnp.sum(onehot * coef[None, :], axis=1)
    grad_out = (coef_row[None, :, None] * error).astype(jnp.bfloat16)

    def backward_one(quad):
        return head_backward(quad[0], quad[1], quad[2], quad[3], allowed)

    grad_query, grad_key, grad_value = lax.map(
        backward_one, (query_heads, key_heads, value_heads, grad_out)
    )
    back_shape = (lead_dim, mid_dim, 1, local_heads, HD)
    grad_query = jnp.swapaxes(grad_query, 0, 1).reshape(back_shape)
    grad_key = jnp.swapaxes(grad_key, 0, 1).reshape(back_shape)
    grad_value = jnp.swapaxes(grad_value, 0, 1).reshape(back_shape)
    returned = (
        lax.all_to_all(grad_query, "seq", split_axis=0, concat_axis=2, tiled=True),
        lax.all_to_all(grad_key, "seq", split_axis=0, concat_axis=2, tiled=True),
        lax.all_to_all(grad_value, "seq", split_axis=0, concat_axis=2, tiled=True),
    )
    returned = (
        lax.all_to_all(returned[0], "dp", split_axis=0, concat_axis=0, tiled=True),
        lax.all_to_all(returned[1], "dp", split_axis=0, concat_axis=0, tiled=True),
        lax.all_to_all(returned[2], "dp", split_axis=0, concat_axis=0, tiled=True),
    )
    full_width = seq_size * local_heads * HD
    return (
        returned[0].reshape(tok_rows, full_width),
        returned[1].reshape(tok_rows, full_width),
        returned[2].reshape(tok_rows, full_width),
        loss[None, :],
    )


def solution(mesh):
    placed = (
        P(("dp", "seq"), None),
        P(("dp", "seq"), None),
        P(("dp", "seq"), None),
        P(("dp", "seq"), None),
        P(("dp", "seq")),
        P("dp", None),
        P("dp", None),
        P(),
    )
    return jax.shard_map(
        shards,
        mesh=mesh,
        in_specs=placed,
        out_specs=(
            P(("dp", "seq"), None),
            P(("dp", "seq"), None),
            P(("dp", "seq"), None),
            P("dp", None),
        ),
        check_vma=False,
    )
```

profile of v0, /device:TPU:1, one launch (start us, length us, event | category | flops | bytes accessed | tf_op | source)
XLA Modules:
  0.0 425.9 jit_solution(8752961556817146489)
XLA Ops:
  1.6 20.4 %all_to_all.157 = bf16[32,4,8]{2,1,0:T(4,128)(2,1)S(1)} all-to-all(bf16[32,4,8]{2,1,0:T(4,128)(2,1)S(1)} %broadcast_in_dim.48), channel_id=1, replica_groups=mesh['dp'=32,'seq'=8] {'dp'}, dimensions={0} | all-to-all | bytes 4096 | tf_op jit(solution)/shard_map/all_to_all | solution.py:71
  22.7 6.6 %all-to-all-start.5 = ((bf16[32,4,8]{0,1,2:T(4,128)(2,1)}), bf16[32,4,8]{0,1,2:T(4,128)(2,1)S(1)}, u32[]{:S(2)}, u32[]{:S(2)}) async-start(bf16[32,4,8]{0,1,2:T(4,128)(2,1)} %copy.61), calls=%async_computation.5 | async-start | bytes 16384 | tf_op jit(solution)/shard_map/all_to_all | solution.py:78
  29.3 2.7 reshape.100
  33.9 3.9 all-to-all-start.6
  40.0 16.6 %all-to-all-done.6 = bf16[32,4,8,3,128]{4,2,3,1,0:T(8,128)(2,1)S(1)} async-done(((bf16[32,4,8,3,128]{4,2,3,1,0:T(8,128)(2,1)}), bf16[32,4,8,3,128]{4,2,3,1,0:T(8,128)(2,1)S(1)}, u32[]{:S(2)}, u32[]{:S(2)}) %all-to-all-start.6) | async-done | bytes 786464 | tf_op jit(solution)/shard_map/all_to_all | solution.py:69
  56.7 8.9 %all-to-all-start = ((bf16[32,4,8,3,128]{4,2,3,1,0:T(8,128)(2,1)}), bf16[32,4,8,3,128]{4,2,3,1,0:T(8,128)(2,1)S(1)}, u32[]{:S(2)}, u32[]{:S(2)}) async-start(bf16[32,4,8,3,128]{4,2,3,1,0:T(8,128)(2,1)} %copy.55), calls=%async_computation | async-start | bytes 1572864 | tf_op jit(solution)/shard_map/all_to_all | solution.py:67
  67.8 17.6 %all-to-all-done = bf16[32,4,8,3,128]{4,2,3,1,0:T(8,128)(2,1)S(1)} async-done(((bf16[32,4,8,3,128]{4,2,3,1,0:T(8,128)(2,1)}), bf16[32,4,8,3,128]{4,2,3,1,0:T(8,128)(2,1)S(1)}, u32[]{:S(2)}, u32[]{:S(2)}) %all-to-all-start) | async-done | bytes 786464 | tf_op jit(solution)/shard_map/all_to_all | solution.py:67
  85.4 7.6 %all-to-all-start.2 = ((bf16[32,4,8,3,128]{4,2,3,1,0:T(8,128)(2,1)}), bf16[32,4,8,3,128]{4,2,3,1,0:T(8,128)(2,1)S(1)}, u32[]{:S(2)}, u32[]{:S(2)}) async-start(bf16[32,4,8,3,128]{4,2,3,1,0:T(8,128)(2,1)} %copy.58), calls=%async_computation.2 | async-start | bytes 1572864 | tf_op jit(solution)/shard_map/all_to_all | solution.py:68
  93.0 2.7 reshape.102
  96.8 15.9 %all-to-all-done.2 = bf16[32,4,8,3,128]{4,2,3,1,0:T(8,128)(2,1)S(1)} async-done(((bf16[32,4,8,3,128]{4,2,3,1,0:T(8,128)(2,1)}), bf16[32,4,8,3,128]{4,2,3,1,0:T(8,128)(2,1)S(1)}, u32[]{:S(2)}, u32[]{:S(2)}) %all-to-all-start.2) | async-done | bytes 786464 | tf_op jit(solution)/shard_map/all_to_all | solution.py:68
  113.6 7.6 %all-to-all-start.8 = ((bf16[32,4,8,3,128]{4,2,3,1,0:T(8,128)(2,1)}), bf16[32,4,8,3,128]{4,2,3,1,0:T(8,128)(2,1)S(1)}, u32[]{:S(2)}, u32[]{:S(2)}) async-start(bf16[32,4,8,3,128]{4,2,3,1,0:T(8,128)(2,1)} %copy.66), calls=%async_computation.8 | async-start | bytes 1572864 | tf_op jit(solution)/shard_map/all_to_all | solution.py:70
  122.3 17.6 %all-to-all-done.8 = bf16[32,4,8,3,128]{4,2,3,1,0:T(8,128)(2,1)S(1)} async-done(((bf16[32,4,8,3,128]{4,2,3,1,0:T(8,128)(2,1)}), bf16[32,4,8,3,128]{4,2,3,1,0:T(8,128)(2,1)S(1)}, u32[]{:S(2)}, u32[]{:S(2)}) %all-to-all-start.8) | async-done | bytes 786464 | tf_op jit(solution)/shard_map/all_to_all | solution.py:70
  139.9 9.3 %all-to-all-start.7 = ((bf16[32,4,8,3,128]{4,0,3,1,2:T(8,128)(2,1)}), bf16[32,4,8,3,128]{4,0,3,1,2:T(8,128)(2,1)S(1)}, u32[]{:S(2)}, u32[]{:S(2)}) async-start(bf16[32,4,8,3,128]{4,0,3,1,2:T(8,128)(2,1)} %copy.64), calls=%async_computation.7 | async-start | bytes 1572864 | tf_op jit(solution)/shard_map/all_to_all | solution.py:76
  150.4 11.1 %all-to-all-done.7 = bf16[32,4,8,3,128]{4,0,3,1,2:T(8,128)(2,1)S(1)} async-done(((bf16[32,4,8,3,128]{4,0,3,1,2:T(8,128)(2,1)}), bf16[32,4,8,3,128]{4,0,3,1,2:T(8,128)(2,1)S(1)}, u32[]{:S(2)}, u32[]{:S(2)}) %all-to-all-start.7) | async-done | bytes 786464 | tf_op jit(solution)/shard_map/all_to_all | solution.py:76
  161.5 4.3 %all-to-all-start.1 = ((bf16[32,4,8,3,128]{4,0,3,1,2:T(8,128)(2,1)}), bf16[32,4,8,3,128]{4,0,3,1,2:T(8,128)(2,1)S(1)}, u32[]{:S(2)}, u32[]{:S(2)}) async-start(bf16[32,4,8,3,128]{4,0,3,1,2:T(8,128)(2,1)} %copy.56), calls=%async_computation.1 | async-start | bytes 1572864 | tf_op jit(solution)/shard_map/all_to_all | solution.py:74
  168.1 10.0 %all-to-all-done.1 = bf16[32,4,8,3,128]{4,0,3,1,2:T(8,128)(2,1)S(1)} async-done(((bf16[32,4,8,3,128]{4,0,3,1,2:T(8,128)(2,1)}), bf16[32,4,8,3,128]{4,0,3,1,2:T(8,128)(2,1)S(1)}, u32[]{:S(2)}, u32[]{:S(2)}) %all-to-all-start.1) | async-done | bytes 786464 | tf_op jit(solution)/shard_map/all_to_all | solution.py:74
  178.1 4.3 %all-to-all-start.3 = ((bf16[32,4,8,3,128]{4,0,3,1,2:T(8,128)(2,1)}), bf16[32,4,8,3,128]{4,0,3,1,2:T(8,128)(2,1)S(1)}, u32[]{:S(2)}, u32[]{:S(2)}) async-start(bf16[32,4,8,3,128]{4,0,3,1,2:T(8,128)(2,1)} %copy.59), calls=%async_computation.3 | async-start | bytes 1572864 | tf_op jit(solution)/shard_map/all_to_all | solution.py:75
  186.4 8.4 %all-to-all-done.3 = bf16[32,4,8,3,128]{4,0,3,1,2:T(8,128)(2,1)S(1)} async-done(((bf16[32,4,8,3,128]{4,0,3,1,2:T(8,128)(2,1)}), bf16[32,4,8,3,128]{4,0,3,1,2:T(8,128)(2,1)S(1)}, u32[]{:S(2)}, u32[]{:S(2)}) %all-to-all-start.3) | async-done | bytes 786464 | tf_op jit(solution)/shard_map/all_to_all | solution.py:75
  194.7 4.3 %all-to-all-start.9 = ((bf16[32,4,8,3,128]{4,0,3,1,2:T(8,128)(2,1)}), bf16[32,4,8,3,128]{4,0,3,1,2:T(8,128)(2,1)S(1)}, u32[]{:S(2)}, u32[]{:S(2)}) async-start(bf16[32,4,8,3,128]{4,0,3,1,2:T(8,128)(2,1)} %copy.67), calls=%async_computation.9 | async-start | bytes 1572864 | tf_op jit(solution)/shard_map/all_to_all | solution.py:77
  200.3 23.1 %while.26 = (s32[]{:T(128)}, f32[3,1024,128]{2,1,0:T(8,128)}, bf16[3,1024,128]{2,1,0:T(8,128)(2,1)S(1)}, bf16[3,1024,128]{2,1,0:T(8,128)(2,1)}, bf16[3,1024,128]...) while((s32[]{:T(128)}, f32[3,1024,128]{2,1,0:T(8,128)}, ...), condition=%wide.region_3.4_spmd.clone, body=%wide.region_0.3_spmd.clone.sunk | while | flops 555743232 | bytes 13939797 | solution.py:93
  204.4 3.6 fusion.82
  212.1 3.6 fusion.82
  219.9 3.6 fusion.82
  225.6 12.4 %psum.7 = f32[2]{0:T(128)S(1)} all-reduce(f32[2]{0:T(128)S(1)} %get-tuple-element.132), channel_id=1, replica_groups=mesh['dp'=32,'seq'=8] {'seq'}, use_global_device_ids=true, to_apply=%region_6.7 | all-reduce | flops 2 | bytes 16 | tf_op jit(solution)/shard_map/psum | solution.py:101
  238.9 52.1 %while.27 = (s32[]{:T(128)}, bf16[3,1024,128]{2,1,0:T(8,128)(2,1)}, bf16[3,1024,128]{2,1,0:T(8,128)(2,1)}, bf16[3,1024,128]{2,1,0:T(8,128)(2,1)}, bf16[3,1024,12...) while((s32[]{:T(128)}, bf16[3,1024,128]{2,1,0:T(8,128)(2,1)}, ...), condition=%wide.region_13.14_spmd.clone, body=%wide.region_9.13_spmd.clone.sunk | while | flops 1379529728 | bytes 44652708 | solution.py:113
  238.9 2.5 fusion.89
  243.1 2.8 fusion.93
  245.9 3.1 multiply_reduce_fusion.3
  256.3 2.5 fusion.89
  260.5 2.8 fusion.93
  263.3 3.1 multiply_reduce_fusion.3
  268.6 2.4 fusion.92
  273.7 2.5 fusion.89
  277.9 2.8 fusion.93
  280.7 3.1 multiply_reduce_fusion.3
  291.0 2.4 copy.69
  293.4 6.7 %all-to-all-start.10 = ((bf16[256,4,1,3,128]{4,1,3,2,0:T(4,128)(2,1)}), bf16[256,4,1,3,128]{4,1,3,2,0:T(4,128)(2,1)S(1)}, u32[]{:S(2)}, u32[]{:S(2)}) async-start(bf16[256,4,1,3,128]{4,1,3,2,0:T(4,128)(2,1)} %copy.69), calls=%async_computation.10 | async-start | bytes 1572864 | tf_op jit(solution)/shard_map/all_to_all | solution.py:121
  302.3 10.0 %all-to-all-done.10 = bf16[256,4,1,3,128]{4,1,3,2,0:T(4,128)(2,1)S(1)} async-done(((bf16[256,4,1,3,128]{4,1,3,2,0:T(4,128)(2,1)}), bf16[256,4,1,3,128]{4,1,3,2,0:T(4,128)(2,1)S(1)}, u32[]{:S(2)}, u32[]{:S(2)}) %all-to-all-start.10) | async-done | bytes 786464 | tf_op jit(solution)/shard_map/all_to_all | solution.py:121
  312.4 4.3 %all-to-all-start.12 = ((bf16[256,4,1,3,128]{4,1,3,2,0:T(4,128)(2,1)}), bf16[256,4,1,3,128]{4,1,3,2,0:T(4,128)(2,1)S(1)}, u32[]{:S(2)}, u32[]{:S(2)}) async-start(bf16[256,4,1,3,128]{4,1,3,2,0:T(4,128)(2,1)} %copy.73), calls=%async_computation.12 | async-start | bytes 1572864 | tf_op jit(solution)/shard_map/all_to_all | solution.py:122
  317.9 11.2 %all-to-all-done.12 = bf16[256,4,1,3,128]{4,1,3,2,0:T(4,128)(2,1)S(1)} async-done(((bf16[256,4,1,3,128]{4,1,3,2,0:T(4,128)(2,1)}), bf16[256,4,1,3,128]{4,1,3,2,0:T(4,128)(2,1)S(1)}, u32[]{:S(2)}, u32[]{:S(2)}) %all-to-all-start.12) | async-done | bytes 786464 | tf_op jit(solution)/shard_map/all_to_all | solution.py:122
  329.0 4.3 %all-to-all-start.14 = ((bf16[256,4,1,3,128]{4,1,3,2,0:T(4,128)(2,1)}), bf16[256,4,1,3,128]{4,1,3,2,0:T(4,128)(2,1)S(1)}, u32[]{:S(2)}, u32[]{:S(2)}) async-start(bf16[256,4,1,3,128]{4,1,3,2,0:T(4,128)(2,1)} %copy.77), calls=%async_computation.14 | async-start | bytes 1572864 | tf_op jit(solution)/shard_map/all_to_all | solution.py:123
  334.7 11.0 %all-to-all-done.14 = bf16[256,4,1,3,128]{4,1,3,2,0:T(4,128)(2,1)S(1)} async-done(((bf16[256,4,1,3,128]{4,1,3,2,0:T(4,128)(2,1)}), bf16[256,4,1,3,128]{4,1,3,2,0:T(4,128)(2,1)S(1)}, u32[]{:S(2)}, u32[]{:S(2)}) %all-to-all-start.14) | async-done | bytes 786464 | tf_op jit(solution)/shard_map/all_to_all | solution.py:123
  345.6 4.5 %all-to-all-start.11 = ((bf16[32,4,8,3,128]{4,2,3,1,0:T(8,128)(2,1)}), bf16[32,4,8,3,128]{4,2,3,1,0:T(8,128)(2,1)S(1)}, u32[]{:S(2)}, u32[]{:S(2)}) async-start(bf16[32,4,8,3,128]{4,2,3,1,0:T(8,128)(2,1)} %copy.71), calls=%async_computation.11 | async-start | bytes 1572864 | tf_op jit(solution)/shard_map/all_to_all | solution.py:126
  351.5 18.3 %all-to-all-done.11 = bf16[32,4,8,3,128]{4,2,3,1,0:T(8,128)(2,1)S(1)} async-done(((bf16[32,4,8,3,128]{4,2,3,1,0:T(8,128)(2,1)}), bf16[32,4,8,3,128]{4,2,3,1,0:T(8,128)(2,1)S(1)}, u32[]{:S(2)}, u32[]{:S(2)}) %all-to-all-start.11) | async-done | bytes 786464 | tf_op jit(solution)/shard_map/all_to_all | solution.py:126
  369.9 7.9 %all-to-all-start.13 = ((bf16[32,4,8,3,128]{4,2,3,1,0:T(8,128)(2,1)}), bf16[32,4,8,3,128]{4,2,3,1,0:T(8,128)(2,1)S(1)}, u32[]{:S(2)}, u32[]{:S(2)}) async-start(bf16[32,4,8,3,128]{4,2,3,1,0:T(8,128)(2,1)} %copy.75), calls=%async_computation.13 | async-start | bytes 1572864 | tf_op jit(solution)/shard_map/all_to_all | solution.py:127
  379.1 18.4 %all-to-all-done.13 = bf16[32,4,8,3,128]{4,2,3,1,0:T(8,128)(2,1)S(1)} async-done(((bf16[32,4,8,3,128]{4,2,3,1,0:T(8,128)(2,1)}), bf16[32,4,8,3,128]{4,2,3,1,0:T(8,128)(2,1)S(1)}, u32[]{:S(2)}, u32[]{:S(2)}) %all-to-all-start.13) | async-done | bytes 786464 | tf_op jit(solution)/shard_map/all_to_all | solution.py:127
  397.6 7.8 %all-to-all-start.15 = ((bf16[32,4,8,3,128]{4,2,3,1,0:T(8,128)(2,1)}), bf16[32,4,8,3,128]{4,2,3,1,0:T(8,128)(2,1)S(1)}, u32[]{:S(2)}, u32[]{:S(2)}) async-start(bf16[32,4,8,3,128]{4,2,3,1,0:T(8,128)(2,1)} %copy.79), calls=%async_computation.15 | async-start | bytes 1572864 | tf_op jit(solution)/shard_map/all_to_all | solution.py:128
  409.4 14.5 %all-to-all-done.15 = bf16[32,4,8,3,128]{4,2,3,1,0:T(8,128)(2,1)S(1)} async-done(((bf16[32,4,8,3,128]{4,2,3,1,0:T(8,128)(2,1)}), bf16[32,4,8,3,128]{4,2,3,1,0:T(8,128)(2,1)S(1)}, u32[]{:S(2)}, u32[]{:S(2)}) %all-to-all-start.15) | async-done | bytes 786464 | tf_op jit(solution)/shard_map/all_to_all | solution.py:128
  (93 shorter events, 71.9 us)
Async XLA Ops:
  0.6 37.2 %copy-start.2 = (bf16[128,3072]{1,0:T(8,128)(2,1)S(1)}, bf16[128,3072]{1,0:T(8,128)(2,1)}, u32[]{:S(2)}) copy-start(bf16[128,3072]{1,0:T(8,128)(2,1)} %param.12) | copy-start | bytes 2359300
  22.7 11.2 %all-to-all-start.5 = ((bf16[32,4,8]{0,1,2:T(4,128)(2,1)}), bf16[32,4,8]{0,1,2:T(4,128)(2,1)S(1)}, u32[]{:S(2)}, u32[]{:S(2)}) async-start(bf16[32,4,8]{0,1,2:T(4,128)(2,1)} %copy.61), calls=%async_computation.5 | async-start | bytes 16384 | tf_op jit(solution)/shard_map/all_to_all | solution.py:78
  33.1 32.5 %copy-start.3 = (bf16[128,3072]{1,0:T(8,128)(2,1)S(1)}, bf16[128,3072]{1,0:T(8,128)(2,1)}, u32[]{:S(2)}) copy-start(bf16[128,3072]{1,0:T(8,128)(2,1)} %param.13) | copy-start | bytes 2359300
  33.9 22.8 %all-to-all-start.6 = ((bf16[32,4,8,3,128]{4,2,3,1,0:T(8,128)(2,1)}), bf16[32,4,8,3,128]{4,2,3,1,0:T(8,128)(2,1)S(1)}, u32[]{:S(2)}, u32[]{:S(2)}) async-start(bf16[32,4,8,3,128]{4,2,3,1,0:T(8,128)(2,1)} %copy.63), calls=%async_computation.6 | async-start | bytes 1572864 | tf_op jit(solution)/shard_map/all_to_all | solution.py:69
  56.7 28.7 %all-to-all-start = ((bf16[32,4,8,3,128]{4,2,3,1,0:T(8,128)(2,1)}), bf16[32,4,8,3,128]{4,2,3,1,0:T(8,128)(2,1)S(1)}, u32[]{:S(2)}, u32[]{:S(2)}) async-start(bf16[32,4,8,3,128]{4,2,3,1,0:T(8,128)(2,1)} %copy.55), calls=%async_computation | async-start | bytes 1572864 | tf_op jit(solution)/shard_map/all_to_all | solution.py:67
  85.4 27.3 %all-to-all-start.2 = ((bf16[32,4,8,3,128]{4,2,3,1,0:T(8,128)(2,1)}), bf16[32,4,8,3,128]{4,2,3,1,0:T(8,128)(2,1)S(1)}, u32[]{:S(2)}, u32[]{:S(2)}) async-start(bf16[32,4,8,3,128]{4,2,3,1,0:T(8,128)(2,1)} %copy.58), calls=%async_computation.2 | async-start | bytes 1572864 | tf_op jit(solution)/shard_map/all_to_all | solution.py:68
  112.7 0.9 copy-start
  113.6 26.3 %all-to-all-start.8 = ((bf16[32,4,8,3,128]{4,2,3,1,0:T(8,128)(2,1)}), bf16[32,4,8,3,128]{4,2,3,1,0:T(8,128)(2,1)S(1)}, u32[]{:S(2)}, u32[]{:S(2)}) async-start(bf16[32,4,8,3,128]{4,2,3,1,0:T(8,128)(2,1)} %copy.66), calls=%async_computation.8 | async-start | bytes 1572864 | tf_op jit(solution)/shard_map/all_to_all | solution.py:70
  139.9 21.6 %all-to-all-start.7 = ((bf16[32,4,8,3,128]{4,0,3,1,2:T(8,128)(2,1)}), bf16[32,4,8,3,128]{4,0,3,1,2:T(8,128)(2,1)S(1)}, u32[]{:S(2)}, u32[]{:S(2)}) async-start(bf16[32,4,8,3,128]{4,0,3,1,2:T(8,128)(2,1)} %copy.64), calls=%async_computation.7 | async-start | bytes 1572864 | tf_op jit(solution)/shard_map/all_to_all | solution.py:76
  161.5 16.6 %all-to-all-start.1 = ((bf16[32,4,8,3,128]{4,0,3,1,2:T(8,128)(2,1)}), bf16[32,4,8,3,128]{4,0,3,1,2:T(8,128)(2,1)S(1)}, u32[]{:S(2)}, u32[]{:S(2)}) async-start(bf16[32,4,8,3,128]{4,0,3,1,2:T(8,128)(2,1)} %copy.56), calls=%async_computation.1 | async-start | bytes 1572864 | tf_op jit(solution)/shard_map/all_to_all | solution.py:74
  178.1 16.6 %all-to-all-start.3 = ((bf16[32,4,8,3,128]{4,0,3,1,2:T(8,128)(2,1)}), bf16[32,4,8,3,128]{4,0,3,1,2:T(8,128)(2,1)S(1)}, u32[]{:S(2)}, u32[]{:S(2)}) async-start(bf16[32,4,8,3,128]{4,0,3,1,2:T(8,128)(2,1)} %copy.59), calls=%async_computation.3 | async-start | bytes 1572864 | tf_op jit(solution)/shard_map/all_to_all | solution.py:75
  194.7 28.7 %all-to-all-start.9 = ((bf16[32,4,8,3,128]{4,0,3,1,2:T(8,128)(2,1)}), bf16[32,4,8,3,128]{4,0,3,1,2:T(8,128)(2,1)S(1)}, u32[]{:S(2)}, u32[]{:S(2)}) async-start(bf16[32,4,8,3,128]{4,0,3,1,2:T(8,128)(2,1)} %copy.67), calls=%async_computation.9 | async-start | bytes 1572864 | tf_op jit(solution)/shard_map/all_to_all | solution.py:77
  223.5 1.5 copy-start.4
  223.5 1.7 copy-start.1
  223.7 14.4 %copy-start.8 = (f32[1,2]{1,0:T(1,128)S(1)}, f32[1,2]{1,0:T(1,128)}, u32[]{:S(2)}) copy-start(f32[1,2]{1,0:T(1,128)} %param.18) | copy-start | bytes 28
  223.7 14.4 %copy-start.9 = (f32[1,2]{1,0:T(1,128)S(1)}, f32[1,2]{1,0:T(1,128)}, u32[]{:S(2)}) copy-start(f32[1,2]{1,0:T(1,128)} %param.17) | copy-start | bytes 28
  249.1 4.5 %copy-start.5 = (bf16[3,1024,128]{2,1,0:T(8,128)(2,1)S(1)}, bf16[3,1024,128]{2,1,0:T(8,128)(2,1)}, u32[]{:S(2)}) copy-start(bf16[3,1024,128]{2,1,0:T(8,128)(2,1)} %get-tuple-element.329) | copy-start | bytes 2359300 | tf_op jit(solution)/shard_map/while
  255.4 0.9 copy-start.6
  266.4 4.5 %copy-start.5 = (bf16[3,1024,128]{2,1,0:T(8,128)(2,1)S(1)}, bf16[3,1024,128]{2,1,0:T(8,128)(2,1)}, u32[]{:S(2)}) copy-start(bf16[3,1024,128]{2,1,0:T(8,128)(2,1)} %get-tuple-element.329) | copy-start | bytes 2359300 | tf_op jit(solution)/shard_map/while
  272.8 0.9 copy-start.6
  283.8 4.5 %copy-start.5 = (bf16[3,1024,128]{2,1,0:T(8,128)(2,1)S(1)}, bf16[3,1024,128]{2,1,0:T(8,128)(2,1)}, u32[]{:S(2)}) copy-start(bf16[3,1024,128]{2,1,0:T(8,128)(2,1)} %get-tuple-element.329) | copy-start | bytes 2359300 | tf_op jit(solution)/shard_map/while
  290.1 0.9 copy-start.6
  291.0 25.7 %copy-start.7 = (bf16[3,1024,128]{2,1,0:T(8,128)(2,1)S(1)}, bf16[3,1024,128]{2,1,0:T(8,128)(2,1)}, u32[]{:S(2)}) copy-start(bf16[3,1024,128]{2,1,0:T(8,128)(2,1)} %get-tuple-element.88) | copy-start | bytes 2359300
  293.4 19.0 %all-to-all-start.10 = ((bf16[256,4,1,3,128]{4,1,3,2,0:T(4,128)(2,1)}), bf16[256,4,1,3,128]{4,1,3,2,0:T(4,128)(2,1)S(1)}, u32[]{:S(2)}, u32[]{:S(2)}) async-start(bf16[256,4,1,3,128]{4,1,3,2,0:T(4,128)(2,1)} %copy.69), calls=%async_computation.10 | async-start | bytes 1572864 | tf_op jit(solution)/shard_map/all_to_all | solution.py:121
  312.4 16.6 %all-to-all-start.12 = ((bf16[256,4,1,3,128]{4,1,3,2,0:T(4,128)(2,1)}), bf16[256,4,1,3,128]{4,1,3,2,0:T(4,128)(2,1)S(1)}, u32[]{:S(2)}, u32[]{:S(2)}) async-start(bf16[256,4,1,3,128]{4,1,3,2,0:T(4,128)(2,1)} %copy.73), calls=%async_computation.12 | async-start | bytes 1572864 | tf_op jit(solution)/shard_map/all_to_all | solution.py:122
  329.0 16.6 %all-to-all-start.14 = ((bf16[256,4,1,3,128]{4,1,3,2,0:T(4,128)(2,1)}), bf16[256,4,1,3,128]{4,1,3,2,0:T(4,128)(2,1)S(1)}, u32[]{:S(2)}, u32[]{:S(2)}) async-start(bf16[256,4,1,3,128]{4,1,3,2,0:T(4,128)(2,1)} %copy.77), calls=%async_computation.14 | async-start | bytes 1572864 | tf_op jit(solution)/shard_map/all_to_all | solution.py:123
  345.6 24.2 %all-to-all-start.11 = ((bf16[32,4,8,3,128]{4,2,3,1,0:T(8,128)(2,1)}), bf16[32,4,8,3,128]{4,2,3,1,0:T(8,128)(2,1)S(1)}, u32[]{:S(2)}, u32[]{:S(2)}) async-start(bf16[32,4,8,3,128]{4,2,3,1,0:T(8,128)(2,1)} %copy.71), calls=%async_computation.11 | async-start | bytes 1572864 | tf_op jit(solution)/shard_map/all_to_all | solution.py:126
  369.9 27.7 %all-to-all-start.13 = ((bf16[32,4,8,3,128]{4,2,3,1,0:T(8,128)(2,1)}), bf16[32,4,8,3,128]{4,2,3,1,0:T(8,128)(2,1)S(1)}, u32[]{:S(2)}, u32[]{:S(2)}) async-start(bf16[32,4,8,3,128]{4,2,3,1,0:T(8,128)(2,1)} %copy.75), calls=%async_computation.13 | async-start | bytes 1572864 | tf_op jit(solution)/shard_map/all_to_all | solution.py:127
  397.6 26.3 %all-to-all-start.15 = ((bf16[32,4,8,3,128]{4,2,3,1,0:T(8,128)(2,1)}), bf16[32,4,8,3,128]{4,2,3,1,0:T(8,128)(2,1)S(1)}, u32[]{:S(2)}, u32[]{:S(2)}) async-start(bf16[32,4,8,3,128]{4,2,3,1,0:T(8,128)(2,1)} %copy.79), calls=%async_computation.15 | async-start | bytes 1572864 | tf_op jit(solution)/shard_map/all_to_all | solution.py:128
where the time goes:
time: 432 us; the launch traced here: 426 us
  waiting for transfers between devices  181 us (42%)
  starting transfers between devices  92.3 us (21%)
  matrix products  55.8 us (13%)
  local copies, waits for them, and re-layouts  42.7 us (10%)
  blocking collectives  32.9 us (8%)
  other arithmetic  18.8 us (4%)
    all_to_all x1, blocking collectives, shards(): lax.all_to_all(labels, 'dp', split_axis=0, concat_axis=0, tiled=True)  20.4 us
    all_to_all x1, waiting for transfers between devices, shards(): lax.all_to_all(returned[1], 'dp', split_axis=0, concat_axis=0, tiled=True)  18.4 us
    all_to_all x1, waiting for transfers between devices, shards(): lax.all_to_all(returned[0], 'dp', split_axis=0, concat_axis=0, tiled=True)  18.3 us
    all_to_all x1, waiting for transfers between devices, shards(): lax.all_to_all(query_in, 'dp', split_axis=0, concat_axis=0, tiled=True)  17.6 us
    all_to_all x1, waiting for transfers between devices, shards(): lax.all_to_all(target_in, 'dp', split_axis=0, concat_axis=0, tiled=True)  17.6 us
    all_to_all x1, waiting for transfers between devices, shards(): lax.all_to_all(value_in, 'dp', split_axis=0, concat_axis=0, tiled=True)  16.6 us
    all_to_all x1, waiting for transfers between devices, shards(): lax.all_to_all(key_in, 'dp', split_axis=0, concat_axis=0, tiled=True)  15.9 us
    dot_general x6, matrix products, head_probs(): jnp.dot(query_head, key_head.T, preferred_element_type=jnp.float32)  14.6 us
  transfers between devices with their start and end apart: 15, of which 14 were waited for; matrix products, arithmetic and copies ran while one was open for 13% of the time, Pallas kernels for 0%

commit v1 on v0

v1 whole, which is shorter than its diff:
```python
import functools

import jax
import jax.numpy as jnp
from jax import lax
from jax.experimental import pallas as pl
from jax.experimental.pallas import tpu as pltpu
from jax.sharding import PartitionSpec as P

HEADS = 24
HD = 128
CLIPS_G = 2
LEVELS = 1000

SHIFT_FACTOR = 5.0
LOSS_SCALE = 2.0**21
MASK_FILL = 1e30
LOG2E = 1.4426950408889634
WIDTH = HEADS * HD

CAP = 4
IN_PIECES = 13
OUT_PIECES = 10
BLOCK = 256


def level_weight(noise_level):
    fraction = 1.0 - noise_level[0].astype(jnp.float32) / LEVELS
    sigma = SHIFT_FACTOR * fraction / (1.0 + (SHIFT_FACTOR - 1.0) * fraction)
    return 1.0 / (sigma * sigma + (1.0 - sigma) * (1.0 - sigma))


def low_half(shape=(8, HD)):
    return lax.broadcasted_iota(jnp.int32, shape, 0) % 8 < CAP


def swap(tile):
    return pltpu.roll(tile, CAP, 0)


def pack_kernel(q_ref, k_ref, v_ref, t_ref, clip_ref, out_ref):
    low = low_half()
    tensors = [ref[...].astype(jnp.float32) for ref in (q_ref, k_ref, v_ref, t_ref)]
    step = pl.program_id(0)
    rows = q_ref.shape[0]
    pick = lax.broadcasted_iota(jnp.int32, (rows, HD), 0) + step * rows
    lane = lax.broadcasted_iota(jnp.int32, (rows, HD), 1)
    labels = jnp.sum(
        jnp.where(pick == lane, jnp.broadcast_to(clip_ref[...].astype(jnp.float32), (rows, HD)), 0.0),
        axis=1,
        keepdims=True,
    )
    labels = jnp.broadcast_to(labels, (rows, HD))
    seq_size = tensors[0].shape[1] // (3 * HD)
    for tile in range(rows // 8):
        at = slice(tile * 8, tile * 8 + 8)
        label_tile = labels[at]
        for half in range(2):
            made = []
            for dest in range(seq_size):
                pieces = []
                for head in range(3):
                    col = (dest * 3 + head) * HD
                    for tensor in tensors:
                        pieces.append(tensor[at, col : col + HD])
                pieces.append(label_tile)
                made.extend(pieces)
            tiles = []
            for first, second in zip(made[::2], made[1::2]):
                if half == 0:
                    tiles.append(jnp.where(low, first, swap(second)))
                else:
                    tiles.append(jnp.where(low, swap(first), second))
            count = 8 * len(tiles)
            start = (tile * 2 + half) * count
            out_ref[start : start + count, :] = jnp.concatenate(tiles, axis=0).astype(jnp.bfloat16)


def pack(queries, key_rows, values, target, clip_row):
    tok_rows, width = queries.shape
    steps = 4
    rows = tok_rows // steps
    spec = pl.BlockSpec((rows, width), lambda i: (i, 0))
    out_rows = tok_rows // CAP * (width // (3 * HD)) * IN_PIECES * CAP
    return pl.pallas_call(
        pack_kernel,
        grid=(steps,),
        in_specs=[spec] * 4 + [pl.BlockSpec((1, tok_rows), lambda i: (0, 0))],
        out_specs=pl.BlockSpec((out_rows // steps, HD), lambda i: (i, 0)),
        out_shape=jax.ShapeDtypeStruct((out_rows, HD), jnp.bfloat16),
        compiler_params=pltpu.CompilerParams(vmem_limit_bytes=40 * 2**20),
        name="pack",
    )(queries, key_rows, values, target, clip_row)


def split3(value):
    high = value.astype(jnp.bfloat16).astype(jnp.float32)
    rest = value - high
    mid = rest.astype(jnp.bfloat16).astype(jnp.float32)
    return high, mid, rest - mid


def nt_dot(a, b):
    return lax.dot_general(a, b, (((1,), (1,)), ((), ())), preferred_element_type=jnp.float32)


def tn_dot(a, b):
    return lax.dot_general(a, b, (((0,), (0,)), ((), ())), preferred_element_type=jnp.float32)


def attend_kernel(in_ref, factor_ref, out_ref, x_ref, lab_ref, fq_ref, fk_ref, g_ref):
    low = low_half()
    total = x_ref.shape[1]
    pair = 2 * IN_PIECES * CAP

    def sort_in(i, carry):
        base = pl.multiple_of(i * (2 * pair), 2 * pair)
        block = in_ref[pl.ds(base, 2 * pair), :].astype(jnp.float32)
        at = pl.ds(pl.multiple_of(i * 16, 16), 16)
        for j in range(IN_PIECES):
            halves = []
            for u in range(2):
                a, b = j // 2, (IN_PIECES + j) // 2
                lo = block[u * pair + a * 8 : u * pair + a * 8 + 8]
                hi = block[u * pair + b * 8 : u * pair + b * 8 + 8]
                if j % 2 == 0:
                    halves.append(jnp.where(low, lo, hi))
                else:
                    halves.append(swap(jnp.where(low, hi, lo)))
            both = jnp.concatenate(halves, axis=0)
            if j < IN_PIECES - 1:
                x_ref[j, at, :] = both.astype(jnp.bfloat16)
            else:
                lab_ref[at, :] = both
        return carry

    lax.fori_loop(0, total // 16, sort_in, 0, unroll=4)

    label = lab_ref[...]
    lane = lax.broadcasted_iota(jnp.int32, (total, HD), 1)
    is0 = jnp.where(label == 0.0, 1.0, 0.0)
    is1 = jnp.where(label == 1.0, 1.0, 0.0)
    empty = jnp.where(label < 0.0, 1.0, 0.0)
    fk_ref[...] = jnp.where(
        lane == 0, is0, jnp.where(lane == 1, is1, jnp.where(lane == 2, empty, 0.0))
    ).astype(jnp.bfloat16)
    fq_ref[...] = jnp.where(
        lane == 0,
        (is0 - 1.0) * MASK_FILL,
        jnp.where(lane == 1, (is1 - 1.0) * MASK_FILL, jnp.where(lane == 2, -MASK_FILL, 0.0)),
    ).astype(jnp.bfloat16)
    counts = (jnp.sum(is0, axis=0, keepdims=True), jnp.sum(is1, axis=0, keepdims=True))

    scale = HD**-0.5

    def one_head(head, sums):
        s0, s1 = sums
        key = x_ref[head * 4 + 1]
        value = x_ref[head * 4 + 2]
        key_wide = jnp.concatenate([key, fk_ref[...]], axis=1)
        for block in range(total // BLOCK):
            at = slice(block * BLOCK, (block + 1) * BLOCK)
            query = x_ref[head * 4, at, :]
            query_wide = jnp.concatenate([query, fq_ref[at, :]], axis=1)
            scores = nt_dot(query_wide, key_wide)
            largest = jnp.max(scores, axis=1, keepdims=True)
            expo = jnp.exp2((scores - largest) * (scale * LOG2E))
            probs = expo * (1.0 / jnp.sum(expo, axis=1, keepdims=True))
            probs_low = probs.astype(jnp.bfloat16)
            output = jnp.dot(probs_low, value, preferred_element_type=jnp.float32)
            error = output - x_ref[head * 4 + 3, at, :].astype(jnp.float32)
            lab = lab_ref[at, :]
            error = jnp.where(lab >= 0.0, error, 0.0)
            square = error * error
            s0 = s0 + jnp.sum(jnp.where(lab == 0.0, square, 0.0), axis=0, keepdims=True)
            s1 = s1 + jnp.sum(jnp.where(lab == 1.0, square, 0.0), axis=0, keepdims=True)
            grad_low = error.astype(jnp.bfloat16)
            grad_probs = nt_dot(grad_low, value)
            inner = jnp.sum(probs * grad_probs, axis=1, keepdims=True)
            grad_scores = (probs * (grad_probs - inner)).astype(jnp.bfloat16)
            g_ref[head * 3, at, :] = jnp.dot(grad_scores, key, preferred_element_type=jnp.float32) * scale
            grad_key = tn_dot(grad_scores, query) * scale
            grad_value = tn_dot(probs_low, grad_low)
            if block == 0:
                g_ref[head * 3 + 1] = grad_key
                g_ref[head * 3 + 2] = grad_value
            else:
                g_ref[head * 3 + 1] += grad_key
                g_ref[head * 3 + 2] += grad_value
        return s0, s1

    zero = jnp.zeros((1, HD), jnp.float32)
    s0, s1 = lax.fori_loop(0, 3, one_head, (zero, zero))

    parts = []
    for clip, (acc, count) in enumerate(zip((s0, s1), counts)):
        both = factor_ref[:, :HD] / (count * WIDTH)
        loss = jnp.sum(acc, axis=1, keepdims=True) * both
        parts.append((loss, loss * factor_ref[:, (1 + clip) * HD : (2 + clip) * HD] * both))
    lane_row = lax.broadcasted_iota(jnp.int32, (1, HD), 1)

    def spread(value, first):
        high, mid, rest = split3(value)
        return jnp.where(
            lane_row == first,
            high,
            jnp.where(lane_row == first + 1, mid, jnp.where(lane_row == first + 2, rest, 0.0)),
        )

    losses = spread(parts[0][0], 3) + spread(parts[1][0], 6)
    extra0 = losses + spread(parts[0][1], 0)
    extra1 = losses + spread(parts[1][1], 0)
    out_pair = 2 * OUT_PIECES * CAP

    def sort_out(i, carry):
        at = pl.ds(pl.multiple_of(i * 8, 8), 8)
        lab = lab_ref[at, :]
        tiles = [g_ref[j, at, :] for j in range(OUT_PIECES - 1)]
        tiles.append(jnp.where(lab == 0.0, extra0, jnp.where(lab == 1.0, extra1, losses)))
        turned = [swap(tile) for tile in tiles]
        first = [jnp.where(low, tiles[j], turned[j + 1]) for j in range(0, OUT_PIECES, 2)]
        second = [jnp.where(low, turned[j], tiles[j + 1]) for j in range(0, OUT_PIECES, 2)]
        base = pl.multiple_of(i * out_pair, out_pair)
        out_ref[pl.ds(base, out_pair), :] = jnp.concatenate(first + second, axis=0).astype(jnp.bfloat16)
        return carry

    lax.fori_loop(0, total // 8, sort_out, 0, unroll=4)


def attend(arrived, factors, sources):
    total = sources * CAP
    whole = pl.BlockSpec(memory_space=pltpu.VMEM)
    return pl.pallas_call(
        attend_kernel,
        in_specs=[whole, whole],
        out_specs=whole,
        out_shape=jax.ShapeDtypeStruct((sources * OUT_PIECES * CAP, HD), jnp.bfloat16),
        scratch_shapes=[
            pltpu.VMEM((12, total, HD), jnp.bfloat16),
            pltpu.VMEM((total, HD), jnp.float32),
            pltpu.VMEM((total, HD), jnp.bfloat16),
            pltpu.VMEM((total, HD), jnp.bfloat16),
            pltpu.VMEM((9, total, HD), jnp.float32),
        ],
        compiler_params=pltpu.CompilerParams(vmem_limit_bytes=50 * 2**20),
        name="attend",
    )(arrived, factors)


def unpack_kernel(here_ref, in_ref, dq_ref, dk_ref, dv_ref, loss_ref, *, seq_size):
    low = low_half()
    lane = lax.broadcasted_iota(jnp.int32, (8, HD), 1)
    rows = dq_ref.shape[0]
    chunk = OUT_PIECES * CAP
    step = pl.program_id(0)
    outs = (dq_ref, dk_ref, dv_ref)
    block = in_ref[...].astype(jnp.float32)

    def piece(tile, dest, j):
        even = ((tile * 2) * seq_size + dest) * chunk + (j // 2) * 8
        odd = ((tile * 2 + 1) * seq_size + dest) * chunk + (j // 2) * 8
        a, b = block[even : even + 8], block[odd : odd + 8]
        if j % 2 == 0:
            return jnp.where(low, a, swap(b))
        return jnp.where(low, swap(a), b)

    for two in range(rows // 16):
        coefs = []
        for tile in (two * 2, two * 2 + 1):
            extra = piece(tile, 0, OUT_PIECES - 1)
            for dest in range(1, seq_size):
                extra = extra + piece(tile, dest, OUT_PIECES - 1)
            coef = jnp.sum(jnp.where(lane < 3, extra, 0.0), axis=1, keepdims=True)
            coefs.append(jnp.broadcast_to(coef, (8, HD)))
            for half in range(2):
                group = step * (rows // CAP) + tile * 2 + half

                @pl.when(group == here_ref[0])
                def _():
                    line = extra[half * CAP : half * CAP + 1]
                    lane_row = lax.broadcasted_iota(jnp.int32, (1, HD), 1)
                    for clip in range(CLIPS_G):
                        mine = (lane_row >= 3 + 3 * clip) & (lane_row < 6 + 3 * clip)
                        loss_ref[0:1, clip : clip + 1] = jnp.sum(
                            jnp.where(mine, line, 0.0), axis=1, keepdims=True
                        )

        for dest in range(seq_size):
            for head in range(3):
                col = (dest * 3 + head) * HD
                for index, ref in enumerate(outs):
                    both = [
                        piece(two * 2 + n, dest, head * 3 + index) * coefs[n] for n in range(2)
                    ]
                    ref[two * 16 : two * 16 + 16, col : col + HD] = jnp.concatenate(
                        both, axis=0
                    ).astype(jnp.bfloat16)


def unpack(returned, here, tok_rows, seq_size):
    steps = 4
    rows = tok_rows // steps
    width = seq_size * 3 * HD
    grad_spec = pl.BlockSpec((rows, width), lambda i: (i, 0))
    grad_shape = jax.ShapeDtypeStruct((tok_rows, width), jnp.bfloat16)
    return pl.pallas_call(
        functools.partial(unpack_kernel, seq_size=seq_size),
        grid=(steps,),
        in_specs=[
            pl.BlockSpec(memory_space=pltpu.SMEM),
            pl.BlockSpec((returned.shape[0] // steps, HD), lambda i: (i, 0)),
        ],
        out_specs=[grad_spec] * 3 + [pl.BlockSpec((1, CLIPS_G), lambda i: (0, 0))],
        out_shape=[grad_shape] * 3 + [jax.ShapeDtypeStruct((1, CLIPS_G), jnp.float32)],
        compiler_params=pltpu.CompilerParams(vmem_limit_bytes=40 * 2**20),
        name="unpack",
    )(here, returned)


def shards(queries, key_rows, values, target, row_clip, ratios, ref_loss, noise_level):
    seq_size = lax.axis_size("seq")
    devices = lax.axis_size("dp") * seq_size
    tok_rows = queries.shape[0]
    sent = pack(queries, key_rows, values, target, row_clip.reshape(1, tok_rows))
    sent = sent.reshape(devices * IN_PIECES, CAP, HD)
    arrived = lax.all_to_all(sent, ("dp", "seq"), split_axis=0, concat_axis=0, tiled=True)
    arrived = arrived.reshape(devices * IN_PIECES * CAP, HD)
    weight_level = level_weight(noise_level)
    step = ratios / ref_loss * (2.0 * LOSS_SCALE)
    factors = jnp.concatenate(
        [jnp.broadcast_to(weight_level, (1, HD))]
        + [jnp.broadcast_to(step[:, c : c + 1], (1, HD)) for c in range(CLIPS_G)],
        axis=1,
    )
    grads = attend(arrived, factors, devices)
    grads = grads.reshape(devices, OUT_PIECES * CAP, HD)
    returned = lax.all_to_all(grads, ("dp", "seq"), split_axis=0, concat_axis=0, tiled=True)
    returned = returned.reshape(devices * OUT_PIECES * CAP, HD)
    here = lax.axis_index("dp").reshape(1).astype(jnp.int32)
    return tuple(unpack(returned, here, tok_rows, seq_size))


def solution(mesh):
    placed = (
        P(("dp", "seq"), None),
        P(("dp", "seq"), None),
        P(("dp", "seq"), None),
        P(("dp", "seq"), None),
        P(("dp", "seq")),
        P("dp", None),
        P("dp", None),
        P(),
    )
    return jax.shard_map(
        shards,
        mesh=mesh,
        in_specs=placed,
        out_specs=(
            P(("dp", "seq"), None),
            P(("dp", "seq"), None),
            P(("dp", "seq"), None),
            P("dp", None),
        ),
        check_vma=False,
    )
```

time: 432 us -> 205 us (0.47); the launches traced: 426 us -> 204 us
  starting transfers between devices: 92.3 us -> 22.2 us
  matrix products: 55.8 us -> 0 us
  waiting for transfers between devices: 181 us -> 143 us
  blocking collectives: 32.9 us -> 0 us
  local copies, waits for them, and re-layouts: 42.7 us -> 10.3 us
  Pallas kernels: 0 us -> 27.3 us
  other arithmetic: 18.8 us -> 0.01 us
    all_to_all x15 -> x2, starting transfers between devices: 92.3 us -> 22.2 us  [the longest x1 15.7 us: shards(): lax.all_to_all(sent, ('dp', 'seq'), split_axis=0, concat_axis=0, tiled=True)]
    dot_general x21 -> x0, matrix products: 55.8 us -> none  [the longest x6 14.6 us: head_probs(): jnp.dot(query_head, key_head.T, preferred_element_type=jnp.float32)]
    all_to_all x15 -> x2, waiting for transfers between devices: 181 us -> 143 us  [the longest x1 78.5 us: shards(): lax.all_to_all(sent, ('dp', 'seq'), split_axis=0, concat_axis=0, tiled=True)]
    pallas_call x0 -> x3, Pallas kernels: none -> 27.3 us  [the longest x1 21.2 us: attend(): pl.pallas_call(attend_kernel, in_specs=[whole, whole], out_specs=whole, o...]
    reshape x14 -> x0, local copies, waits for them, and re-layouts: 22.1 us -> none  [the longest x2 3.77 us: shards(): target_in = target.reshape(layout)]
    all_to_all x1 -> x0, blocking collectives: 20.4 us -> none  [shards(): lax.all_to_all(labels, 'dp', split_axis=0, concat_axis=0, tiled=True)]
    all_to_all x17 -> x0, local copies, waits for them, and re-layouts: 15.2 us -> none  [the longest x1 2.32 us: shards(): lax.all_to_all(key_in, 'dp', split_axis=0, concat_axis=0, tiled=True)]
    psum x1 -> x0, blocking collectives: 12.4 us -> none  [shards(): sums = lax.psum(partial_sums, 'seq')]
  transfers between devices with their start and end apart: 15 -> 2, of which waited for: 14 -> 2; matrix products, arithmetic and copies ran while one was open for 13% -> 1% of each run, Pallas kernels for 0% -> 0%
where the time goes in v1:
time: 205 us; the launch traced here: 204 us
  waiting for transfers between devices  143 us (70%)
  Pallas kernels  27.3 us (13%)
  starting transfers between devices  22.2 us (11%)
  local copies, waits for them, and re-layouts  10.3 us (5%)
    all_to_all x1, waiting for transfers between devices, shards(): lax.all_to_all(sent, ('dp', 'seq'), split_axis=0, concat_axis=0, tiled=True)  78.5 us
    all_to_all x1, waiting for transfers between devices, shards(): lax.all_to_all(grads, ('dp', 'seq'), split_axis=0, concat_axis=0, tiled=T...  64.5 us
    pallas_call x1, Pallas kernels, attend(): pl.pallas_call(attend_kernel, in_specs=[whole, whole], out_specs=whole, o...  21.2 us
    all_to_all x1, starting transfers between devices, shards(): lax.all_to_all(sent, ('dp', 'seq'), split_axis=0, concat_axis=0, tiled=True)  15.7 us
    unnamed x18, local copies, waits for them, and re-layouts  8.4 us
    all_to_all x1, starting transfers between devices, shards(): lax.all_to_all(grads, ('dp', 'seq'), split_axis=0, concat_axis=0, tiled=T...  6.5 us
  transfers between devices with their start and end apart: 2, of which 2 were waited for; matrix products, arithmetic and copies ran while one was open for 1% of the time, Pallas kernels for 0%

profile of v1, /device:TPU:1, one launch (start us, length us, event | category | flops | bytes accessed | tf_op | source)
XLA Modules:
  0.0 204.3 jit_solution(8088457595411984076)
XLA Ops:
  0.6 0.0 copy-start.1
  0.6 1.1 copy-done.1
  1.8 0.0 copy-start.2
  1.8 1.1 copy-done.2
  2.9 0.0 copy-start.3
  2.9 1.1 copy-done.3
  4.0 0.0 copy-start.4
  4.0 1.1 copy-done.4
  5.2 0.0 copy-start.5
  5.2 0.7 copy-done.5
  5.8 2.7 %pack.1 = bf16[13312,128]{1,0:T(8,128)(2,1)} custom-call(bf16[128,3072]{1,0:T(8,128)(2,1)S(1)} %copy-done.1, bf16[128,3072]{1,0:T(8,128)(2,1)S(1)} %copy-done.2, bf16[128,3072]{1,0:T(8,128)(2,1)S(1)} %copy-done.3, bf16[128,3072]{1,0:T(8,128)(2,1)S(1)} %copy-done.4, s32[1,128]{1,0:T(1,128)S(1)} %bitcast.11), custom_call_target="tpu_custom_call" | custom-call | tf_op jit(solution)/shard_map/pack/pallas_call | solution.py:85
  8.6 0.0 copy-start.7
  8.6 0.0 copy-start.8
  8.6 15.7 %all-to-all-start = ((bf16[3328,4,128]{2,1,0:T(4,128)(2,1)}), bf16[3328,4,128]{2,1,0:T(4,128)(2,1)S(1)}, u32[]{:S(2)}, u32[]{:S(2)}) async-start(bf16[3328,4,128]{2,1,0:T(4,128)(2,1)} %bitcast.2), calls=%async_computation | async-start | bytes 6815744 | tf_op jit(solution)/shard_map/all_to_all | solution.py:326
  24.9 0.0 copy-done.7
  24.9 0.0 copy-done.8
  24.9 0.6 fusion
  25.5 0.6 broadcast_in_dim.21
  26.2 0.6 broadcast_in_dim.19
  27.0 78.5 %all-to-all-done = bf16[3328,4,128]{2,1,0:T(4,128)(2,1)S(1)} async-done(((bf16[3328,4,128]{2,1,0:T(4,128)(2,1)}), bf16[3328,4,128]{2,1,0:T(4,128)(2,1)S(1)}, u32[]{:S(2)}, u32[]{:S(2)}) %all-to-all-start) | async-done | bytes 3407904 | tf_op jit(solution)/shard_map/all_to_all | solution.py:326
  105.5 0.0 copy-start.6
  105.5 1.7 copy-done.6
  107.2 21.2 %attend.1 = bf16[10240,128]{1,0:T(8,128)(2,1)S(1)} custom-call(bf16[13312,128]{1,0:T(8,128)(2,1)} %bitcast.12, f32[1,384]{1,0:T(1,128)S(1)} %reshape_maximum_fusion.factor_ref), custom_call_target="tpu_custom_call" | custom-call | tf_op jit(solution)/shard_map/attend/pallas_call | solution.py:233
  128.4 0.0 copy-start
  128.4 1.5 copy-done
  129.9 6.5 %all-to-all-start.1 = ((bf16[256,40,128]{2,1,0:T(8,128)(2,1)}), bf16[256,40,128]{2,1,0:T(8,128)(2,1)S(1)}, u32[]{:S(2)}, u32[]{:S(2)}) async-start(bf16[256,40,128]{2,1,0:T(8,128)(2,1)} %bitcast.10), calls=%async_computation.1 | async-start | bytes 5242880 | tf_op jit(solution)/shard_map/all_to_all | solution.py:337
  136.4 64.5 %all-to-all-done.1 = bf16[256,40,128]{2,1,0:T(8,128)(2,1)S(1)} async-done(((bf16[256,40,128]{2,1,0:T(8,128)(2,1)}), bf16[256,40,128]{2,1,0:T(8,128)(2,1)S(1)}, u32[]{:S(2)}, u32[]{:S(2)}) %all-to-all-start.1) | async-done | bytes 2621472 | tf_op jit(solution)/shard_map/all_to_all | solution.py:337
  200.9 3.3 %unpack.1 = (bf16[128,3072]{1,0:T(8,128)(2,1)}, bf16[128,3072]{1,0:T(8,128)(2,1)}, bf16[128,3072]{1,0:T(8,128)(2,1)}, f32[1,2]{1,0:T(1,128)}) custom-call(s32[1]{0:T(128)} %bitcast.here_ref, bf16[10240,128]{1,0:T(8,128)(2,1)S(1)} %bitcast.9), custom_call_target="tpu_custom_call" | custom-call | tf_op jit(solution)/shard_map/unpack/pallas_call | solution.py:306
  (6 shorter events, 0.0 us)
Async XLA Ops:
  0.6 1.1 copy-start.1
  1.8 1.1 copy-start.2
  2.9 1.1 copy-start.3
  4.0 1.1 copy-start.4
  5.2 0.7 copy-start.5
  8.6 16.4 %copy-start.7 = (f32[1,2]{1,0:T(1,128)S(1)}, f32[1,2]{1,0:T(1,128)}, u32[]{:S(2)}) copy-start(f32[1,2]{1,0:T(1,128)} %param.13) | copy-start | bytes 28
  8.6 16.4 %copy-start.8 = (f32[1,2]{1,0:T(1,128)S(1)}, f32[1,2]{1,0:T(1,128)}, u32[]{:S(2)}) copy-start(f32[1,2]{1,0:T(1,128)} %param.14) | copy-start | bytes 28
  8.6 96.9 %all-to-all-start = ((bf16[3328,4,128]{2,1,0:T(4,128)(2,1)}), bf16[3328,4,128]{2,1,0:T(4,128)(2,1)S(1)}, u32[]{:S(2)}, u32[]{:S(2)}) async-start(bf16[3328,4,128]{2,1,0:T(4,128)(2,1)} %bitcast.2), calls=%async_computation | async-start | bytes 6815744 | tf_op jit(solution)/shard_map/all_to_all | solution.py:326
  105.5 1.7 copy-start.6
  128.4 1.5 copy-start
  129.9 71.0 %all-to-all-start.1 = ((bf16[256,40,128]{2,1,0:T(8,128)(2,1)}), bf16[256,40,128]{2,1,0:T(8,128)(2,1)S(1)}, u32[]{:S(2)}, u32[]{:S(2)}) async-start(bf16[256,40,128]{2,1,0:T(8,128)(2,1)} %bitcast.10), calls=%async_computation.1 | async-start | bytes 5242880 | tf_op jit(solution)/shard_map/all_to_all | solution.py:337

commit v2 on v1

v2 whole, which is shorter than its diff:
```python
import functools

import jax
import jax.numpy as jnp
from jax import lax
from jax.experimental import pallas as pl
from jax.experimental.pallas import tpu as pltpu
from jax.sharding import PartitionSpec as P

HEADS = 24
HD = 128
CLIPS_G = 2
LEVELS = 1000

SHIFT_FACTOR = 5.0
LOSS_SCALE = 2.0**21
MASK_FILL = 1e30
LOG2E = 1.4426950408889634
WIDTH = HEADS * HD

CAP = 4
IN_PIECES = 13
OUT_PIECES = 10
BLOCK = 512
STRIP = 32
NCUT = 256
PARTS = 8
VMEM_LIMIT = 40 * 2**20
PACK_LIMIT = 61 * 2**20


def level_weight(noise_level):
    fraction = 1.0 - noise_level[0].astype(jnp.float32) / LEVELS
    sigma = SHIFT_FACTOR * fraction / (1.0 + (SHIFT_FACTOR - 1.0) * fraction)
    return 1.0 / (sigma * sigma + (1.0 - sigma) * (1.0 - sigma))


def low_half(shape=(8, HD)):
    return lax.broadcasted_iota(jnp.int32, shape, 0) % 8 < CAP


def swap(tile):
    return pltpu.roll(tile, CAP, 0)


def pack_kernel(q_ref, k_ref, v_ref, t_ref, clip_ref, out_ref, x_ref, c_ref, lab_ref, o_ref, in_sem, clip_sem, out_sem):
    low = low_half()
    tok_rows, width = q_ref.shape
    seq_size = width // (3 * HD)
    chunks = tok_rows // 16
    out_rows = o_ref.shape[0] // chunks

    def fetch(chunk, tensor):
        at = pl.ds(chunk * 16, 16)
        ref = (q_ref, k_ref, v_ref, t_ref)[tensor]
        return pltpu.make_async_copy(ref.at[at], x_ref.at[tensor, at], in_sem.at[chunk, tensor])

    def emit(chunk):
        at = pl.ds(chunk * out_rows, out_rows)
        return pltpu.make_async_copy(o_ref.at[at], out_ref.at[at], out_sem.at[chunk])

    clip_copy = pltpu.make_async_copy(clip_ref, c_ref, clip_sem.at[0])
    clip_copy.start()
    for chunk in range(chunks):
        for tensor in range(4):
            fetch(chunk, tensor).start()
    clip_copy.wait()
    row = lax.broadcasted_iota(jnp.int32, (tok_rows, tok_rows), 0)
    lane = lax.broadcasted_iota(jnp.int32, (tok_rows, tok_rows), 1)
    clips = jnp.broadcast_to(c_ref[...].astype(jnp.float32), (tok_rows, tok_rows))
    labels = jnp.sum(jnp.where(row == lane, clips, 0.0), axis=1, keepdims=True)
    lab_ref[...] = jnp.broadcast_to(labels, (tok_rows, HD))
    for chunk in range(chunks):
        for tensor in range(4):
            fetch(chunk, tensor).wait()
        at = slice(chunk * 16, chunk * 16 + 16)
        tensors = [x_ref[tensor, at, :].astype(jnp.float32) for tensor in range(4)]
        for tile in range(2):
            eight = slice(tile * 8, tile * 8 + 8)
            label_tile = lab_ref[chunk * 16 + tile * 8 : chunk * 16 + tile * 8 + 8, :]
            for half in range(2):
                made = []
                for dest in range(seq_size):
                    for head in range(3):
                        col = (dest * 3 + head) * HD
                        made.extend(tensor[eight, col : col + HD] for tensor in tensors)
                    made.append(label_tile)
                tiles = []
                for first, second in zip(made[::2], made[1::2]):
                    if half == 0:
                        tiles.append(jnp.where(low, first, swap(second)))
                    else:
                        tiles.append(jnp.where(low, swap(first), second))
                count = 8 * len(tiles)
                start = ((chunk * 2 + tile) * 2 + half) * count
                o_ref[start : start + count, :] = jnp.concatenate(tiles, axis=0).astype(jnp.bfloat16)
        emit(chunk).start()
    for chunk in range(chunks):
        emit(chunk).wait()


def pack(queries, key_rows, values, target, clip_row):
    tok_rows, width = queries.shape
    chunks = tok_rows // 16
    out_rows = tok_rows // CAP * (width // (3 * HD)) * IN_PIECES * CAP
    return pl.pallas_call(
        pack_kernel,
        in_specs=[pl.BlockSpec(memory_space=pltpu.HBM)] * 5,
        out_specs=pl.BlockSpec(memory_space=pltpu.HBM),
        out_shape=jax.ShapeDtypeStruct((out_rows, HD), jnp.bfloat16),
        scratch_shapes=[
            pltpu.VMEM((4, tok_rows, width), jnp.bfloat16),
            pltpu.VMEM((1, tok_rows), jnp.int32),
            pltpu.VMEM((tok_rows, HD), jnp.float32),
            pltpu.VMEM((out_rows, HD), jnp.bfloat16),
            pltpu.SemaphoreType.DMA((chunks, 4)),
            pltpu.SemaphoreType.DMA((1,)),
            pltpu.SemaphoreType.DMA((chunks,)),
        ],
        compiler_params=pltpu.CompilerParams(vmem_limit_bytes=PACK_LIMIT),
        name="pack",
    )(queries, key_rows, values, target, clip_row)


def split3(value):
    high = value.astype(jnp.bfloat16).astype(jnp.float32)
    rest = value - high
    mid = rest.astype(jnp.bfloat16).astype(jnp.float32)
    return high, mid, rest - mid


def nt_dot(a, b):
    return lax.dot_general(a, b, (((1,), (1,)), ((), ())), preferred_element_type=jnp.float32)


def tn_dot(a, b):
    return lax.dot_general(a, b, (((0,), (0,)), ((), ())), preferred_element_type=jnp.float32)


def attend_kernel(
    in_ref, factor_ref, sent_ref, out_ref, x_ref, lab_ref, fq_ref, fk_ref, g_ref,
    s_ref, p_ref, dp_ref, pl_ref, ds_ref, e_ref, out_sem,
):
    low = low_half()
    total = x_ref.shape[1]
    pair = 2 * IN_PIECES * CAP
    out_part = out_ref.shape[0] // PARTS

    def emit(part):
        at = pl.ds(part * out_part, out_part)
        return pltpu.make_async_copy(out_ref.at[at], sent_ref.at[at], out_sem.at[part])


    def sort_in(i, carry):
        base = pl.multiple_of(i * (2 * pair), 2 * pair)
        block = in_ref[pl.ds(base, 2 * pair), :].astype(jnp.float32)
        at = pl.ds(pl.multiple_of(i * 16, 16), 16)
        for j in range(IN_PIECES):
            halves = []
            for u in range(2):
                a, b = j // 2, (IN_PIECES + j) // 2
                lo = block[u * pair + a * 8 : u * pair + a * 8 + 8]
                hi = block[u * pair + b * 8 : u * pair + b * 8 + 8]
                if j % 2 == 0:
                    halves.append(jnp.where(low, lo, hi))
                else:
                    halves.append(swap(jnp.where(low, hi, lo)))
            both = jnp.concatenate(halves, axis=0)
            if j < IN_PIECES - 1:
                x_ref[j, at, :] = both.astype(jnp.bfloat16)
            else:
                lab_ref[at, :] = both
        return carry

    lax.fori_loop(0, total // 16, sort_in, 0, unroll=8)

    label = lab_ref[...]
    lane = lax.broadcasted_iota(jnp.int32, (total, HD), 1)
    is0 = jnp.where(label == 0.0, 1.0, 0.0)
    is1 = jnp.where(label == 1.0, 1.0, 0.0)
    empty = jnp.where(label < 0.0, 1.0, 0.0)
    fk_ref[...] = jnp.where(
        lane == 0, is0, jnp.where(lane == 1, is1, jnp.where(lane == 2, empty, 0.0))
    ).astype(jnp.bfloat16)
    fq_ref[...] = jnp.where(
        lane == 0,
        (is0 - 1.0) * MASK_FILL,
        jnp.where(lane == 1, (is1 - 1.0) * MASK_FILL, jnp.where(lane == 2, -MASK_FILL, 0.0)),
    ).astype(jnp.bfloat16)
    counts = (jnp.sum(is0, axis=0, keepdims=True), jnp.sum(is1, axis=0, keepdims=True))

    scale = HD**-0.5

    steps = [(head, block) for head in range(3) for block in range(total // BLOCK)]

    def rows_of(step):
        return slice(steps[step][1] * BLOCK, (steps[step][1] + 1) * BLOCK)

    def score_parts(step):
        head, at, slot = steps[step][0], rows_of(step), step % 2

        def part(n):
            cols = slice(n, n + NCUT)
            key_wide = jnp.concatenate([x_ref[head * 4 + 1, cols, :], fk_ref[cols, :]], axis=1)
            query_wide = jnp.concatenate([x_ref[head * 4, at, :], fq_ref[at, :]], axis=1)
            s_ref[slot, :, cols] = nt_dot(query_wide, key_wide)

        return [functools.partial(part, n) for n in range(0, total, NCUT)]

    def soft_parts(step):
        slot = step % 2

        def part(r):
            rows = slice(r, r + STRIP)
            scores = s_ref[slot, rows, :]
            largest = jnp.max(scores, axis=1, keepdims=True)
            expo = jnp.exp2((scores - largest) * (scale * LOG2E))
            probs = expo * (1.0 / jnp.sum(expo, axis=1, keepdims=True))
            p_ref[slot, rows, :] = probs
            pl_ref[slot, rows, :] = probs.astype(jnp.bfloat16)

        return [functools.partial(part, r) for r in range(0, BLOCK, STRIP)]

    def error_part(step, sums):
        head, at, slot = steps[step][0], rows_of(step), step % 2
        s0, s1 = sums
        output = jnp.dot(pl_ref[slot], x_ref[head * 4 + 2], preferred_element_type=jnp.float32)
        error = output - x_ref[head * 4 + 3, at, :].astype(jnp.float32)
        lab = lab_ref[at, :]
        error = jnp.where(lab >= 0.0, error, 0.0)
        square = error * error
        s0 = s0 + jnp.sum(jnp.where(lab == 0.0, square, 0.0), axis=0, keepdims=True)
        s1 = s1 + jnp.sum(jnp.where(lab == 1.0, square, 0.0), axis=0, keepdims=True)
        e_ref[slot] = error.astype(jnp.bfloat16)
        return s0, s1

    def grad_prob_parts(step):
        head, slot = steps[step][0], step % 2

        def part(n):
            cols = slice(n, n + NCUT)
            dp_ref[slot, :, cols] = nt_dot(e_ref[slot], x_ref[head * 4 + 2, cols, :])

        return [functools.partial(part, n) for n in range(0, total, NCUT)]

    def grad_score_parts(step):
        slot = step % 2

        def part(r):
            rows = slice(r, r + STRIP)
            grad_probs = dp_ref[slot, rows, :]
            probs = p_ref[slot, rows, :]
            inner = jnp.sum(probs * grad_probs, axis=1, keepdims=True)
            ds_ref[slot, rows, :] = (probs * (grad_probs - inner)).astype(jnp.bfloat16)

        return [functools.partial(part, r) for r in range(0, BLOCK, STRIP)]

    def grad_parts(step):
        (head, block), at, slot = steps[step], rows_of(step), step % 2

        def add(index, value):
            if block == 0:
                g_ref[index] = value
            else:
                g_ref[index] += value

        def part_q():
            g_ref[head * 3, at, :] = (
                jnp.dot(ds_ref[slot], x_ref[head * 4 + 1], preferred_element_type=jnp.float32) * scale
            )

        def part_k():
            add(head * 3 + 1, tn_dot(ds_ref[slot], x_ref[head * 4, at, :]) * scale)

        def part_v():
            add(head * 3 + 2, tn_dot(pl_ref[slot], e_ref[slot]))

        return [part_v, part_q, part_k]

    def weave(first, second):
        count = max(len(first), len(second))
        for i in range(count):
            for parts in (first, second):
                for part in parts[i * len(parts) // count : (i + 1) * len(parts) // count]:
                    part()

    zero = jnp.zeros((1, HD), jnp.float32)
    sums = (zero, zero)
    weave(score_parts(0), [])
    weave(soft_parts(0), [])
    for step in range(len(steps)):
        more = step + 1 < len(steps)
        sums = error_part(step, sums)
        weave(grad_prob_parts(step), [])
        weave(grad_score_parts(step), score_parts(step + 1) if more else [])
        weave(grad_parts(step), soft_parts(step + 1) if more else [])
    s0, s1 = sums

    parts = []
    for clip, (acc, count) in enumerate(zip((s0, s1), counts)):
        both = factor_ref[:, :HD] / (count * WIDTH)
        loss = jnp.sum(acc, axis=1, keepdims=True) * both
        parts.append((loss, loss * factor_ref[:, (1 + clip) * HD : (2 + clip) * HD] * both))
    lane_row = lax.broadcasted_iota(jnp.int32, (1, HD), 1)

    def spread(value, first):
        high, mid, rest = split3(value)
        return jnp.where(
            lane_row == first,
            high,
            jnp.where(lane_row == first + 1, mid, jnp.where(lane_row == first + 2, rest, 0.0)),
        )

    losses = spread(parts[0][0], 3) + spread(parts[1][0], 6)
    extra0 = losses + spread(parts[0][1], 0)
    extra1 = losses + spread(parts[1][1], 0)
    out_pair = 2 * OUT_PIECES * CAP

    def sort_out(i, carry):
        at = pl.ds(pl.multiple_of(i * 8, 8), 8)
        lab = lab_ref[at, :]
        tiles = [g_ref[j, at, :] for j in range(OUT_PIECES - 1)]
        tiles.append(jnp.where(lab == 0.0, extra0, jnp.where(lab == 1.0, extra1, losses)))
        turned = [swap(tile) for tile in tiles]
        first = [jnp.where(low, tiles[j], turned[j + 1]) for j in range(0, OUT_PIECES, 2)]
        second = [jnp.where(low, turned[j], tiles[j + 1]) for j in range(0, OUT_PIECES, 2)]
        base = pl.multiple_of(i * out_pair, out_pair)
        out_ref[pl.ds(base, out_pair), :] = jnp.concatenate(first + second, axis=0).astype(jnp.bfloat16)
        return carry

    loops = total // 8 // PARTS
    for part in range(PARTS):
        lax.fori_loop(part * loops, (part + 1) * loops, sort_out, 0, unroll=4)
        emit(part).start()
    for part in range(PARTS):
        emit(part).wait()


def attend(arrived, factors, sources):
    total = sources * CAP
    return pl.pallas_call(
        attend_kernel,
        in_specs=[pl.BlockSpec(memory_space=pltpu.VMEM)] * 2,
        out_specs=pl.BlockSpec(memory_space=pltpu.HBM),
        out_shape=jax.ShapeDtypeStruct((sources * OUT_PIECES * CAP, HD), jnp.bfloat16),
        scratch_shapes=[
            pltpu.VMEM((sources * OUT_PIECES * CAP, HD), jnp.bfloat16),
            pltpu.VMEM((12, total, HD), jnp.bfloat16),
            pltpu.VMEM((total, HD), jnp.float32),
            pltpu.VMEM((total, HD), jnp.bfloat16),
            pltpu.VMEM((total, HD), jnp.bfloat16),
            pltpu.VMEM((9, total, HD), jnp.float32),
            pltpu.VMEM((2, BLOCK, total), jnp.float32),
            pltpu.VMEM((2, BLOCK, total), jnp.float32),
            pltpu.VMEM((2, BLOCK, total), jnp.float32),
            pltpu.VMEM((2, BLOCK, total), jnp.bfloat16),
            pltpu.VMEM((2, BLOCK, total), jnp.bfloat16),
            pltpu.VMEM((2, BLOCK, HD), jnp.bfloat16),
            pltpu.SemaphoreType.DMA((PARTS,)),
        ],
        compiler_params=pltpu.CompilerParams(vmem_limit_bytes=VMEM_LIMIT),
        name="attend",
    )(arrived, factors)


def unpack_kernel(
    here_ref, in_ref, dq_ref, dk_ref, dv_ref, loss_ref, g_ref, out_sem, *, seq_size
):
    low = low_half()
    lane = lax.broadcasted_iota(jnp.int32, (8, HD), 1)
    tok_rows = dq_ref.shape[0]
    chunks = tok_rows // 16
    in_rows = in_ref.shape[0] // chunks
    stride = OUT_PIECES * CAP
    outs = (dq_ref, dk_ref, dv_ref)

    def emit(chunk, index):
        at = pl.ds(chunk * 16, 16)
        return pltpu.make_async_copy(g_ref.at[index, at], outs[index].at[at], out_sem.at[chunk, index])

    line = jnp.zeros((1, HD), jnp.float32)
    for chunk in range(chunks):
        block = in_ref[chunk * in_rows : (chunk + 1) * in_rows, :].astype(jnp.float32)

        def piece(tile, dest, j):
            even = ((tile * 2) * seq_size + dest) * stride + (j // 2) * 8
            odd = ((tile * 2 + 1) * seq_size + dest) * stride + (j // 2) * 8
            a, b = block[even : even + 8], block[odd : odd + 8]
            if j % 2 == 0:
                return jnp.where(low, a, swap(b))
            return jnp.where(low, swap(a), b)

        coefs = []
        for tile in range(2):
            extra = piece(tile, 0, OUT_PIECES - 1)
            for dest in range(1, seq_size):
                extra = extra + piece(tile, dest, OUT_PIECES - 1)
            coef = jnp.sum(jnp.where(lane < 3, extra, 0.0), axis=1, keepdims=True)
            coefs.append(jnp.broadcast_to(coef, (8, HD)))
            row = lax.broadcasted_iota(jnp.int32, (8, HD), 0)
            own = (here_ref[0] - chunk * 4 - tile * 2) * CAP
            line = line + jnp.sum(jnp.where(row == own, extra, 0.0), axis=0, keepdims=True)

        for index in range(3):
            for dest in range(seq_size):
                for head in range(3):
                    col = (dest * 3 + head) * HD
                    both = [piece(n, dest, head * 3 + index) * coefs[n] for n in range(2)]
                    g_ref[index, chunk * 16 : chunk * 16 + 16, col : col + HD] = jnp.concatenate(
                        both, axis=0
                    ).astype(jnp.bfloat16)
            emit(chunk, index).start()
    lane_row = lax.broadcasted_iota(jnp.int32, (1, HD), 1)
    for clip in range(CLIPS_G):
        mine = (lane_row >= 3 + 3 * clip) & (lane_row < 6 + 3 * clip)
        loss_ref[0:1, clip : clip + 1] = jnp.sum(jnp.where(mine, line, 0.0), axis=1, keepdims=True)
    for chunk in range(chunks):
        for index in range(3):
            emit(chunk, index).wait()


def unpack(returned, here, tok_rows, seq_size):
    chunks = tok_rows // 16
    width = seq_size * 3 * HD
    outside = pl.BlockSpec(memory_space=pltpu.HBM)
    grad_shape = jax.ShapeDtypeStruct((tok_rows, width), jnp.bfloat16)
    return pl.pallas_call(
        functools.partial(unpack_kernel, seq_size=seq_size),
        in_specs=[pl.BlockSpec(memory_space=pltpu.SMEM), pl.BlockSpec(memory_space=pltpu.VMEM)],
        out_specs=[outside] * 3 + [pl.BlockSpec(memory_space=pltpu.VMEM)],
        out_shape=[grad_shape] * 3 + [jax.ShapeDtypeStruct((1, CLIPS_G), jnp.float32)],
        scratch_shapes=[
            pltpu.VMEM((3, tok_rows, width), jnp.bfloat16),
            pltpu.SemaphoreType.DMA((chunks, 3)),
        ],
        compiler_params=pltpu.CompilerParams(vmem_limit_bytes=24 * 2**20),
        name="unpack",
    )(here, returned)


def shards(queries, key_rows, values, target, row_clip, ratios, ref_loss, noise_level):
    seq_size = lax.axis_size("seq")
    devices = lax.axis_size("dp") * seq_size
    tok_rows = queries.shape[0]
    sent = pack(queries, key_rows, values, target, row_clip.reshape(1, tok_rows))
    sent = sent.reshape(devices * IN_PIECES, CAP, HD)
    arrived = lax.all_to_all(sent, ("dp", "seq"), split_axis=0, concat_axis=0, tiled=True)
    arrived = arrived.reshape(devices * IN_PIECES * CAP, HD)
    weight_level = level_weight(noise_level)
    step = ratios / ref_loss * (2.0 * LOSS_SCALE)
    factors = jnp.concatenate(
        [jnp.broadcast_to(weight_level, (1, HD))]
        + [jnp.broadcast_to(step[:, c : c + 1], (1, HD)) for c in range(CLIPS_G)],
        axis=1,
    )
    grads = attend(arrived, factors, devices)
    grads = grads.reshape(devices, OUT_PIECES * CAP, HD)
    returned = lax.all_to_all(grads, ("dp", "seq"), split_axis=0, concat_axis=0, tiled=True)
    returned = returned.reshape(devices * OUT_PIECES * CAP, HD)
    here = lax.axis_index("dp").reshape(1).astype(jnp.int32)
    return tuple(unpack(returned, here, tok_rows, seq_size))


def solution(mesh):
    placed = (
        P(("dp", "seq"), None),
        P(("dp", "seq"), None),
        P(("dp", "seq"), None),
        P(("dp", "seq"), None),
        P(("dp", "seq")),
        P("dp", None),
        P("dp", None),
        P(),
    )
    return jax.shard_map(
        shards,
        mesh=mesh,
        in_specs=placed,
        out_specs=(
            P(("dp", "seq"), None),
            P(("dp", "seq"), None),
            P(("dp", "seq"), None),
            P("dp", None),
        ),
        check_vma=False,
    )
```

time: 205 us -> 193 us (0.941)
  local copies, waits for them, and re-layouts: 10.3 us -> 3.42 us
  Pallas kernels: 27.3 us -> 22.4 us
    unnamed x18 -> x6, local copies, waits for them, and re-layouts: 8.4 us -> 1.52 us
    pallas_call x3, Pallas kernels: 27.3 us -> 22.4 us  [the longest x1 16 us: attend(): pl.pallas_call(attend_kernel, in_specs=[pl.BlockSpec(memory_space=pltpu.V...]
where the time goes in v2:
time: 193 us
  waiting for transfers between devices  143 us (74%)
  Pallas kernels  22.4 us (12%)
  starting transfers between devices  22.2 us (12%)
  local copies, waits for them, and re-layouts  3.42 us (2%)
    all_to_all x1, waiting for transfers between devices, shards(): lax.all_to_all(sent, ('dp', 'seq'), split_axis=0, concat_axis=0, tiled=True)  78.5 us
    all_to_all x1, waiting for transfers between devices, shards(): lax.all_to_all(grads, ('dp', 'seq'), split_axis=0, concat_axis=0, tiled=T...  64.5 us
    pallas_call x1, Pallas kernels, attend(): pl.pallas_call(attend_kernel, in_specs=[pl.BlockSpec(memory_space=pltpu.V...  16 us
    all_to_all x1, starting transfers between devices, shards(): lax.all_to_all(sent, ('dp', 'seq'), split_axis=0, concat_axis=0, tiled=True)  15.7 us
    all_to_all x1, starting transfers between devices, shards(): lax.all_to_all(grads, ('dp', 'seq'), split_axis=0, concat_axis=0, tiled=T...  6.5 us
    pallas_call x1, Pallas kernels, pack(): pl.pallas_call(pack_kernel, in_specs=[pl.BlockSpec(memory_space=pltpu.HBM...  3.95 us
  transfers between devices with their start and end apart: 2, of which 2 were waited for; matrix products, arithmetic and copies ran while one was open for 1% of the time, Pallas kernels for 0%

profile of v2, /device:TPU:1, one launch (start us, length us, event | category | flops | bytes accessed | tf_op | source)
XLA Modules:
  0.0 192.7 jit_solution(13272593860482759633)
XLA Ops:
  0.6 3.9 %pack.1 = bf16[13312,128]{1,0:T(8,128)(2,1)} custom-call(bf16[128,3072]{1,0:T(8,128)(2,1)} %q_ref.1, bf16[128,3072]{1,0:T(8,128)(2,1)} %k_ref.1, bf16[128,3072]{1,0:T(8,128)(2,1)} %v_ref.1, bf16[128,3072]{1,0:T(8,128)(2,1)} %t_ref.1, s32[1,128]{1,0:T(1,128)} %bitcast.13), custom_call_target="tpu_custom_call" | custom-call | tf_op jit(solution)/shard_map/pack/pallas_call | solution.py:106
  4.6 0.0 copy-start.1
  4.6 0.0 copy-start.2
  4.6 15.7 %all-to-all-start = ((bf16[3328,4,128]{2,1,0:T(4,128)(2,1)}), bf16[3328,4,128]{2,1,0:T(4,128)(2,1)S(1)}, u32[]{:S(2)}, u32[]{:S(2)}) async-start(bf16[3328,4,128]{2,1,0:T(4,128)(2,1)} %bitcast.12), calls=%async_computation | async-start | bytes 6815744 | tf_op jit(solution)/shard_map/all_to_all | solution.py:447
  21.0 0.0 copy-done.1
  21.0 0.0 copy-done.2
  21.0 0.6 fusion
  21.6 0.6 broadcast_in_dim.21
  22.3 0.6 broadcast_in_dim.19
  23.0 78.5 %all-to-all-done = bf16[3328,4,128]{2,1,0:T(4,128)(2,1)S(1)} async-done(((bf16[3328,4,128]{2,1,0:T(4,128)(2,1)}), bf16[3328,4,128]{2,1,0:T(4,128)(2,1)S(1)}, u32[]{:S(2)}, u32[]{:S(2)}) %all-to-all-start) | async-done | bytes 3407904 | tf_op jit(solution)/shard_map/all_to_all | solution.py:447
  101.5 16.0 %attend.1 = bf16[10240,128]{1,0:T(8,128)(2,1)S(1)} custom-call(bf16[13312,128]{1,0:T(8,128)(2,1)S(1)} %bitcast.9, f32[1,384]{1,0:T(1,128)S(1)} %reshape_maximum_fusion.factor_ref), custom_call_target="tpu_custom_call" | custom-call | tf_op jit(solution)/shard_map/attend/pallas_call | solution.py:341
  117.5 0.0 copy-start
  117.5 1.5 copy-done
  119.0 6.5 %all-to-all-start.1 = ((bf16[256,40,128]{2,1,0:T(8,128)(2,1)}), bf16[256,40,128]{2,1,0:T(8,128)(2,1)S(1)}, u32[]{:S(2)}, u32[]{:S(2)}) async-start(bf16[256,40,128]{2,1,0:T(8,128)(2,1)} %bitcast.11), calls=%async_computation.1 | async-start | bytes 5242880 | tf_op jit(solution)/shard_map/all_to_all | solution.py:458
  125.5 64.5 %all-to-all-done.1 = bf16[256,40,128]{2,1,0:T(8,128)(2,1)S(1)} async-done(((bf16[256,40,128]{2,1,0:T(8,128)(2,1)}), bf16[256,40,128]{2,1,0:T(8,128)(2,1)S(1)}, u32[]{:S(2)}, u32[]{:S(2)}) %all-to-all-start.1) | async-done | bytes 2621472 | tf_op jit(solution)/shard_map/all_to_all | solution.py:458
  190.1 2.5 %unpack.1 = (bf16[128,3072]{1,0:T(8,128)(2,1)}, bf16[128,3072]{1,0:T(8,128)(2,1)}, bf16[128,3072]{1,0:T(8,128)(2,1)}, f32[1,2]{1,0:T(1,128)}) custom-call(s32[1]{0:T(128)} %bitcast.here_ref, bf16[10240,128]{1,0:T(8,128)(2,1)S(1)} %bitcast.10), custom_call_target="tpu_custom_call" | custom-call | tf_op jit(solution)/shard_map/unpack/pallas_call | solution.py:427
  (6 shorter events, 0.0 us)
Async XLA Ops:
  4.6 16.4 %copy-start.1 = (f32[1,2]{1,0:T(1,128)S(1)}, f32[1,2]{1,0:T(1,128)}, u32[]{:S(2)}) copy-start(f32[1,2]{1,0:T(1,128)} %param.13) | copy-start | bytes 28
  4.6 16.4 %copy-start.2 = (f32[1,2]{1,0:T(1,128)S(1)}, f32[1,2]{1,0:T(1,128)}, u32[]{:S(2)}) copy-start(f32[1,2]{1,0:T(1,128)} %param.14) | copy-start | bytes 28
  4.6 96.9 %all-to-all-start = ((bf16[3328,4,128]{2,1,0:T(4,128)(2,1)}), bf16[3328,4,128]{2,1,0:T(4,128)(2,1)S(1)}, u32[]{:S(2)}, u32[]{:S(2)}) async-start(bf16[3328,4,128]{2,1,0:T(4,128)(2,1)} %bitcast.12), calls=%async_computation | async-start | bytes 6815744 | tf_op jit(solution)/shard_map/all_to_all | solution.py:447
  117.5 1.5 copy-start
  119.0 71.0 %all-to-all-start.1 = ((bf16[256,40,128]{2,1,0:T(8,128)(2,1)}), bf16[256,40,128]{2,1,0:T(8,128)(2,1)S(1)}, u32[]{:S(2)}, u32[]{:S(2)}) async-start(bf16[256,40,128]{2,1,0:T(8,128)(2,1)} %bitcast.11), calls=%async_computation.1 | async-start | bytes 5242880 | tf_op jit(solution)/shard_map/all_to_all | solution.py:458

commit v3 on v2

--- a/solution.py
+++ b/solution.py
@@ -19,13 +19,16 @@
 WIDTH = HEADS * HD
 
 CAP = 4
-IN_PIECES = 13
-OUT_PIECES = 10
+TAIL = 2
+IN_PIECES = 12
+OUT_PIECES = 9
+IN_ROWS = IN_PIECES * CAP + TAIL
+OUT_ROWS = OUT_PIECES * CAP + TAIL
 BLOCK = 512
 STRIP = 32
 NCUT = 256
 PARTS = 8
-VMEM_LIMIT = 40 * 2**20
+ATTEND_LIMIT = 40 * 2**20
 PACK_LIMIT = 61 * 2**20
 
 
@@ -35,16 +38,42 @@
     return 1.0 / (sigma * sigma + (1.0 - sigma) * (1.0 - sigma))
 
 
-def low_half(shape=(8, HD)):
-    return lax.broadcasted_iota(jnp.int32, shape, 0) % 8 < CAP
-
-
-def swap(tile):
-    return pltpu.roll(tile, CAP, 0)
+def row_iota():
+    return lax.broadcasted_iota(jnp.int32, (8, HD), 0)
+
+
+def shift(tile, by):
+    return pltpu.roll(tile, by % 8, 0) if by % 8 else tile
+
+
+def lay(pieces):
+    row = row_iota()
+    tiles, current, at = [], None, 0
+    for tile, first, rows in pieces:
+        moved = shift(tile, at - first)
+        current = moved if at == 0 else jnp.where(row < at, current, moved)
+        at += rows
+        if at >= 8:
+            tiles.append(current)
+            current, at = moved, at - 8
+    return tiles
+
+
+def find(block, row):
+    index, first = divmod(row, 8)
+    tile = block[index * 8 : index * 8 + 8]
+    if first <= 4:
+        return tile, first
+    return jnp.where(row_iota() < 4, block[index * 8 + 8 : index * 8 + 16], tile), first
+
+
+def join(block, row, other):
+    upper, first = find(block, row)
+    lower, second = find(block, other)
+    return jnp.where(row_iota() < 4, shift(upper, -first), shift(lower, 4 - second))
 
 
 def pack_kernel(q_ref, k_ref, v_ref, t_ref, clip_ref, out_ref, x_ref, c_ref, lab_ref, o_ref, in_sem, clip_sem, out_sem):
-    low = low_half()
     tok_rows, width = q_ref.shape
     seq_size = width // (3 * HD)
     chunks = tok_rows // 16
@@ -70,6 +99,7 @@
     clips = jnp.broadcast_to(c_ref[...].astype(jnp.float32), (tok_rows, tok_rows))
     labels = jnp.sum(jnp.where(row == lane, clips, 0.0), axis=1, keepdims=True)
     lab_ref[...] = jnp.broadcast_to(labels, (tok_rows, HD))
+    front = lax.broadcasted_iota(jnp.int32, (8, HD), 1) < HD // 2
     for chunk in range(chunks):
         for tensor in range(4):
             fetch(chunk, tensor).wait()
@@ -78,22 +108,17 @@
         for tile in range(2):
             eight = slice(tile * 8, tile * 8 + 8)
             label_tile = lab_ref[chunk * 16 + tile * 8 : chunk * 16 + tile * 8 + 8, :]
+            label_tile = jnp.where(front, label_tile, shift(label_tile, -2))
             for half in range(2):
                 made = []
                 for dest in range(seq_size):
                     for head in range(3):
                         col = (dest * 3 + head) * HD
-                        made.extend(tensor[eight, col : col + HD] for tensor in tensors)
-                    made.append(label_tile)
-                tiles = []
-                for first, second in zip(made[::2], made[1::2]):
-                    if half == 0:
-                        tiles.append(jnp.where(low, first, swap(second)))
-                    else:
-                        tiles.append(jnp.where(low, swap(first), second))
-                count = 8 * len(tiles)
+                        made.extend((tensor[eight, col : col + HD], half * CAP, CAP) for tensor in tensors)
+                    made.append((label_tile, half * CAP, TAIL))
+                count = seq_size * IN_ROWS
                 start = ((chunk * 2 + tile) * 2 + half) * count
-                o_ref[start : start + count, :] = jnp.concatenate(tiles, axis=0).astype(jnp.bfloat16)
+                o_ref[start : start + count, :] = jnp.concatenate(lay(made), axis=0).astype(jnp.bfloat16)
         emit(chunk).start()
     for chunk in range(chunks):
         emit(chunk).wait()
@@ -102,7 +127,7 @@
 def pack(queries, key_rows, values, target, clip_row):
     tok_rows, width = queries.shape
     chunks = tok_rows // 16
-    out_rows = tok_rows // CAP * (width // (3 * HD)) * IN_PIECES * CAP
+    out_rows = tok_rows // CAP * (width // (3 * HD)) * IN_ROWS
     return pl.pallas_call(
         pack_kernel,
         in_specs=[pl.BlockSpec(memory_space=pltpu.HBM)] * 5,
@@ -141,9 +166,9 @@
     in_ref, factor_ref, sent_ref, out_ref, x_ref, lab_ref, fq_ref, fk_ref, g_ref,
     s_ref, p_ref, dp_ref, pl_ref, ds_ref, e_ref, out_sem,
 ):
-    low = low_half()
     total = x_ref.shape[1]
-    pair = 2 * IN_PIECES * CAP
+    row = row_iota()
+    front = lax.broadcasted_iota(jnp.int32, (8, HD), 1) < HD // 2
     out_part = out_ref.shape[0] // PARTS
 
     def emit(part):
@@ -152,27 +177,31 @@
 
 
     def sort_in(i, carry):
-        base = pl.multiple_of(i * (2 * pair), 2 * pair)
-        block = in_ref[pl.ds(base, 2 * pair), :].astype(jnp.float32)
-        at = pl.ds(pl.multiple_of(i * 16, 16), 16)
+        base = pl.multiple_of(i * (8 * IN_ROWS), 8 * IN_ROWS)
+        block = in_ref[pl.ds(base, 8 * IN_ROWS), :].astype(jnp.float32)
+        at = pl.ds(pl.multiple_of(i * 32, 32), 32)
         for j in range(IN_PIECES):
-            halves = []
-            for u in range(2):
-                a, b = j // 2, (IN_PIECES + j) // 2
-                lo = block[u * pair + a * 8 : u * pair + a * 8 + 8]
-                hi = block[u * pair + b * 8 : u * pair + b * 8 + 8]
-                if j % 2 == 0:
-                    halves.append(jnp.where(low, lo, hi))
-                else:
-                    halves.append(swap(jnp.where(low, hi, lo)))
-            both = jnp.concatenate(halves, axis=0)
-            if j < IN_PIECES - 1:
-                x_ref[j, at, :] = both.astype(jnp.bfloat16)
-            else:
-                lab_ref[at, :] = both
+            start = j * CAP
+            tiles = [join(block, 2 * u * IN_ROWS + start, (2 * u + 1) * IN_ROWS + start) for u in range(4)]
+            x_ref[j, at, :] = jnp.concatenate(tiles, axis=0).astype(jnp.bfloat16)
+        labels = []
+        for u in range(4):
+            start, other = 2 * u * IN_ROWS + IN_PIECES * CAP, (2 * u + 1) * IN_ROWS + IN_PIECES * CAP
+            upper = shift(block[start // 8 * 8 : start // 8 * 8 + 8], -start)
+            lower = shift(block[other // 8 * 8 : other // 8 * 8 + 8], 4 - other)
+            tile = jnp.where(row < 4, upper, lower)
+            turned = pltpu.roll(tile, HD // 2, 1)
+            labels.append(
+                jnp.where(
+                    row % 4 < 2,
+                    jnp.where(front, tile, turned),
+                    shift(jnp.where(front, turned, tile), 2),
+                )
+            )
+        lab_ref[at, :] = jnp.concatenate(labels, axis=0)
         return carry
 
-    lax.fori_loop(0, total // 16, sort_in, 0, unroll=8)
+    lax.fori_loop(0, total // 32, sort_in, 0, unroll=4)
 
     label = lab_ref[...]
     lane = lax.broadcasted_iota(jnp.int32, (total, HD), 1)
@@ -312,25 +341,30 @@
         )
 
     losses = spread(parts[0][0], 3) + spread(parts[1][0], 6)
-    extra0 = losses + spread(parts[0][1], 0)
-    extra1 = losses + spread(parts[1][1], 0)
-    out_pair = 2 * OUT_PIECES * CAP
+    first0, first1 = spread(parts[0][1], 0), spread(parts[1][1], 0)
+    later0, later1 = spread(parts[0][1], HD // 2), spread(parts[1][1], HD // 2)
 
     def sort_out(i, carry):
-        at = pl.ds(pl.multiple_of(i * 8, 8), 8)
-        lab = lab_ref[at, :]
-        tiles = [g_ref[j, at, :] for j in range(OUT_PIECES - 1)]
-        tiles.append(jnp.where(lab == 0.0, extra0, jnp.where(lab == 1.0, extra1, losses)))
-        turned = [swap(tile) for tile in tiles]
-        first = [jnp.where(low, tiles[j], turned[j + 1]) for j in range(0, OUT_PIECES, 2)]
-        second = [jnp.where(low, turned[j], tiles[j + 1]) for j in range(0, OUT_PIECES, 2)]
-        base = pl.multiple_of(i * out_pair, out_pair)
-        out_ref[pl.ds(base, out_pair), :] = jnp.concatenate(first + second, axis=0).astype(jnp.bfloat16)
+        at = pl.ds(pl.multiple_of(i * 32, 32), 32)
+        grads = [g_ref[j, at, :] for j in range(OUT_PIECES)]
+        labs = lab_ref[at, :]
+        pieces = []
+        for u in range(4):
+            eight = slice(u * 8, u * 8 + 8)
+            lab = labs[eight]
+            tail = losses + jnp.where(lab == 0.0, first0, jnp.where(lab == 1.0, first1, 0.0))
+            later = jnp.where(lab == 0.0, later0, jnp.where(lab == 1.0, later1, 0.0))
+            tail = tail + shift(later, -2)
+            for half in range(2):
+                pieces.extend((grad[eight], half * CAP, CAP) for grad in grads)
+                pieces.append((tail, half * CAP, TAIL))
+        base = pl.multiple_of(i * (8 * OUT_ROWS), 8 * OUT_ROWS)
+        out_ref[pl.ds(base, 8 * OUT_ROWS), :] = jnp.concatenate(lay(pieces), axis=0).astype(jnp.bfloat16)
         return carry
 
-    loops = total // 8 // PARTS
+    loops = total // 32 // PARTS
     for part in range(PARTS):
-        lax.fori_loop(part * loops, (part + 1) * loops, sort_out, 0, unroll=4)
+        lax.fori_loop(part * loops, (part + 1) * loops, sort_out, 0, unroll=True)
         emit(part).start()
     for part in range(PARTS):
         emit(part).wait()
@@ -342,9 +376,9 @@
         attend_kernel,
         in_specs=[pl.BlockSpec(memory_space=pltpu.VMEM)] * 2,
         out_specs=pl.BlockSpec(memory_space=pltpu.HBM),
-        out_shape=jax.ShapeDtypeStruct((sources * OUT_PIECES * CAP, HD), jnp.bfloat16),
+        out_shape=pltpu.HBM((sources * OUT_ROWS, HD), jnp.bfloat16),
         scratch_shapes=[
-            pltpu.VMEM((sources * OUT_PIECES * CAP, HD), jnp.bfloat16),
+            pltpu.VMEM((sources * OUT_ROWS, HD), jnp.bfloat16),
             pltpu.VMEM((12, total, HD), jnp.bfloat16),
             pltpu.VMEM((total, HD), jnp.float32),
             pltpu.VMEM((total, HD), jnp.bfloat16),
@@ -358,7 +392,7 @@
             pltpu.VMEM((2, BLOCK, HD), jnp.bfloat16),
             pltpu.SemaphoreType.DMA((PARTS,)),
         ],
-        compiler_params=pltpu.CompilerParams(vmem_limit_bytes=VMEM_LIMIT),
+        compiler_params=pltpu.CompilerParams(vmem_limit_bytes=ATTEND_LIMIT),
         name="attend",
     )(arrived, factors)
 
@@ -366,12 +400,11 @@
 def unpack_kernel(
     here_ref, in_ref, dq_ref, dk_ref, dv_ref, loss_ref, g_ref, out_sem, *, seq_size
 ):
-    low = low_half()
+    row = row_iota()
     lane = lax.broadcasted_iota(jnp.int32, (8, HD), 1)
     tok_rows = dq_ref.shape[0]
     chunks = tok_rows // 16
     in_rows = in_ref.shape[0] // chunks
-    stride = OUT_PIECES * CAP
     outs = (dq_ref, dk_ref, dv_ref)
 
     def emit(chunk, index):
@@ -382,30 +415,33 @@
     for chunk in range(chunks):
         block = in_ref[chunk * in_rows : (chunk + 1) * in_rows, :].astype(jnp.float32)
 
-        def piece(tile, dest, j):
-            even = ((tile * 2) * seq_size + dest) * stride + (j // 2) * 8
-            odd = ((tile * 2 + 1) * seq_size + dest) * stride + (j // 2) * 8
-            a, b = block[even : even + 8], block[odd : odd + 8]
-            if j % 2 == 0:
-                return jnp.where(low, a, swap(b))
-            return jnp.where(low, swap(a), b)
+        def starts(tile, dest):
+            return [((tile * 2 + n) * seq_size + dest) * OUT_ROWS for n in range(2)]
 
         coefs = []
         for tile in range(2):
-            extra = piece(tile, 0, OUT_PIECES - 1)
-            for dest in range(1, seq_size):
-                extra = extra + piece(tile, dest, OUT_PIECES - 1)
-            coef = jnp.sum(jnp.where(lane < 3, extra, 0.0), axis=1, keepdims=True)
-            coefs.append(jnp.broadcast_to(coef, (8, HD)))
-            row = lax.broadcasted_iota(jnp.int32, (8, HD), 0)
+            extra = None
+            for dest in range(seq_size):
+                start, other = [first + OUT_PIECES * CAP for first in starts(tile, dest)]
+                upper = shift(block[start // 8 * 8 : start // 8 * 8 + 8], -start)
+                lower = shift(block[other // 8 * 8 : other // 8 * 8 + 8], 4 - other)
+                one = jnp.where(row < 4, upper, lower)
+                extra = one if extra is None else extra + one
+            early = jnp.sum(jnp.where(lane < 3, extra, 0.0), axis=1, keepdims=True)
+            late = jnp.where((lane >= HD // 2) & (lane < HD // 2 + 3), extra, 0.0)
+            late = jnp.sum(late, axis=1, keepdims=True)
+            late = shift(jnp.broadcast_to(late, (8, HD)), 2)
+            coefs.append(jnp.where(row % 4 < 2, jnp.broadcast_to(early, (8, HD)), late))
             own = (here_ref[0] - chunk * 4 - tile * 2) * CAP
             line = line + jnp.sum(jnp.where(row == own, extra, 0.0), axis=0, keepdims=True)
-
         for index in range(3):
             for dest in range(seq_size):
                 for head in range(3):
                     col = (dest * 3 + head) * HD
-                    both = [piece(n, dest, head * 3 + index) * coefs[n] for n in range(2)]
+                    both = []
+                    for tile in range(2):
+                        start, other = [first + (head * 3 + index) * CAP for first in starts(tile, dest)]
+                        both.append(join(block, start, other) * coefs[tile])
                     g_ref[index, chunk * 16 : chunk * 16 + 16, col : col + HD] = jnp.concatenate(
                         both, axis=0
                     ).astype(jnp.bfloat16)
@@ -443,9 +479,9 @@
     devices = lax.axis_size("dp") * seq_size
     tok_rows = queries.shape[0]
     sent = pack(queries, key_rows, values, target, row_clip.reshape(1, tok_rows))
-    sent = sent.reshape(devices * IN_PIECES, CAP, HD)
+    sent = sent.reshape(devices * IN_ROWS // TAIL, TAIL, HD)
     arrived = lax.all_to_all(sent, ("dp", "seq"), split_axis=0, concat_axis=0, tiled=True)
-    arrived = arrived.reshape(devices * IN_PIECES * CAP, HD)
+    arrived = arrived.reshape(devices * IN_ROWS, HD)
     weight_level = level_weight(noise_level)
     step = ratios / ref_loss * (2.0 * LOSS_SCALE)
     factors = jnp.concatenate(
@@ -454,9 +490,9 @@
         axis=1,
     )
     grads = attend(arrived, factors, devices)
-    grads = grads.reshape(devices, OUT_PIECES * CAP, HD)
+    grads = grads.reshape(devices * OUT_ROWS // TAIL, TAIL, HD)
     returned = lax.all_to_all(grads, ("dp", "seq"), split_axis=0, concat_axis=0, tiled=True)
-    returned = returned.reshape(devices * OUT_PIECES * CAP, HD)
+    returned = returned.reshape(devices * OUT_ROWS, HD)
     here = lax.axis_index("dp").reshape(1).astype(jnp.int32)
     return tuple(unpack(returned, here, tok_rows, seq_size))
 

time: 193 us -> 186 us (0.964)
  waiting for transfers between devices: 143 us -> 137 us
    all_to_all x1, waiting for transfers between devices: 78.5 us -> 75.7 us  [shards(): lax.all_to_all(sent, ('dp', 'seq'), split_axis=0, concat_axis=0, tiled=True)]
    all_to_all x1, waiting for transfers between devices: 64.5 us -> 61.7 us  [shards(): lax.all_to_all(grads, ('dp', 'seq'), split_axis=0, concat_axis=0, tiled=T...]
where the time goes in v3:
time: 186 us
  waiting for transfers between devices  137 us (74%)
  Pallas kernels  22.8 us (12%)
  starting transfers between devices  22.2 us (12%)
  local copies, waits for them, and re-layouts  1.91 us (1%)
    all_to_all x1, waiting for transfers between devices, shards(): lax.all_to_all(sent, ('dp', 'seq'), split_axis=0, concat_axis=0, tiled=True)  75.7 us
    all_to_all x1, waiting for transfers between devices, shards(): lax.all_to_all(grads, ('dp', 'seq'), split_axis=0, concat_axis=0, tiled=T...  61.7 us
    pallas_call x1, Pallas kernels, attend(): pl.pallas_call(attend_kernel, in_specs=[pl.BlockSpec(memory_space=pltpu.V...  16.4 us
    all_to_all x1, starting transfers between devices, shards(): lax.all_to_all(sent, ('dp', 'seq'), split_axis=0, concat_axis=0, tiled=True)  15.7 us
    all_to_all x1, starting transfers between devices, shards(): lax.all_to_all(grads, ('dp', 'seq'), split_axis=0, concat_axis=0, tiled=T...  6.5 us
    pallas_call x1, Pallas kernels, pack(): pl.pallas_call(pack_kernel, in_specs=[pl.BlockSpec(memory_space=pltpu.HBM...  3.94 us
  transfers between devices with their start and end apart: 2, of which 2 were waited for; matrix products, arithmetic and copies ran while one was open for 1% of the time, Pallas kernels for 0%

profile of v3, /device:TPU:1, one launch (start us, length us, event | category | flops | bytes accessed | tf_op | source)
XLA Modules:
  0.0 186.0 jit_solution(7294919919137772129)
XLA Ops:
  0.6 3.9 %pack.1 = bf16[12800,128]{1,0:T(8,128)(2,1)} custom-call(bf16[128,3072]{1,0:T(8,128)(2,1)} %q_ref.1, bf16[128,3072]{1,0:T(8,128)(2,1)} %k_ref.1, bf16[128,3072]{1,0:T(8,128)(2,1)} %v_ref.1, bf16[128,3072]{1,0:T(8,128)(2,1)} %t_ref.1, s32[1,128]{1,0:T(1,128)} %bitcast.13), custom_call_target="tpu_custom_call" | custom-call | tf_op jit(solution)/shard_map/pack/pallas_call | solution.py:131
  4.6 0.0 copy-start
  4.6 0.0 copy-start.1
  4.6 15.7 %all-to-all-start = ((bf16[6400,2,128]{2,1,0:T(2,128)(2,1)}), bf16[6400,2,128]{2,1,0:T(2,128)(2,1)S(1)}, u32[]{:S(2)}, u32[]{:S(2)}) async-start(bf16[6400,2,128]{2,1,0:T(2,128)(2,1)} %bitcast.11), calls=%async_computation | async-start | bytes 6553600 | tf_op jit(solution)/shard_map/all_to_all | solution.py:483
  21.0 0.0 copy-done
  21.0 0.0 copy-done.1
  21.0 0.6 fusion
  21.6 0.6 broadcast_in_dim.21
  22.3 0.6 broadcast_in_dim.19
  23.0 75.7 %all-to-all-done = bf16[6400,2,128]{2,1,0:T(2,128)(2,1)S(1)} async-done(((bf16[6400,2,128]{2,1,0:T(2,128)(2,1)}), bf16[6400,2,128]{2,1,0:T(2,128)(2,1)S(1)}, u32[]{:S(2)}, u32[]{:S(2)}) %all-to-all-start) | async-done | bytes 3276832 | tf_op jit(solution)/shard_map/all_to_all | solution.py:483
  98.7 16.4 %attend.1 = bf16[9728,128]{1,0:T(8,128)(2,1)} custom-call(bf16[12800,128]{1,0:T(8,128)(2,1)S(1)} %bitcast.9, f32[1,384]{1,0:T(1,128)S(1)} %reshape_maximum_fusion.factor_ref), custom_call_target="tpu_custom_call" | custom-call | tf_op jit(solution)/shard_map/attend/pallas_call | solution.py:375
  115.1 6.5 %all-to-all-start.1 = ((bf16[4864,2,128]{2,1,0:T(2,128)(2,1)}), bf16[4864,2,128]{2,1,0:T(2,128)(2,1)S(1)}, u32[]{:S(2)}, u32[]{:S(2)}) async-start(bf16[4864,2,128]{2,1,0:T(2,128)(2,1)} %bitcast.12), calls=%async_computation.1 | async-start | bytes 4980736 | tf_op jit(solution)/shard_map/all_to_all | solution.py:494
  121.6 61.7 %all-to-all-done.1 = bf16[4864,2,128]{2,1,0:T(2,128)(2,1)S(1)} async-done(((bf16[4864,2,128]{2,1,0:T(2,128)(2,1)}), bf16[4864,2,128]{2,1,0:T(2,128)(2,1)S(1)}, u32[]{:S(2)}, u32[]{:S(2)}) %all-to-all-start.1) | async-done | bytes 2490400 | tf_op jit(solution)/shard_map/all_to_all | solution.py:494
  183.3 2.5 %unpack.1 = (bf16[128,3072]{1,0:T(8,128)(2,1)}, bf16[128,3072]{1,0:T(8,128)(2,1)}, bf16[128,3072]{1,0:T(8,128)(2,1)}, f32[1,2]{1,0:T(1,128)}) custom-call(s32[1]{0:T(128)} %bitcast.here_ref, bf16[9728,128]{1,0:T(8,128)(2,1)S(1)} %bitcast.10), custom_call_target="tpu_custom_call" | custom-call | tf_op jit(solution)/shard_map/unpack/pallas_call | solution.py:463
  (6 shorter events, 0.0 us)
Async XLA Ops:
  4.6 16.4 %copy-start = (f32[1,2]{1,0:T(1,128)S(1)}, f32[1,2]{1,0:T(1,128)}, u32[]{:S(2)}) copy-start(f32[1,2]{1,0:T(1,128)} %param.13) | copy-start | bytes 28
  4.6 16.4 %copy-start.1 = (f32[1,2]{1,0:T(1,128)S(1)}, f32[1,2]{1,0:T(1,128)}, u32[]{:S(2)}) copy-start(f32[1,2]{1,0:T(1,128)} %param.14) | copy-start | bytes 28
  4.6 94.1 %all-to-all-start = ((bf16[6400,2,128]{2,1,0:T(2,128)(2,1)}), bf16[6400,2,128]{2,1,0:T(2,128)(2,1)S(1)}, u32[]{:S(2)}, u32[]{:S(2)}) async-start(bf16[6400,2,128]{2,1,0:T(2,128)(2,1)} %bitcast.11), calls=%async_computation | async-start | bytes 6553600 | tf_op jit(solution)/shard_map/all_to_all | solution.py:483
  115.1 68.2 %all-to-all-start.1 = ((bf16[4864,2,128]{2,1,0:T(2,128)(2,1)}), bf16[4864,2,128]{2,1,0:T(2,128)(2,1)S(1)}, u32[]{:S(2)}, u32[]{:S(2)}) async-start(bf16[4864,2,128]{2,1,0:T(2,128)(2,1)} %bitcast.12), calls=%async_computation.1 | async-start | bytes 4980736 | tf_op jit(solution)/shard_map/all_to_all | solution.py:494

commit v4 on v3

--- a/solution.py
+++ b/solution.py
@@ -18,9 +18,10 @@
 LOG2E = 1.4426950408889634
 WIDTH = HEADS * HD
 
+Z_SIZE = 8
 CAP = 4
 TAIL = 2
-IN_PIECES = 12
+IN_PIECES = 8
 OUT_PIECES = 9
 IN_ROWS = IN_PIECES * CAP + TAIL
 OUT_ROWS = OUT_PIECES * CAP + TAIL
@@ -73,10 +74,14 @@
     return jnp.where(row_iota() < 4, shift(upper, -first), shift(lower, 4 - second))
 
 
-def pack_kernel(q_ref, k_ref, v_ref, t_ref, clip_ref, out_ref, x_ref, c_ref, lab_ref, o_ref, in_sem, clip_sem, out_sem):
+def pack_kernel(
+    q_ref, k_ref, v_ref, t_ref, clip_ref, out_ref, third_ref, x_ref, c_ref, lab_ref, o_ref, third,
+    in_sem, clip_sem, out_sem, third_sem,
+):
     tok_rows, width = q_ref.shape
     seq_size = width // (3 * HD)
     chunks = tok_rows // 16
+    groups = tok_rows // CAP
     out_rows = o_ref.shape[0] // chunks
 
     def fetch(chunk, tensor):
@@ -109,10 +114,18 @@
             eight = slice(tile * 8, tile * 8 + 8)
             label_tile = lab_ref[chunk * 16 + tile * 8 : chunk * 16 + tile * 8 + 8, :]
             label_tile = jnp.where(front, label_tile, shift(label_tile, -2))
+            for dest in range(seq_size):
+                col = (dest * 3 + 2) * HD
+                for part in range(2):
+                    pair = [tensor[eight, col : col + HD] for tensor in tensors[part * 2 : part * 2 + 2]]
+                    both = [lay([(one, half * CAP, CAP) for one in pair])[0] for half in range(2)]
+                    group = (chunk * 2 + tile) * 2
+                    start = (((part * 2 + dest % 2) * (seq_size // 2) + dest // 2) * groups + group) * 8
+                    third[start : start + 16, :] = jnp.concatenate(both, axis=0).astype(jnp.bfloat16)
             for half in range(2):
                 made = []
                 for dest in range(seq_size):
-                    for head in range(3):
+                    for head in range(2):
                         col = (dest * 3 + head) * HD
                         made.extend((tensor[eight, col : col + HD], half * CAP, CAP) for tensor in tensors)
                     made.append((label_tile, half * CAP, TAIL))
@@ -120,27 +133,36 @@
                 start = ((chunk * 2 + tile) * 2 + half) * count
                 o_ref[start : start + count, :] = jnp.concatenate(lay(made), axis=0).astype(jnp.bfloat16)
         emit(chunk).start()
+    last_copy = pltpu.make_async_copy(third, third_ref, third_sem.at[0])
+    last_copy.start()
     for chunk in range(chunks):
         emit(chunk).wait()
+    last_copy.wait()
 
 
 def pack(queries, key_rows, values, target, clip_row):
     tok_rows, width = queries.shape
     chunks = tok_rows // 16
     out_rows = tok_rows // CAP * (width // (3 * HD)) * IN_ROWS
+    third_rows = tok_rows * 4 * (width // (3 * HD))
     return pl.pallas_call(
         pack_kernel,
         in_specs=[pl.BlockSpec(memory_space=pltpu.HBM)] * 5,
-        out_specs=pl.BlockSpec(memory_space=pltpu.HBM),
-        out_shape=jax.ShapeDtypeStruct((out_rows, HD), jnp.bfloat16),
+        out_specs=[pl.BlockSpec(memory_space=pltpu.HBM)] * 2,
+        out_shape=[
+            pltpu.HBM((out_rows, HD), jnp.bfloat16),
+            pltpu.HBM((third_rows, HD), jnp.bfloat16),
+        ],
         scratch_shapes=[
             pltpu.VMEM((4, tok_rows, width), jnp.bfloat16),
             pltpu.VMEM((1, tok_rows), jnp.int32),
             pltpu.VMEM((tok_rows, HD), jnp.float32),
             pltpu.VMEM((out_rows, HD), jnp.bfloat16),
+            pltpu.VMEM((third_rows, HD), jnp.bfloat16),
             pltpu.SemaphoreType.DMA((chunks, 4)),
             pltpu.SemaphoreType.DMA((1,)),
             pltpu.SemaphoreType.DMA((chunks,)),
+            pltpu.SemaphoreType.DMA((1,)),
         ],
         compiler_params=pltpu.CompilerParams(vmem_limit_bytes=PACK_LIMIT),
         name="pack",
@@ -162,19 +184,133 @@
     return lax.dot_general(a, b, (((0,), (0,)), ((), ())), preferred_element_type=jnp.float32)
 
 
-def attend_kernel(
-    in_ref, factor_ref, sent_ref, out_ref, x_ref, lab_ref, fq_ref, fk_ref, g_ref,
-    s_ref, p_ref, dp_ref, pl_ref, ds_ref, e_ref, out_sem,
+def run_heads(heads, sums, x_ref, lab_ref, fq_ref, fk_ref, g_ref, s_ref, p_ref, dp_ref, pl_ref, ds_ref, e_ref):
+    total = x_ref.shape[1]
+    scale = HD**-0.5
+    label = lab_ref[...]
+    lane = lax.broadcasted_iota(jnp.int32, (total, HD), 1)
+    is0 = jnp.where(label == 0.0, 1.0, 0.0)
+    is1 = jnp.where(label == 1.0, 1.0, 0.0)
+    empty = jnp.where(label < 0.0, 1.0, 0.0)
+    fk_ref[...] = jnp.where(
+        lane == 0, is0, jnp.where(lane == 1, is1, jnp.where(lane == 2, empty, 0.0))
+    ).astype(jnp.bfloat16)
+    fq_ref[...] = jnp.where(
+        lane == 0,
+        (is0 - 1.0) * MASK_FILL,
+        jnp.where(lane == 1, (is1 - 1.0) * MASK_FILL, jnp.where(lane == 2, -MASK_FILL, 0.0)),
+    ).astype(jnp.bfloat16)
+
+    steps = [(head, block) for head in range(heads) for block in range(total // BLOCK)]
+
+    def rows_of(step):
+        return slice(steps[step][1] * BLOCK, (steps[step][1] + 1) * BLOCK)
+
+    def score_parts(step):
+        head, at, slot = steps[step][0], rows_of(step), step % 2
+
+        def part(n):
+            cols = slice(n, n + NCUT)
+            key_wide = jnp.concatenate([x_ref[head * 4 + 1, cols, :], fk_ref[cols, :]], axis=1)
+            query_wide = jnp.concatenate([x_ref[head * 4, at, :], fq_ref[at, :]], axis=1)
+            s_ref[slot, :, cols] = nt_dot(query_wide, key_wide)
+
+        return [functools.partial(part, n) for n in range(0, total, NCUT)]
+
+    def soft_parts(step):
+        slot = step % 2
+
+        def part(r):
+            rows = slice(r, r + STRIP)
+            scores = s_ref[slot, rows, :]
+            largest = jnp.max(scores, axis=1, keepdims=True)
+            expo = jnp.exp2((scores - largest) * (scale * LOG2E))
+            probs = expo * (1.0 / jnp.sum(expo, axis=1, keepdims=True))
+            p_ref[slot, rows, :] = probs
+            pl_ref[slot, rows, :] = probs.astype(jnp.bfloat16)
+
+        return [functools.partial(part, r) for r in range(0, BLOCK, STRIP)]
+
+    def error_part(step, sums):
+        head, at, slot = steps[step][0], rows_of(step), step % 2
+        s0, s1 = sums
+        output = jnp.dot(pl_ref[slot], x_ref[head * 4 + 2], preferred_element_type=jnp.float32)
+        error = output - x_ref[head * 4 + 3, at, :].astype(jnp.float32)
+        lab = lab_ref[at, :]
+        error = jnp.where(lab >= 0.0, error, 0.0)
+        square = error * error
+        s0 = s0 + jnp.sum(jnp.where(lab == 0.0, square, 0.0), axis=0, keepdims=True)
+        s1 = s1 + jnp.sum(jnp.where(lab == 1.0, square, 0.0), axis=0, keepdims=True)
+        e_ref[slot] = error.astype(jnp.bfloat16)
+        return s0, s1
+
+    def grad_prob_parts(step):
+        head, slot = steps[step][0], step % 2
+
+        def part(n):
+            cols = slice(n, n + NCUT)
+            dp_ref[slot, :, cols] = nt_dot(e_ref[slot], x_ref[head * 4 + 2, cols, :])
+
+        return [functools.partial(part, n) for n in range(0, total, NCUT)]
+
+    def grad_score_parts(step):
+        slot = step % 2
+
+        def part(r):
+            rows = slice(r, r + STRIP)
+            grad_probs = dp_ref[slot, rows, :]
+            probs = p_ref[slot, rows, :]
+            inner = jnp.sum(probs * grad_probs, axis=1, keepdims=True)
+            ds_ref[slot, rows, :] = (probs * (grad_probs - inner)).astype(jnp.bfloat16)
+
+        return [functools.partial(part, r) for r in range(0, BLOCK, STRIP)]
+
+    def grad_parts(step):
+        (head, block), at, slot = steps[step], rows_of(step), step % 2
+
+        def add(index, value):
+            if block == 0:
+                g_ref[index] = value
+            else:
+                g_ref[index] += value
+
+        def part_q():
+            g_ref[head * 3, at, :] = (
+                jnp.dot(ds_ref[slot], x_ref[head * 4 + 1], preferred_element_type=jnp.float32) * scale
+            )
+
+        def part_k():
+            add(head * 3 + 1, tn_dot(ds_ref[slot], x_ref[head * 4, at, :]) * scale)
+
+        def part_v():
+            add(head * 3 + 2, tn_dot(pl_ref[slot], e_ref[slot]))
+
+        return [part_v, part_q, part_k]
+
+    def weave(first, second):
+        count = max(len(first), len(second))
+        for i in range(count):
+            for parts in (first, second):
+                for part in parts[i * len(parts) // count : (i + 1) * len(parts) // count]:
+                    part()
+
+    weave(score_parts(0), [])
+    weave(soft_parts(0), [])
+    for step in range(len(steps)):
+        more = step + 1 < len(steps)
+        sums = error_part(step, sums)
+        weave(grad_prob_parts(step), [])
+        weave(grad_score_parts(step), score_parts(step + 1) if more else [])
+        weave(grad_parts(step), soft_parts(step + 1) if more else [])
+    return sums
+
+
+def first_kernel(
+    in_ref, g_out, lab_ref, sums_ref, x_ref, fq_ref, fk_ref, g_ref, *scratch
 ):
     total = x_ref.shape[1]
     row = row_iota()
     front = lax.broadcasted_iota(jnp.int32, (8, HD), 1) < HD // 2
-    out_part = out_ref.shape[0] // PARTS
-
-    def emit(part):
-        at = pl.ds(part * out_part, out_part)
-        return pltpu.make_async_copy(out_ref.at[at], sent_ref.at[at], out_sem.at[part])
-
 
     def sort_in(i, carry):
         base = pl.multiple_of(i * (8 * IN_ROWS), 8 * IN_ROWS)
@@ -202,129 +338,59 @@
         return carry
 
     lax.fori_loop(0, total // 32, sort_in, 0, unroll=4)
-
+    zero = jnp.zeros((1, HD), jnp.float32)
+    s0, s1 = run_heads(2, (zero, zero), x_ref, lab_ref, fq_ref, fk_ref, g_ref, *scratch)
+    sums_ref[...] = jnp.where(row == 0, s0, jnp.where(row == 1, s1, 0.0))
+    for j in range(6):
+        g_out[j] = g_ref[j].astype(jnp.bfloat16)
+
+
+def last_kernel(
+    here_ref, g_in, lab_ref, sums_ref, factor_ref, *refs, z_size
+):
+    block_refs = refs[:z_size]
+    sent_ref, out_ref, x_ref, fq_ref, fk_ref, g_ref = refs[z_size : z_size + 6]
+    scratch, out_sem = refs[z_size + 6 : -1], refs[-1]
+    total = x_ref.shape[1]
+    out_part = out_ref.shape[0] // PARTS
+
+    def emit(part):
+        at = pl.ds(part * out_part, out_part)
+        return pltpu.make_async_copy(out_ref.at[at], sent_ref.at[at], out_sem.at[part])
+
+    row = row_iota()
+    z_here, x_here, y_here, c_here = (here_ref[i] for i in range(4))
+    y_odd, y_high, core_one = y_here % 2 == 1, y_here >= 2, c_here == 1
+    for k, block_ref in enumerate(block_refs):
+        block = block_ref[...].astype(jnp.float32)
+        for kx in range(4):
+            place = lax.bitwise_xor(x_here, kx) * z_size + lax.bitwise_xor(z_here, k)
+            at = pl.ds(pl.multiple_of(place * 32, 32), 32)
+            for part in range(2):
+                made = []
+                for ky in range(4):
+                    tiles = []
+                    for kc in range(2):
+                        start = (((part * 2 + kc) * 4 + ky) * 4 + kx) * 8
+                        tiles.append(block[start : start + 8])
+                    made.append(
+                        (jnp.where(core_one, tiles[1], tiles[0]), jnp.where(core_one, tiles[0], tiles[1]))
+                    )
+                for bit, flag in ((1, y_odd), (2, y_high)):
+                    made = [
+                        tuple(jnp.where(flag, made[i ^ bit][n], made[i][n]) for n in range(2)) for i in range(4)
+                    ]
+                upper = [jnp.where(row < CAP, one, shift(two, CAP)) for one, two in made]
+                lower = [jnp.where(row < CAP, shift(one, CAP), two) for one, two in made]
+                x_ref[part * 2, at, :] = jnp.concatenate(upper, axis=0).astype(jnp.bfloat16)
+                x_ref[part * 2 + 1, at, :] = jnp.concatenate(lower, axis=0).astype(jnp.bfloat16)
+
+    sums = (sums_ref[0:1, :], sums_ref[1:2, :])
+    s0, s1 = run_heads(1, sums, x_ref, lab_ref, fq_ref, fk_ref, g_ref, *scratch)
     label = lab_ref[...]
-    lane = lax.broadcasted_iota(jnp.int32, (total, HD), 1)
-    is0 = jnp.where(label == 0.0, 1.0, 0.0)
-    is1 = jnp.where(label == 1.0, 1.0, 0.0)
-    empty = jnp.where(label < 0.0, 1.0, 0.0)
-    fk_ref[...] = jnp.where(
-        lane == 0, is0, jnp.where(lane == 1, is1, jnp.where(lane == 2, empty, 0.0))
-    ).astype(jnp.bfloat16)
-    fq_ref[...] = jnp.where(
-        lane == 0,
-        (is0 - 1.0) * MASK_FILL,
-        jnp.where(lane == 1, (is1 - 1.0) * MASK_FILL, jnp.where(lane == 2, -MASK_FILL, 0.0)),
-    ).astype(jnp.bfloat16)
-    counts = (jnp.sum(is0, axis=0, keepdims=True), jnp.sum(is1, axis=0, keepdims=True))
-
-    scale = HD**-0.5
-
-    steps = [(head, block) for head in range(3) for block in range(total // BLOCK)]
-
-    def rows_of(step):
-        return slice(steps[step][1] * BLOCK, (steps[step][1] + 1) * BLOCK)
-
-    def score_parts(step):
-        head, at, slot = steps[step][0], rows_of(step), step % 2
-
-        def part(n):
-            cols = slice(n, n + NCUT)
-            key_wide = jnp.concatenate([x_ref[head * 4 + 1, cols, :], fk_ref[cols, :]], axis=1)
-            query_wide = jnp.concatenate([x_ref[head * 4, at, :], fq_ref[at, :]], axis=1)
-            s_ref[slot, :, cols] = nt_dot(query_wide, key_wide)
-
-        return [functools.partial(part, n) for n in range(0, total, NCUT)]
-
-    def soft_parts(step):
-        slot = step % 2
-
-        def part(r):
-            rows = slice(r, r + STRIP)
-            scores = s_ref[slot, rows, :]
-            largest = jnp.max(scores, axis=1, keepdims=True)
-            expo = jnp.exp2((scores - largest) * (scale * LOG2E))
-            probs = expo * (1.0 / jnp.sum(expo, axis=1, keepdims=True))
-            p_ref[slot, rows, :] = probs
-            pl_ref[slot, rows, :] = probs.astype(jnp.bfloat16)
-
-        return [functools.partial(part, r) for r in range(0, BLOCK, STRIP)]
-
-    def error_part(step, sums):
-        head, at, slot = steps[step][0], rows_of(step), step % 2
-        s0, s1 = sums
-        output = jnp.dot(pl_ref[slot], x_ref[head * 4 + 2], preferred_element_type=jnp.float32)
-        error = output - x_ref[head * 4 + 3, at, :].astype(jnp.float32)
-        lab = lab_ref[at, :]
-        error = jnp.where(lab >= 0.0, error, 0.0)
-        square = error * error
-        s0 = s0 + jnp.sum(jnp.where(lab == 0.0, square, 0.0), axis=0, keepdims=True)
-        s1 = s1 + jnp.sum(jnp.where(lab == 1.0, square, 0.0), axis=0, keepdims=True)
-        e_ref[slot] = error.astype(jnp.bfloat16)
-        return s0, s1
-
-    def grad_prob_parts(step):
-        head, slot = steps[step][0], step % 2
-
-        def part(n):
-            cols = slice(n, n + NCUT)
-            dp_ref[slot, :, cols] = nt_dot(e_ref[slot], x_ref[head * 4 + 2, cols, :])
-
-        return [functools.partial(part, n) for n in range(0, total, NCUT)]
-
-    def grad_score_parts(step):
-        slot = step % 2
-
-        def part(r):
-            rows = slice(r, r + STRIP)
-            grad_probs = dp_ref[slot, rows, :]
-            probs = p_ref[slot, rows, :]
-            inner = jnp.sum(probs * grad_probs, axis=1, keepdims=True)
-            ds_ref[slot, rows, :] = (probs * (grad_probs - inner)).astype(jnp.bfloat16)
-
-        return [functools.partial(part, r) for r in range(0, BLOCK, STRIP)]
-
-    def grad_parts(step):
-        (head, block), at, slot = steps[step], rows_of(step), step % 2
-
-        def add(index, value):
-            if block == 0:
-                g_ref[index] = value
-            else:
-                g_ref[index] += value
-
-        def part_q():
-            g_ref[head * 3, at, :] = (
-                jnp.dot(ds_ref[slot], x_ref[head * 4 + 1], preferred_element_type=jnp.float32) * scale
-            )
-
-        def part_k():
-            add(head * 3 + 1, tn_dot(ds_ref[slot], x_ref[head * 4, at, :]) * scale)
-
-        def part_v():
-            add(head * 3 + 2, tn_dot(pl_ref[slot], e_ref[slot]))
-
-        return [part_v, part_q, part_k]
-
-    def weave(first, second):
-        count = max(len(first), len(second))
-        for i in range(count):
-            for parts in (first, second):
-                for part in parts[i * len(parts) // count : (i + 1) * len(parts) // count]:
-                    part()
-
-    zero = jnp.zeros((1, HD), jnp.float32)
-    sums = (zero, zero)
-    weave(score_parts(0), [])
-    weave(soft_parts(0), [])
-    for step in range(len(steps)):
-        more = step + 1 < len(steps)
-        sums = error_part(step, sums)
-        weave(grad_prob_parts(step), [])
-        weave(grad_score_parts(step), score_parts(step + 1) if more else [])
-        weave(grad_parts(step), soft_parts(step + 1) if more else [])
-    s0, s1 = sums
-
+    counts = tuple(
+        jnp.sum(jnp.where(label == clip, 1.0, 0.0), axis=0, keepdims=True) for clip in (0.0, 1.0)
+    )
     parts = []
     for clip, (acc, count) in enumerate(zip((s0, s1), counts)):
         both = factor_ref[:, :HD] / (count * WIDTH)
@@ -346,7 +412,8 @@
 
     def sort_out(i, carry):
         at = pl.ds(pl.multiple_of(i * 32, 32), 32)
-        grads = [g_ref[j, at, :] for j in range(OUT_PIECES)]
+        grads = [g_in[j, at, :].astype(jnp.float32) for j in range(6)]
+        grads += [g_ref[j, at, :] for j in range(3)]
         labs = lab_ref[at, :]
         pieces = []
         for u in range(4):
@@ -370,31 +437,55 @@
         emit(part).wait()
 
 
-def attend(arrived, factors, sources):
+def scratch_of(heads, total):
+    return [
+        pltpu.VMEM((4 * heads, total, HD), jnp.bfloat16),
+        pltpu.VMEM((total, HD), jnp.bfloat16),
+        pltpu.VMEM((total, HD), jnp.bfloat16),
+        pltpu.VMEM((3 * heads, total, HD), jnp.float32),
+        pltpu.VMEM((2, BLOCK, total), jnp.float32),
+        pltpu.VMEM((2, BLOCK, total), jnp.float32),
+        pltpu.VMEM((2, BLOCK, total), jnp.float32),
+        pltpu.VMEM((2, BLOCK, total), jnp.bfloat16),
+        pltpu.VMEM((2, BLOCK, total), jnp.bfloat16),
+        pltpu.VMEM((2, BLOCK, HD), jnp.bfloat16),
+    ]
+
+
+def attend_first(arrived, sources):
     total = sources * CAP
+    inside = pl.BlockSpec(memory_space=pltpu.VMEM)
     return pl.pallas_call(
-        attend_kernel,
-        in_specs=[pl.BlockSpec(memory_space=pltpu.VMEM)] * 2,
+        first_kernel,
+        in_specs=[inside],
+        out_specs=[inside] * 3,
+        out_shape=[
+            jax.ShapeDtypeStruct((6, total, HD), jnp.bfloat16),
+            jax.ShapeDtypeStruct((total, HD), jnp.float32),
+            jax.ShapeDtypeStruct((8, HD), jnp.float32),
+        ],
+        scratch_shapes=scratch_of(2, total),
+        compiler_params=pltpu.CompilerParams(vmem_limit_bytes=ATTEND_LIMIT),
+        cost_estimate=pl.CostEstimate(flops=2 * 12 * total * total * HD, bytes_accessed=2**23, transcendentals=2 * total * total),
+        name="attend_first",
+    )(arrived)
+
+
+def attend_last(grads, labels, sums, factors, blocks, here, sources):
+    total = sources * CAP
+    inside = pl.BlockSpec(memory_space=pltpu.VMEM)
+    return pl.pallas_call(
+        functools.partial(last_kernel, z_size=len(blocks)),
+        in_specs=[pl.BlockSpec(memory_space=pltpu.SMEM)] + [inside] * (4 + len(blocks)),
         out_specs=pl.BlockSpec(memory_space=pltpu.HBM),
         out_shape=pltpu.HBM((sources * OUT_ROWS, HD), jnp.bfloat16),
-        scratch_shapes=[
-            pltpu.VMEM((sources * OUT_ROWS, HD), jnp.bfloat16),
-            pltpu.VMEM((12, total, HD), jnp.bfloat16),
-            pltpu.VMEM((total, HD), jnp.float32),
-            pltpu.VMEM((total, HD), jnp.bfloat16),
-            pltpu.VMEM((total, HD), jnp.bfloat16),
-            pltpu.VMEM((9, total, HD), jnp.float32),
-            pltpu.VMEM((2, BLOCK, total), jnp.float32),
-            pltpu.VMEM((2, BLOCK, total), jnp.float32),
-            pltpu.VMEM((2, BLOCK, total), jnp.float32),
-            pltpu.VMEM((2, BLOCK, total), jnp.bfloat16),
-            pltpu.VMEM((2, BLOCK, total), jnp.bfloat16),
-            pltpu.VMEM((2, BLOCK, HD), jnp.bfloat16),
-            pltpu.SemaphoreType.DMA((PARTS,)),
-        ],
+        scratch_shapes=[pltpu.VMEM((sources * OUT_ROWS, HD), jnp.bfloat16)]
+        + scratch_of(1, total)
+        + [pltpu.SemaphoreType.DMA((PARTS,))],
         compiler_params=pltpu.CompilerParams(vmem_limit_bytes=ATTEND_LIMIT),
-        name="attend",
-    )(arrived, factors)
+        cost_estimate=pl.CostEstimate(flops=12 * total * total * HD, bytes_accessed=2**23, transcendentals=total * total),
+        name="attend_last",
+    )(here, grads, labels, sums, factors, *blocks)
 
 
 def unpack_kernel(
@@ -474,14 +565,50 @@
     )(here, returned)
 
 
+def pick(array, index, dim):
+    return lax.dynamic_slice_in_dim(array, index, 1, dim)
+
+
+def spread_third(third, seq_size, groups):
+    s_here, d_here = lax.axis_index("seq"), lax.axis_index("dp")
+    c_here, y_here = lax.rem(s_here, 2), lax.div(s_here, 2)
+    x_here, z_here = lax.div(d_here, Z_SIZE), lax.rem(d_here, Z_SIZE)
+    y_size, x_size = seq_size // 2, groups // Z_SIZE
+    xor = lax.bitwise_xor
+
+    def send(array, axis, distance, whole):
+        return lax.ppermute(array, axis, [(i, i ^ distance) for i in range(whole)])
+
+    array = third.reshape(2, 2, y_size, x_size, Z_SIZE, 8, HD)
+    other = send(pick(array, xor(c_here, 1), 1), "seq", 1, seq_size)
+    array = jnp.concatenate([pick(array, c_here, 1), other], axis=1)
+
+    def both_ways(first, second):
+        outs = [pick(first, xor(y_here, k), 1) for k in range(y_size)]
+        outs += [pick(second, xor(x_here, k), 2) for k in range(x_size)]
+        outs = lax.optimization_barrier(outs)
+        came = [send(out, "seq", 2 * k, seq_size) if k else out for k, out in enumerate(outs[:y_size])]
+        came += [send(out, "dp", Z_SIZE * k, groups) if k else out for k, out in enumerate(outs[y_size:])]
+        came = lax.optimization_barrier(came)
+        return jnp.concatenate(came[:y_size], axis=1), jnp.concatenate(came[y_size:], axis=2)
+
+    front, back = both_ways(array[0], array[1])
+    back, front = both_ways(back, front)
+    array = jnp.stack([front, back])
+    outs = [pick(array, xor(z_here, k), 4).reshape(-1, HD) for k in range(Z_SIZE)]
+    outs = lax.optimization_barrier(outs)
+    return [send(out, "dp", k, groups) if k > 1 else out for k, out in enumerate(outs)]
+
+
 def shards(queries, key_rows, values, target, row_clip, ratios, ref_loss, noise_level):
     seq_size = lax.axis_size("seq")
     devices = lax.axis_size("dp") * seq_size
     tok_rows = queries.shape[0]
-    sent = pack(queries, key_rows, values, target, row_clip.reshape(1, tok_rows))
+    sent, third = pack(queries, key_rows, values, target, row_clip.reshape(1, tok_rows))
     sent = sent.reshape(devices * IN_ROWS // TAIL, TAIL, HD)
     arrived = lax.all_to_all(sent, ("dp", "seq"), split_axis=0, concat_axis=0, tiled=True)
     arrived = arrived.reshape(devices * IN_ROWS, HD)
+    blocks = spread_third(third, seq_size, devices // seq_size)
     weight_level = level_weight(noise_level)
     step = ratios / ref_loss * (2.0 * LOSS_SCALE)
     factors = jnp.concatenate(
@@ -489,7 +616,13 @@
         + [jnp.broadcast_to(step[:, c : c + 1], (1, HD)) for c in range(CLIPS_G)],
         axis=1,
     )
-    grads = attend(arrived, factors, devices)
+    first = attend_first(arrived, devices)
+    near, first = lax.optimization_barrier((blocks[1], first))
+    blocks[1] = lax.ppermute(near, "dp", [(i, i ^ 1) for i in range(devices // seq_size)])
+    s_here, d_here = lax.axis_index("seq"), lax.axis_index("dp")
+    places = (lax.rem(d_here, Z_SIZE), lax.div(d_here, Z_SIZE), lax.div(s_here, 2), lax.rem(s_here, 2))
+    places = jnp.stack([place.astype(jnp.int32) for place in places])
+    grads = attend_last(*first, factors, blocks, places, devices)
     grads = grads.reshape(devices * OUT_ROWS // TAIL, TAIL, HD)
     returned = lax.all_to_all(grads, ("dp", "seq"), split_axis=0, concat_axis=0, tiled=True)
     returned = returned.reshape(devices * OUT_ROWS, HD)

time: 186 us -> 186 us (level)
  waiting for transfers between devices: 137 us -> 31.9 us
  blocking collectives: 0 us -> 73.5 us
  starting transfers between devices: 22.2 us -> 46.3 us
  local copies, waits for them, and re-layouts: 1.91 us -> 4.52 us
  Pallas kernels: 22.8 us -> 25.1 us
  other arithmetic: 0.01 us -> 2.23 us
    all_to_all x1, waiting for transfers between devices: 75.7 us -> 0.01 us  [shards(): lax.all_to_all(sent, ('dp', 'seq'), split_axis=0, concat_axis=0, tiled=True)]
    all_to_all x0 -> x1, blocking collectives: none -> 73.5 us  [shards(): lax.all_to_all(grads, ('dp', 'seq'), split_axis=0, concat_axis=0, tiled=T...]
    all_to_all x1 -> x0, waiting for transfers between devices: 61.7 us -> none  [shards(): lax.all_to_all(grads, ('dp', 'seq'), split_axis=0, concat_axis=0, tiled=T...]
    ppermute x0 -> x20, waiting for transfers between devices: none -> 31.9 us  [the longest x19 31.9 us: send(): return lax.ppermute(array, axis, [(i, i ^ distance) for i in range(whole)])]
    ppermute x0 -> x20, starting transfers between devices: none -> 30.6 us  [the longest x19 29.4 us: send(): return lax.ppermute(array, axis, [(i, i ^ distance) for i in range(whole)])]
    all_to_all x1 -> x0, starting transfers between devices: 6.5 us -> none  [shards(): lax.all_to_all(grads, ('dp', 'seq'), split_axis=0, concat_axis=0, tiled=T...]
    dynamic_slice x0 -> x8, local copies, waits for them, and re-layouts: none -> 2.53 us  [pick(): return lax.dynamic_slice_in_dim(array, index, 1, dim)]
    another operation x0 -> x5, other arithmetic: none -> 2.1 us  [the longest x4 2.03 us: spread_third(): array = jnp.stack([front, back])]
  transfers between devices with their start and end apart: 2 -> 21, of which waited for: 2 -> 11; matrix products, arithmetic and copies ran while one was open for 1% -> 4% of each run, Pallas kernels for 0% -> 6%
where the time goes in v4:
time: 186 us; the launch traced here: 185 us
  blocking collectives  73.5 us (40%)
  starting transfers between devices  46.3 us (25%)
  waiting for transfers between devices  31.9 us (17%)
  Pallas kernels  25.1 us (13%)
  local copies, waits for them, and re-layouts  4.52 us (2%)
  other arithmetic  2.23 us (1%)
  between operations  1.92 us (1%)
    all_to_all x1, blocking collectives, shards(): lax.all_to_all(grads, ('dp', 'seq'), split_axis=0, concat_axis=0, tiled=T...  73.5 us
    ppermute x19, waiting for transfers between devices, send(): return lax.ppermute(array, axis, [(i, i ^ distance) for i in range(whole)])  31.9 us
    ppermute x19, starting transfers between devices, send(): return lax.ppermute(array, axis, [(i, i ^ distance) for i in range(whole)])  29.4 us
    all_to_all x1, starting transfers between devices, shards(): lax.all_to_all(sent, ('dp', 'seq'), split_axis=0, concat_axis=0, tiled=True)  15.7 us
    pallas_call x1, Pallas kernels, attend_first(): pl.pallas_call(first_kernel, in_specs=[inside], out_specs=[inside] * 3, o...  10.4 us
    pallas_call x1, Pallas kernels, attend_last(): pl.pallas_call(functools.partial(last_kernel, z_size=len(blocks)), in_spe...  8.02 us
    pallas_call x1, Pallas kernels, pack(): pl.pallas_call(pack_kernel, in_specs=[pl.BlockSpec(memory_space=pltpu.HBM...  4.16 us
  transfers between devices with their start and end apart: 21, of which 11 were waited for; matrix products, arithmetic and copies ran while one was open for 4% of the time, Pallas kernels for 6%

profile of v4, /device:TPU:1, one launch (start us, length us, event | category | flops | bytes accessed | tf_op | source)
XLA Modules:
  0.0 185.5 jit_solution(9077485243455124160)
XLA Ops:
  0.6 4.2 %pack.1 = (bf16[8704,128]{1,0:T(8,128)(2,1)}, bf16[4096,128]{1,0:T(8,128)(2,1)}) custom-call(bf16[128,3072]{1,0:T(8,128)(2,1)} %q_ref.1, bf16[128,3072]{1,0:T(8,128)(2,1)} %k_ref.1, bf16[128,3072]{1,0:T(8,128)(2,1)} %v_ref.1, bf16[128,3072]{1,0:T(8,128)(2,1)} %t_ref.1, s32[1,128]{1,0:T(1,128)} %bitcast.52), custom_call_target="tpu_custom_call" | custom-call | tf_op jit(solution)/shard_map/pack/pallas_call | solution.py:148
  4.8 15.7 %all-to-all-start = ((bf16[4352,2,128]{2,1,0:T(2,128)(2,1)}), bf16[4352,2,128]{2,1,0:T(2,128)(2,1)S(1)}, u32[]{:S(2)}, u32[]{:S(2)}) async-start(bf16[4352,2,128]{2,1,0:T(2,128)(2,1)} %bitcast.46), calls=%async_computation | async-start | bytes 4456448 | tf_op jit(solution)/shard_map/all_to_all | solution.py:609
  20.5 2.1 %constant_dynamic-slice_fusion.12 = (bf16[2,1,4,4,8,8,128]{6,5,4,3,2,1,0:T(8,128)(2,1)}, bf16[2,1,4,4,8,8,128]{6,5,4,3,2,1,0:T(8,128)(2,1)S(1)}) fusion(bf16[2,2,4,4,8,8,128]{6,5,4,3,2,1,0:T(8,128)(2,1)} %bitcast.47, s32[]{:T(128)S(6)} %select_n.63, s32[]{:T(128)S(6)} %select_n.62), kind=kLoop, calls=%fused_computation.69 | loop fusion | bytes 2097160 | tf_op jit(solution)/shard_map/dynamic_slice | solution.py:569
  22.6 2.1 %collective-permute-start = (bf16[2,1,4,4,8,8,128]{6,5,4,3,2,1,0:T(8,128)(2,1)}, bf16[2,1,4,4,8,8,128]{6,5,4,3,2,1,0:T(8,128)(2,1)S(1)}, u32[]{:S(2)}, u32[]{:S(2)}) collective-permute-start(bf16[2,1,4,4,8,8,128]{6,5,4,3,2,1,0:T(8,128)(2,1)} %get-tuple-element.114), channel_id=1, source_target_pairs={{0,1},{1,0},{2,3},{3,2},{4,5},{5,4},{6,7},{7,6},{8,9},{9,8},{10,11... | collective-permute-start | bytes 1572872 | tf_op jit(solution)/shard_map/ppermute | solution.py:580
  24.7 1.7 collective-permute-done
  26.5 0.1 fusion
  26.6 0.1 fusion.9
  26.7 0.1 copy_bitcast_fusion.4
  26.7 0.1 copy_bitcast_fusion
  26.8 0.1 copy_bitcast_fusion.6
  26.8 0.1 copy_bitcast_fusion.2
  26.9 0.1 collective-permute-start.1
  27.0 2.0 %collective-permute-start.2 = (bf16[2,1,4,8,8,128]{5,4,2,1,0,3:T(8,128)(2,1)S(1)}, bf16[2,1,4,8,8,128]{5,4,2,1,0,3:T(8,128)(2,1)S(1)}, u32[]{:S(2)}, u32[]{:S(2)}) collective-permute-start(bf16[2,1,4,8,8,128]{5,4,2,1,0,3:T(8,128)(2,1)S(1)} %get-tuple-element.56), channel_id=1, source_target_pairs={{0,4},{1,5},{2,6},{3,7},{4,0},{5,1},{6,2},{7,3},{8,12},{9,13},{10,... | collective-permute-start | bytes 393224 | tf_op jit(solution)/shard_map/ppermute | solution.py:580
  29.1 1.8 collective-permute-start.3
  30.9 2.0 %collective-permute-start.5 = (bf16[2,4,1,8,8,128]{5,4,2,1,0,3:T(8,128)(2,1)S(1)}, bf16[2,4,1,8,8,128]{5,4,2,1,0,3:T(8,128)(2,1)S(1)}, u32[]{:S(2)}, u32[]{:S(2)}) collective-permute-start(bf16[2,4,1,8,8,128]{5,4,2,1,0,3:T(8,128)(2,1)S(1)} %get-tuple-element.60), channel_id=1, source_target_pairs={{0,128},{8,136},{16,144},{24,152},{32,160},{40,168},{48,176},{56,1... | collective-permute-start | bytes 393224 | tf_op jit(solution)/shard_map/ppermute | solution.py:580
  32.9 0.6 collective-permute-done.1
  33.5 1.2 collective-permute-start.6
  34.7 4.8 %collective-permute-done.2 = bf16[2,1,4,8,8,128]{5,4,2,1,0,3:T(8,128)(2,1)S(1)} collective-permute-done((bf16[2,1,4,8,8,128]{5,4,2,1,0,3:T(8,128)(2,1)S(1)}, bf16[2,1,4,8,8,128]{5,4,2,1,0,3:T(8,128)(2,1)S(1)}, u32[]{:S(2)}, u32[]{:S(2)}) %collective-permute-start.2) | collective-permute-done | bytes 131104 | tf_op jit(solution)/shard_map/ppermute | solution.py:580
  39.5 3.4 %collective-permute-done.3 = bf16[2,1,4,8,8,128]{5,4,2,1,0,3:T(8,128)(2,1)S(1)} collective-permute-done((bf16[2,1,4,8,8,128]{5,4,2,1,0,3:T(8,128)(2,1)S(1)}, bf16[2,1,4,8,8,128]{5,4,2,1,0,3:T(8,128)(2,1)S(1)}, u32[]{:S(2)}, u32[]{:S(2)}) %collective-permute-start.3) | collective-permute-done | bytes 131104 | tf_op jit(solution)/shard_map/ppermute | solution.py:580
  42.9 3.2 %collective-permute-done.6 = bf16[2,4,1,8,8,128]{5,4,2,1,0,3:T(8,128)(2,1)S(1)} collective-permute-done((bf16[2,4,1,8,8,128]{5,4,2,1,0,3:T(8,128)(2,1)S(1)}, bf16[2,4,1,8,8,128]{5,4,2,1,0,3:T(8,128)(2,1)S(1)}, u32[]{:S(2)}, u32[]{:S(2)}) %collective-permute-start.6) | collective-permute-done | bytes 131104 | tf_op jit(solution)/shard_map/ppermute | solution.py:580
  46.4 0.1 constant_dynamic-slice_fusion
  46.6 1.4 collective-permute-start.7
  47.9 1.4 collective-permute-start.8
  49.3 1.2 collective-permute-start.9
  50.5 3.4 %collective-permute-start.11 = (bf16[2,4,1,8,8,128]{5,4,2,1,0,3:T(8,128)(2,1)S(1)}, bf16[2,4,1,8,8,128]{5,4,2,1,0,3:T(8,128)(2,1)}, u32[]{:S(2)}, u32[]{:S(2)}) collective-permute-start(bf16[2,4,1,8,8,128]{5,4,2,1,0,3:T(8,128)(2,1)S(1)} %get-tuple-element.76), channel_id=1, source_target_pairs={{0,128},{8,136},{16,144},{24,152},{32,160},{40,168},{48,176},{56,1... | collective-permute-start | bytes 393224 | tf_op jit(solution)/shard_map/ppermute | solution.py:580
  53.9 0.5 collective-permute-start.12
  54.4 0.6 fusion.13
  55.0 3.6 %collective-permute-done.8 = bf16[2,1,4,8,8,128]{5,4,2,1,0,3:T(8,128)(2,1)S(1)} collective-permute-done((bf16[2,1,4,8,8,128]{5,4,2,1,0,3:T(8,128)(2,1)S(1)}, bf16[2,1,4,8,8,128]{5,4,2,1,0,3:T(8,128)(2,1)S(1)}, u32[]{:S(2)}, u32[]{:S(2)}) %collective-permute-start.8) | collective-permute-done | bytes 131104 | tf_op jit(solution)/shard_map/ppermute | solution.py:580
  58.6 3.0 %collective-permute-done.9 = bf16[2,1,4,8,8,128]{5,4,2,1,0,3:T(8,128)(2,1)S(1)} collective-permute-done((bf16[2,1,4,8,8,128]{5,4,2,1,0,3:T(8,128)(2,1)S(1)}, bf16[2,1,4,8,8,128]{5,4,2,1,0,3:T(8,128)(2,1)S(1)}, u32[]{:S(2)}, u32[]{:S(2)}) %collective-permute-start.9) | collective-permute-done | bytes 131104 | tf_op jit(solution)/shard_map/ppermute | solution.py:580
  61.6 0.7 collective-permute-done.11
  62.3 3.6 %collective-permute-done.12 = bf16[2,4,1,8,8,128]{5,4,2,1,0,3:T(8,128)(2,1)} collective-permute-done((bf16[2,4,1,8,8,128]{5,4,2,1,0,3:T(8,128)(2,1)S(1)}, bf16[2,4,1,8,8,128]{5,4,2,1,0,3:T(8,128)(2,1)}, u32[]{:S(2)}, u32[]{:S(2)}) %collective-permute-start.12) | collective-permute-done | bytes 131104 | tf_op jit(solution)/shard_map/ppermute | solution.py:580
  65.9 1.1 maximum_bitcast_fusion
  67.0 0.1 maximum_bitcast_fusion.1
  67.1 0.8 fusion.1
  67.9 3.4 %collective-permute-start.15 = (bf16[512,128]{1,0:T(8,128)(2,1)}, bf16[512,128]{1,0:T(8,128)(2,1)S(1)}, u32[]{:S(2)}, u32[]{:S(2)}) collective-permute-start(bf16[512,128]{1,0:T(8,128)(2,1)} %bitcast.20), channel_id=1, source_target_pairs={{0,24},{8,16},{16,8},{24,0},{32,56},{40,48},{48,40},{56,32},{64,88... | collective-permute-start | bytes 393224 | tf_op jit(solution)/shard_map/ppermute | solution.py:580
  71.3 4.6 %collective-permute-start.16 = (bf16[512,128]{1,0:T(8,128)(2,1)}, bf16[512,128]{1,0:T(8,128)(2,1)S(1)}, u32[]{:S(2)}, u32[]{:S(2)}) collective-permute-start(bf16[512,128]{1,0:T(8,128)(2,1)} %bitcast.21), channel_id=1, source_target_pairs={{0,32},{8,40},{16,48},{24,56},{32,0},{40,8},{48,16},{56,24},{64,96... | collective-permute-start | bytes 393224 | tf_op jit(solution)/shard_map/ppermute | solution.py:580
  75.9 4.2 %collective-permute-start.18 = (bf16[512,128]{1,0:T(8,128)(2,1)S(1)}, bf16[512,128]{1,0:T(8,128)(2,1)S(1)}, u32[]{:S(2)}, u32[]{:S(2)}) collective-permute-start(bf16[512,128]{1,0:T(8,128)(2,1)S(1)} %bitcast.48), channel_id=1, source_target_pairs={{0,48},{8,56},{16,32},{24,40},{32,16},{40,24},{48,0},{56,8},{64,11... | collective-permute-start | bytes 393224 | tf_op jit(solution)/shard_map/ppermute | solution.py:580
  80.1 10.4 %attend_first.1 = (bf16[6,1024,128]{2,1,0:T(8,128)(2,1)S(1)}, f32[1024,128]{1,0:T(8,128)S(1)}, f32[8,128]{1,0:T(8,128)S(1)}) custom-call(bf16[8704,128]{1,0:T(8,128)(2,1)S(1)} %bitcast.43), custom_call_target="tpu_custom_call" | custom-call | flops 3221225472 | bytes 8388608 | tf_op jit(solution)/shard_map/attend_first/pallas_call | solution.py:458
  90.6 0.1 collective-permute-start.19
  90.7 1.2 collective-permute-start.13
  91.9 0.1 pad_add_fusion.here_ref
  92.7 0.6 broadcast_in_dim.21
  93.3 0.6 broadcast_in_dim.19
  94.0 1.4 collective-permute-done.17.refs_5_
  95.4 5.8 %collective-permute-done.19.refs_7_ = bf16[512,128]{1,0:T(8,128)(2,1)S(1)} collective-permute-done((bf16[512,128]{1,0:T(8,128)(2,1)S(1)}, bf16[512,128]{1,0:T(8,128)(2,1)S(1)}, u32[]{:S(2)}, u32[]{:S(2)}) %collective-permute-start.19) | collective-permute-done | bytes 131104 | tf_op jit(solution)/shard_map/ppermute | solution.py:580
  101.2 8.0 %attend_last.1 = bf16[9728,128]{1,0:T(8,128)(2,1)} custom-call(s32[4]{0:T(128)S(1)} %pad_add_fusion.here_ref, bf16[6,1024,128]{2,1,0:T(8,128)(2,1)S(1)} %get-tuple-element.91.g_in, f32[1024,128]{1,0:T(8,128)S(1)} %get-tuple-element.92.lab_ref, f32[8,128]{1,0:T(8,128)S(1)} %get-tuple-element.93.sums_ref, f32[1,384]{1,0:T(1,128)S(1)} %reshape_maximum_fusion.factor_ref, ...), custom_call_target="tpu_custom_call" | custom-call | flops 1610612736 | bytes 8388608 | tf_op jit(solution)/shard_map/attend_last/pallas_call | solution.py:477
  109.3 73.5 %all_to_all.10 = bf16[4864,2,128]{2,1,0:T(2,128)(2,1)S(1)} all-to-all(bf16[4864,2,128]{2,1,0:T(2,128)(2,1)} %bitcast.45), channel_id=1, replica_groups=mesh['dp'=32,'seq'=8] {'dp','seq'}, dimensions={0} | all-to-all | bytes 4980736 | tf_op jit(solution)/shard_map/all_to_all | solution.py:627
  182.8 2.5 %unpack.1 = (bf16[128,3072]{1,0:T(8,128)(2,1)}, bf16[128,3072]{1,0:T(8,128)(2,1)}, bf16[128,3072]{1,0:T(8,128)(2,1)}, f32[1,2]{1,0:T(1,128)}) custom-call(s32[1]{0:T(128)} %bitcast.here_ref, bf16[9728,128]{1,0:T(8,128)(2,1)S(1)} %bitcast.42), custom_call_target="tpu_custom_call" | custom-call | tf_op jit(solution)/shard_map/unpack/pallas_call | solution.py:554
  (35 shorter events, 0.4 us)
Async XLA Ops:
  4.8 75.3 %all-to-all-start = ((bf16[4352,2,128]{2,1,0:T(2,128)(2,1)}), bf16[4352,2,128]{2,1,0:T(2,128)(2,1)S(1)}, u32[]{:S(2)}, u32[]{:S(2)}) async-start(bf16[4352,2,128]{2,1,0:T(2,128)(2,1)} %bitcast.46), calls=%async_computation | async-start | bytes 4456448 | tf_op jit(solution)/shard_map/all_to_all | solution.py:609
  22.6 3.9 %collective-permute-start = (bf16[2,1,4,4,8,8,128]{6,5,4,3,2,1,0:T(8,128)(2,1)}, bf16[2,1,4,4,8,8,128]{6,5,4,3,2,1,0:T(8,128)(2,1)S(1)}, u32[]{:S(2)}, u32[]{:S(2)}) collective-permute-start(bf16[2,1,4,4,8,8,128]{6,5,4,3,2,1,0:T(8,128)(2,1)} %get-tuple-element.114), channel_id=1, source_target_pairs={{0,1},{1,0},{2,3},{3,2},{4,5},{5,4},{6,7},{7,6},{8,9},{9,8},{10,11... | collective-permute-start | bytes 1572872 | tf_op jit(solution)/shard_map/ppermute | solution.py:580
  26.9 27.5 %copy-start = (f32[1,2]{1,0:T(1,128)S(1)}, f32[1,2]{1,0:T(1,128)}, u32[]{:S(2)}) copy-start(f32[1,2]{1,0:T(1,128)} %param.13) | copy-start | bytes 28
  26.9 27.4 %copy-start.1 = (f32[1,2]{1,0:T(1,128)S(1)}, f32[1,2]{1,0:T(1,128)}, u32[]{:S(2)}) copy-start(f32[1,2]{1,0:T(1,128)} %param.14) | copy-start | bytes 28
  26.9 6.6 %collective-permute-start.1 = (bf16[2,1,4,8,8,128]{5,4,2,1,0,3:T(8,128)(2,1)S(1)}, bf16[2,1,4,8,8,128]{5,4,2,1,0,3:T(8,128)(2,1)S(1)}, u32[]{:S(2)}, u32[]{:S(2)}) collective-permute-start(bf16[2,1,4,8,8,128]{5,4,2,1,0,3:T(8,128)(2,1)S(1)} %get-tuple-element.55), channel_id=1, source_target_pairs={{0,2},{1,3},{2,0},{3,1},{4,6},{5,7},{6,4},{7,5},{8,10},{9,11},{10,... | collective-permute-start | bytes 393224 | tf_op jit(solution)/shard_map/ppermute | solution.py:580
  27.0 12.5 %collective-permute-start.2 = (bf16[2,1,4,8,8,128]{5,4,2,1,0,3:T(8,128)(2,1)S(1)}, bf16[2,1,4,8,8,128]{5,4,2,1,0,3:T(8,128)(2,1)S(1)}, u32[]{:S(2)}, u32[]{:S(2)}) collective-permute-start(bf16[2,1,4,8,8,128]{5,4,2,1,0,3:T(8,128)(2,1)S(1)} %get-tuple-element.56), channel_id=1, source_target_pairs={{0,4},{1,5},{2,6},{3,7},{4,0},{5,1},{6,2},{7,3},{8,12},{9,13},{10,... | collective-permute-start | bytes 393224 | tf_op jit(solution)/shard_map/ppermute | solution.py:580
  29.1 13.8 %collective-permute-start.3 = (bf16[2,1,4,8,8,128]{5,4,2,1,0,3:T(8,128)(2,1)S(1)}, bf16[2,1,4,8,8,128]{5,4,2,1,0,3:T(8,128)(2,1)S(1)}, u32[]{:S(2)}, u32[]{:S(2)}) collective-permute-start(bf16[2,1,4,8,8,128]{5,4,2,1,0,3:T(8,128)(2,1)S(1)} %get-tuple-element.57), channel_id=1, source_target_pairs={{0,6},{1,7},{2,4},{3,5},{4,2},{5,3},{6,0},{7,1},{8,14},{9,15},{10,... | collective-permute-start | bytes 393224 | tf_op jit(solution)/shard_map/ppermute | solution.py:580
  30.9 12.0 %collective-permute-start.4 = (bf16[2,4,1,8,8,128]{5,4,2,1,0,3:T(8,128)(2,1)S(1)}, bf16[2,4,1,8,8,128]{5,4,2,1,0,3:T(8,128)(2,1)S(1)}, u32[]{:S(2)}, u32[]{:S(2)}) collective-permute-start(bf16[2,4,1,8,8,128]{5,4,2,1,0,3:T(8,128)(2,1)S(1)} %get-tuple-element.59), channel_id=1, source_target_pairs={{0,64},{8,72},{16,80},{24,88},{32,96},{40,104},{48,112},{56,120},{... | collective-permute-start | bytes 393224 | tf_op jit(solution)/shard_map/ppermute | solution.py:580
  30.9 12.0 %collective-permute-start.5 = (bf16[2,4,1,8,8,128]{5,4,2,1,0,3:T(8,128)(2,1)S(1)}, bf16[2,4,1,8,8,128]{5,4,2,1,0,3:T(8,128)(2,1)S(1)}, u32[]{:S(2)}, u32[]{:S(2)}) collective-permute-start(bf16[2,4,1,8,8,128]{5,4,2,1,0,3:T(8,128)(2,1)S(1)} %get-tuple-element.60), channel_id=1, source_target_pairs={{0,128},{8,136},{16,144},{24,152},{32,160},{40,168},{48,176},{56,1... | collective-permute-start | bytes 393224 | tf_op jit(solution)/shard_map/ppermute | solution.py:580
  33.5 12.6 %collective-permute-start.6 = (bf16[2,4,1,8,8,128]{5,4,2,1,0,3:T(8,128)(2,1)S(1)}, bf16[2,4,1,8,8,128]{5,4,2,1,0,3:T(8,128)(2,1)S(1)}, u32[]{:S(2)}, u32[]{:S(2)}) collective-permute-start(bf16[2,4,1,8,8,128]{5,4,2,1,0,3:T(8,128)(2,1)S(1)} %get-tuple-element.61), channel_id=1, source_target_pairs={{0,192},{8,200},{16,208},{24,216},{32,224},{40,232},{48,240},{56,2... | collective-permute-start | bytes 393224 | tf_op jit(solution)/shard_map/ppermute | solution.py:580
  46.6 7.4 %collective-permute-start.7 = (bf16[2,1,4,8,8,128]{5,4,2,1,0,3:T(8,128)(2,1)S(1)}, bf16[2,1,4,8,8,128]{5,4,2,1,0,3:T(8,128)(2,1)S(1)}, u32[]{:S(2)}, u32[]{:S(2)}) collective-permute-start(bf16[2,1,4,8,8,128]{5,4,2,1,0,3:T(8,128)(2,1)S(1)} %get-tuple-element.71), channel_id=1, source_target_pairs={{0,2},{1,3},{2,0},{3,1},{4,6},{5,7},{6,4},{7,5},{8,10},{9,11},{10,... | collective-permute-start | bytes 393224 | tf_op jit(solution)/shard_map/ppermute | solution.py:580
  47.9 10.7 %collective-permute-start.8 = (bf16[2,1,4,8,8,128]{5,4,2,1,0,3:T(8,128)(2,1)S(1)}, bf16[2,1,4,8,8,128]{5,4,2,1,0,3:T(8,128)(2,1)S(1)}, u32[]{:S(2)}, u32[]{:S(2)}) collective-permute-start(bf16[2,1,4,8,8,128]{5,4,2,1,0,3:T(8,128)(2,1)S(1)} %get-tuple-element.72), channel_id=1, source_target_pairs={{0,4},{1,5},{2,6},{3,7},{4,0},{5,1},{6,2},{7,3},{8,12},{9,13},{10,... | collective-permute-start | bytes 393224 | tf_op jit(solution)/shard_map/ppermute | solution.py:580
  49.3 12.2 %collective-permute-start.9 = (bf16[2,1,4,8,8,128]{5,4,2,1,0,3:T(8,128)(2,1)S(1)}, bf16[2,1,4,8,8,128]{5,4,2,1,0,3:T(8,128)(2,1)S(1)}, u32[]{:S(2)}, u32[]{:S(2)}) collective-permute-start(bf16[2,1,4,8,8,128]{5,4,2,1,0,3:T(8,128)(2,1)S(1)} %get-tuple-element.73), channel_id=1, source_target_pairs={{0,6},{1,7},{2,4},{3,5},{4,2},{5,3},{6,0},{7,1},{8,14},{9,15},{10,... | collective-permute-start | bytes 393224 | tf_op jit(solution)/shard_map/ppermute | solution.py:580
  50.5 11.1 %collective-permute-start.10 = (bf16[2,4,1,8,8,128]{5,4,2,1,0,3:T(8,128)(2,1)S(1)}, bf16[2,4,1,8,8,128]{5,4,2,1,0,3:T(8,128)(2,1)}, u32[]{:S(2)}, u32[]{:S(2)}) collective-permute-start(bf16[2,4,1,8,8,128]{5,4,2,1,0,3:T(8,128)(2,1)S(1)} %get-tuple-element.75), channel_id=1, source_target_pairs={{0,64},{8,72},{16,80},{24,88},{32,96},{40,104},{48,112},{56,120},{... | collective-permute-start | bytes 393224 | tf_op jit(solution)/shard_map/ppermute | solution.py:580
  50.5 11.8 %collective-permute-start.11 = (bf16[2,4,1,8,8,128]{5,4,2,1,0,3:T(8,128)(2,1)S(1)}, bf16[2,4,1,8,8,128]{5,4,2,1,0,3:T(8,128)(2,1)}, u32[]{:S(2)}, u32[]{:S(2)}) collective-permute-start(bf16[2,4,1,8,8,128]{5,4,2,1,0,3:T(8,128)(2,1)S(1)} %get-tuple-element.76), channel_id=1, source_target_pairs={{0,128},{8,136},{16,144},{24,152},{32,160},{40,168},{48,176},{56,1... | collective-permute-start | bytes 393224 | tf_op jit(solution)/shard_map/ppermute | solution.py:580
  53.9 11.9 %collective-permute-start.12 = (bf16[2,4,1,8,8,128]{5,4,2,1,0,3:T(8,128)(2,1)S(1)}, bf16[2,4,1,8,8,128]{5,4,2,1,0,3:T(8,128)(2,1)}, u32[]{:S(2)}, u32[]{:S(2)}) collective-permute-start(bf16[2,4,1,8,8,128]{5,4,2,1,0,3:T(8,128)(2,1)S(1)} %get-tuple-element.77), channel_id=1, source_target_pairs={{0,192},{8,200},{16,208},{24,216},{32,224},{40,232},{48,240},{56,2... | collective-permute-start | bytes 393224 | tf_op jit(solution)/shard_map/ppermute | solution.py:580
  67.9 22.7 %collective-permute-start.14 = (bf16[512,128]{1,0:T(8,128)(2,1)}, bf16[512,128]{1,0:T(8,128)(2,1)S(1)}, u32[]{:S(2)}, u32[]{:S(2)}) collective-permute-start(bf16[512,128]{1,0:T(8,128)(2,1)} %bitcast.19), channel_id=1, source_target_pairs={{0,16},{8,24},{16,0},{24,8},{32,48},{40,56},{48,32},{56,40},{64,80... | collective-permute-start | bytes 393224 | tf_op jit(solution)/shard_map/ppermute | solution.py:580
  67.9 22.8 %collective-permute-start.15 = (bf16[512,128]{1,0:T(8,128)(2,1)}, bf16[512,128]{1,0:T(8,128)(2,1)S(1)}, u32[]{:S(2)}, u32[]{:S(2)}) collective-permute-start(bf16[512,128]{1,0:T(8,128)(2,1)} %bitcast.20), channel_id=1, source_target_pairs={{0,24},{8,16},{16,8},{24,0},{32,56},{40,48},{48,40},{56,32},{64,88... | collective-permute-start | bytes 393224 | tf_op jit(solution)/shard_map/ppermute | solution.py:580
  71.3 22.6 %collective-permute-start.16 = (bf16[512,128]{1,0:T(8,128)(2,1)}, bf16[512,128]{1,0:T(8,128)(2,1)S(1)}, u32[]{:S(2)}, u32[]{:S(2)}) collective-permute-start(bf16[512,128]{1,0:T(8,128)(2,1)} %bitcast.21), channel_id=1, source_target_pairs={{0,32},{8,40},{16,48},{24,56},{32,0},{40,8},{48,16},{56,24},{64,96... | collective-permute-start | bytes 393224 | tf_op jit(solution)/shard_map/ppermute | solution.py:580
  75.9 19.5 %collective-permute-start.17 = (bf16[512,128]{1,0:T(8,128)(2,1)S(1)}, bf16[512,128]{1,0:T(8,128)(2,1)S(1)}, u32[]{:S(2)}, u32[]{:S(2)}) collective-permute-start(bf16[512,128]{1,0:T(8,128)(2,1)S(1)} %bitcast.49), channel_id=1, source_target_pairs={{0,40},{8,32},{16,56},{24,48},{32,8},{40,0},{48,24},{56,16},{64,10... | collective-permute-start | bytes 393224 | tf_op jit(solution)/shard_map/ppermute | solution.py:580
  75.9 19.5 %collective-permute-start.18 = (bf16[512,128]{1,0:T(8,128)(2,1)S(1)}, bf16[512,128]{1,0:T(8,128)(2,1)S(1)}, u32[]{:S(2)}, u32[]{:S(2)}) collective-permute-start(bf16[512,128]{1,0:T(8,128)(2,1)S(1)} %bitcast.48), channel_id=1, source_target_pairs={{0,48},{8,56},{16,32},{24,40},{32,16},{40,24},{48,0},{56,8},{64,11... | collective-permute-start | bytes 393224 | tf_op jit(solution)/shard_map/ppermute | solution.py:580
  90.6 10.7 %collective-permute-start.19 = (bf16[512,128]{1,0:T(8,128)(2,1)S(1)}, bf16[512,128]{1,0:T(8,128)(2,1)S(1)}, u32[]{:S(2)}, u32[]{:S(2)}) collective-permute-start(bf16[512,128]{1,0:T(8,128)(2,1)S(1)} %bitcast.51), channel_id=1, source_target_pairs={{0,56},{8,48},{16,40},{24,32},{32,24},{40,16},{48,8},{56,0},{64,12... | collective-permute-start | bytes 393224 | tf_op jit(solution)/shard_map/ppermute | solution.py:580
  90.7 10.6 %collective-permute-start.13 = (bf16[512,128]{1,0:T(8,128)(2,1)S(1)}, bf16[512,128]{1,0:T(8,128)(2,1)S(1)}, u32[]{:S(2)}, u32[]{:S(2)}) collective-permute-start(bf16[512,128]{1,0:T(8,128)(2,1)S(1)} %bitcast.50), channel_id=1, source_target_pairs={{0,8},{8,0},{16,24},{24,16},{32,40},{40,32},{48,56},{56,48},{64,72... | collective-permute-start | bytes 393224 | tf_op jit(solution)/shard_map/ppermute | solution.py:621

commit v5 on v4

--- a/solution.py
+++ b/solution.py
@@ -22,7 +22,8 @@
 CAP = 4
 TAIL = 2
 IN_PIECES = 8
-OUT_PIECES = 9
+OUT_PIECES = 3
+FIRST_ROWS = 6 * CAP
 IN_ROWS = IN_PIECES * CAP + TAIL
 OUT_ROWS = OUT_PIECES * CAP + TAIL
 BLOCK = 512
@@ -306,9 +307,16 @@
 
 
 def first_kernel(
-    in_ref, g_out, lab_ref, sums_ref, x_ref, fq_ref, fk_ref, g_ref, *scratch
+    in_ref, sent_ref, lab_ref, sums_ref, out_ref, x_ref, fq_ref, fk_ref, g_ref, *refs
 ):
+    scratch, out_sem = refs[:-1], refs[-1]
     total = x_ref.shape[1]
+    out_part = out_ref.shape[0] // PARTS
+
+    def emit(part):
+        at = pl.ds(part * out_part, out_part)
+        return pltpu.make_async_copy(out_ref.at[at], sent_ref.at[at], out_sem.at[part])
+
     row = row_iota()
     front = lax.broadcasted_iota(jnp.int32, (8, HD), 1) < HD // 2
 
@@ -341,12 +349,28 @@
     zero = jnp.zeros((1, HD), jnp.float32)
     s0, s1 = run_heads(2, (zero, zero), x_ref, lab_ref, fq_ref, fk_ref, g_ref, *scratch)
     sums_ref[...] = jnp.where(row == 0, s0, jnp.where(row == 1, s1, 0.0))
-    for j in range(6):
-        g_out[j] = g_ref[j].astype(jnp.bfloat16)
+
+    def sort_out(i, carry):
+        at = pl.ds(pl.multiple_of(i * 32, 32), 32)
+        grads = [g_ref[j, at, :] for j in range(6)]
+        pieces = []
+        for u in range(4):
+            for half in range(2):
+                pieces.extend((grad[u * 8 : u * 8 + 8], half * CAP, CAP) for grad in grads)
+        base = pl.multiple_of(i * (8 * FIRST_ROWS), 8 * FIRST_ROWS)
+        out_ref[pl.ds(base, 8 * FIRST_ROWS), :] = jnp.concatenate(lay(pieces), axis=0).astype(jnp.bfloat16)
+        return carry
+
+    loops = total // 32 // PARTS
+    for part in range(PARTS):
+        lax.fori_loop(part * loops, (part + 1) * loops, sort_out, 0, unroll=True)
+        emit(part).start()
+    for part in range(PARTS):
+        emit(part).wait()
 
 
 def last_kernel(
-    here_ref, g_in, lab_ref, sums_ref, factor_ref, *refs, z_size
+    here_ref, lab_ref, sums_ref, factor_ref, *refs, z_size
 ):
     block_refs = refs[:z_size]
     sent_ref, out_ref, x_ref, fq_ref, fk_ref, g_ref = refs[z_size : z_size + 6]
@@ -412,8 +436,7 @@
 
     def sort_out(i, carry):
         at = pl.ds(pl.multiple_of(i * 32, 32), 32)
-        grads = [g_in[j, at, :].astype(jnp.float32) for j in range(6)]
-        grads += [g_ref[j, at, :] for j in range(3)]
+        grads = [g_ref[j, at, :] for j in range(OUT_PIECES)]
         labs = lab_ref[at, :]
         pieces = []
         for u in range(4):
@@ -458,25 +481,27 @@
     return pl.pallas_call(
         first_kernel,
         in_specs=[inside],
-        out_specs=[inside] * 3,
+        out_specs=[pl.BlockSpec(memory_space=pltpu.HBM)] + [inside] * 2,
         out_shape=[
-            jax.ShapeDtypeStruct((6, total, HD), jnp.bfloat16),
+            pltpu.HBM((sources * FIRST_ROWS, HD), jnp.bfloat16),
             jax.ShapeDtypeStruct((total, HD), jnp.float32),
             jax.ShapeDtypeStruct((8, HD), jnp.float32),
         ],
-        scratch_shapes=scratch_of(2, total),
+        scratch_shapes=[pltpu.VMEM((sources * FIRST_ROWS, HD), jnp.bfloat16)]
+        + scratch_of(2, total)
+        + [pltpu.SemaphoreType.DMA((PARTS,))],
         compiler_params=pltpu.CompilerParams(vmem_limit_bytes=ATTEND_LIMIT),
         cost_estimate=pl.CostEstimate(flops=2 * 12 * total * total * HD, bytes_accessed=2**23, transcendentals=2 * total * total),
         name="attend_first",
     )(arrived)
 
 
-def attend_last(grads, labels, sums, factors, blocks, here, sources):
+def attend_last(labels, sums, factors, blocks, here, sources):
     total = sources * CAP
     inside = pl.BlockSpec(memory_space=pltpu.VMEM)
     return pl.pallas_call(
         functools.partial(last_kernel, z_size=len(blocks)),
-        in_specs=[pl.BlockSpec(memory_space=pltpu.SMEM)] + [inside] * (4 + len(blocks)),
+        in_specs=[pl.BlockSpec(memory_space=pltpu.SMEM)] + [inside] * (3 + len(blocks)),
         out_specs=pl.BlockSpec(memory_space=pltpu.HBM),
         out_shape=pltpu.HBM((sources * OUT_ROWS, HD), jnp.bfloat16),
         scratch_shapes=[pltpu.VMEM((sources * OUT_ROWS, HD), jnp.bfloat16)]
@@ -485,17 +510,18 @@
         compiler_params=pltpu.CompilerParams(vmem_limit_bytes=ATTEND_LIMIT),
         cost_estimate=pl.CostEstimate(flops=12 * total * total * HD, bytes_accessed=2**23, transcendentals=total * total),
         name="attend_last",
-    )(here, grads, labels, sums, factors, *blocks)
+    )(here, labels, sums, factors, *blocks)
 
 
 def unpack_kernel(
-    here_ref, in_ref, dq_ref, dk_ref, dv_ref, loss_ref, g_ref, out_sem, *, seq_size
+    here_ref, first_ref, in_ref, dq_ref, dk_ref, dv_ref, loss_ref, g_ref, out_sem, *, seq_size
 ):
     row = row_iota()
     lane = lax.broadcasted_iota(jnp.int32, (8, HD), 1)
     tok_rows = dq_ref.shape[0]
     chunks = tok_rows // 16
     in_rows = in_ref.shape[0] // chunks
+    first_rows = first_ref.shape[0] // chunks
     outs = (dq_ref, dk_ref, dv_ref)
 
     def emit(chunk, index):
@@ -505,15 +531,16 @@
     line = jnp.zeros((1, HD), jnp.float32)
     for chunk in range(chunks):
         block = in_ref[chunk * in_rows : (chunk + 1) * in_rows, :].astype(jnp.float32)
-
-        def starts(tile, dest):
-            return [((tile * 2 + n) * seq_size + dest) * OUT_ROWS for n in range(2)]
+        first_block = first_ref[chunk * first_rows : (chunk + 1) * first_rows, :].astype(jnp.float32)
+
+        def starts(tile, dest, rows):
+            return [((tile * 2 + n) * seq_size + dest) * rows for n in range(2)]
 
         coefs = []
         for tile in range(2):
             extra = None
             for dest in range(seq_size):
-                start, other = [first + OUT_PIECES * CAP for first in starts(tile, dest)]
+                start, other = [first + OUT_PIECES * CAP for first in starts(tile, dest, OUT_ROWS)]
                 upper = shift(block[start // 8 * 8 : start // 8 * 8 + 8], -start)
                 lower = shift(block[other // 8 * 8 : other // 8 * 8 + 8], 4 - other)
                 one = jnp.where(row < 4, upper, lower)
@@ -531,8 +558,13 @@
                     col = (dest * 3 + head) * HD
                     both = []
                     for tile in range(2):
-                        start, other = [first + (head * 3 + index) * CAP for first in starts(tile, dest)]
-                        both.append(join(block, start, other) * coefs[tile])
+                        if head < 2:
+                            rows = starts(tile, dest, FIRST_ROWS)
+                            one = join(first_block, *[at + (head * 3 + index) * CAP for at in rows])
+                        else:
+                            rows = starts(tile, dest, OUT_ROWS)
+                            one = join(block, *[at + index * CAP for at in rows])
+                        both.append(one * coefs[tile])
                     g_ref[index, chunk * 16 : chunk * 16 + 16, col : col + HD] = jnp.concatenate(
                         both, axis=0
                     ).astype(jnp.bfloat16)
@@ -546,14 +578,14 @@
             emit(chunk, index).wait()
 
 
-def unpack(returned, here, tok_rows, seq_size):
+def unpack(first, returned, here, tok_rows, seq_size):
     chunks = tok_rows // 16
     width = seq_size * 3 * HD
     outside = pl.BlockSpec(memory_space=pltpu.HBM)
     grad_shape = jax.ShapeDtypeStruct((tok_rows, width), jnp.bfloat16)
     return pl.pallas_call(
         functools.partial(unpack_kernel, seq_size=seq_size),
-        in_specs=[pl.BlockSpec(memory_space=pltpu.SMEM), pl.BlockSpec(memory_space=pltpu.VMEM)],
+        in_specs=[pl.BlockSpec(memory_space=pltpu.SMEM)] + [pl.BlockSpec(memory_space=pltpu.VMEM)] * 2,
         out_specs=[outside] * 3 + [pl.BlockSpec(memory_space=pltpu.VMEM)],
         out_shape=[grad_shape] * 3 + [jax.ShapeDtypeStruct((1, CLIPS_G), jnp.float32)],
         scratch_shapes=[
@@ -562,7 +594,7 @@
         ],
         compiler_params=pltpu.CompilerParams(vmem_limit_bytes=24 * 2**20),
         name="unpack",
-    )(here, returned)
+    )(here, first, returned)
 
 
 def pick(array, index, dim):
@@ -616,18 +648,22 @@
         + [jnp.broadcast_to(step[:, c : c + 1], (1, HD)) for c in range(CLIPS_G)],
         axis=1,
     )
-    first = attend_first(arrived, devices)
-    near, first = lax.optimization_barrier((blocks[1], first))
+    first, *labels_sums = attend_first(arrived, devices)
+    near, first, labels_sums = lax.optimization_barrier((blocks[1], first, labels_sums))
     blocks[1] = lax.ppermute(near, "dp", [(i, i ^ 1) for i in range(devices // seq_size)])
     s_here, d_here = lax.axis_index("seq"), lax.axis_index("dp")
     places = (lax.rem(d_here, Z_SIZE), lax.div(d_here, Z_SIZE), lax.div(s_here, 2), lax.rem(s_here, 2))
     places = jnp.stack([place.astype(jnp.int32) for place in places])
-    grads = attend_last(*first, factors, blocks, places, devices)
+    first = first.reshape(devices * FIRST_ROWS // CAP, CAP, HD)
+    first = lax.all_to_all(first, ("dp", "seq"), split_axis=0, concat_axis=0, tiled=True)
+    first = first.reshape(devices * FIRST_ROWS, HD)
+    grads = attend_last(*labels_sums, factors, blocks, places, devices)
+    first, grads = lax.optimization_barrier((first, grads))
     grads = grads.reshape(devices * OUT_ROWS // TAIL, TAIL, HD)
     returned = lax.all_to_all(grads, ("dp", "seq"), split_axis=0, concat_axis=0, tiled=True)
     returned = returned.reshape(devices * OUT_ROWS, HD)
     here = lax.axis_index("dp").reshape(1).astype(jnp.int32)
-    return tuple(unpack(returned, here, tok_rows, seq_size))
+    return tuple(unpack(first, returned, here, tok_rows, seq_size))
 
 
 def solution(mesh):

time: 186 us -> 206 us (1.11)
  waiting for transfers between devices: 31.9 us -> 75.9 us
  blocking collectives: 73.5 us -> 37 us
  starting transfers between devices: 46.3 us -> 58.2 us
    all_to_all x1, blocking collectives: 73.5 us -> 37 us  [shards(): lax.all_to_all(grads, ('dp', 'seq'), split_axis=0, concat_axis=0, tiled=T...]
    ppermute x19, waiting for transfers between devices: 31.9 us -> 64.3 us  [send(): return lax.ppermute(array, axis, [(i, i ^ distance) for i in range(whole)])]
    all_to_all x1, waiting for transfers between devices: 0.01 us -> 11.6 us  [shards(): lax.all_to_all(sent, ('dp', 'seq'), split_axis=0, concat_axis=0, tiled=True)]
    all_to_all x0 -> x1, starting transfers between devices: none -> 6.43 us  [shards(): lax.all_to_all(first, ('dp', 'seq'), split_axis=0, concat_axis=0, tiled=T...]
    ppermute x1, starting transfers between devices: 1.17 us -> 4.43 us  [shards(): lax.ppermute(near, 'dp', [(i, i ^ 1) for i in range(devices // seq_size)])]
    ppermute x19, starting transfers between devices: 29.4 us -> 31.7 us  [send(): return lax.ppermute(array, axis, [(i, i ^ distance) for i in range(whole)])]
  transfers between devices with their start and end apart: 21 -> 22, of which waited for: 11 -> 11; matrix products, arithmetic and copies ran while one was open for 4% -> 3% of each run, Pallas kernels for 6% -> 4%
where the time goes in v5:
time: 206 us; the launch traced here: 205 us
  waiting for transfers between devices  75.9 us (37%)
  starting transfers between devices  58.2 us (28%)
  blocking collectives  37 us (18%)
  Pallas kernels  25.4 us (12%)
  local copies, waits for them, and re-layouts  4.73 us (2%)
  other arithmetic  2.23 us (1%)
    ppermute x19, waiting for transfers between devices, send(): return lax.ppermute(array, axis, [(i, i ^ distance) for i in range(whole)])  64.3 us
    all_to_all x1, blocking collectives, shards(): lax.all_to_all(grads, ('dp', 'seq'), split_axis=0, concat_axis=0, tiled=T...  37 us
    ppermute x19, starting transfers between devices, send(): return lax.ppermute(array, axis, [(i, i ^ distance) for i in range(whole)])  31.7 us
    all_to_all x1, starting transfers between devices, shards(): lax.all_to_all(sent, ('dp', 'seq'), split_axis=0, concat_axis=0, tiled=True)  15.7 us
    all_to_all x1, waiting for transfers between devices, shards(): lax.all_to_all(sent, ('dp', 'seq'), split_axis=0, concat_axis=0, tiled=True)  11.6 us
    pallas_call x1, Pallas kernels, attend_first(): pl.pallas_call(first_kernel, in_specs=[inside], out_specs=[pl.BlockSpec(m...  11.5 us
    pallas_call x1, Pallas kernels, attend_last(): pl.pallas_call(functools.partial(last_kernel, z_size=len(blocks)), in_spe...  7.33 us
    all_to_all x1, starting transfers between devices, shards(): lax.all_to_all(first, ('dp', 'seq'), split_axis=0, concat_axis=0, tiled=T...  6.43 us
  transfers between devices with their start and end apart: 22, of which 11 were waited for; matrix products, arithmetic and copies ran while one was open for 3% of the time, Pallas kernels for 4%

profile of v5, /device:TPU:1, one launch (start us, length us, event | category | flops | bytes accessed | tf_op | source)
XLA Modules:
  0.0 205.4 jit_solution(4664074581174723579)
XLA Ops:
  0.6 4.2 %pack.1 = (bf16[8704,128]{1,0:T(8,128)(2,1)}, bf16[4096,128]{1,0:T(8,128)(2,1)}) custom-call(bf16[128,3072]{1,0:T(8,128)(2,1)} %q_ref.1, bf16[128,3072]{1,0:T(8,128)(2,1)} %k_ref.1, bf16[128,3072]{1,0:T(8,128)(2,1)} %v_ref.1, bf16[128,3072]{1,0:T(8,128)(2,1)} %t_ref.1, s32[1,128]{1,0:T(1,128)} %bitcast.57), custom_call_target="tpu_custom_call" | custom-call | tf_op jit(solution)/shard_map/pack/pallas_call | solution.py:149
  4.8 15.7 %all-to-all-start = ((bf16[4352,2,128]{2,1,0:T(2,128)(2,1)}), bf16[4352,2,128]{2,1,0:T(2,128)(2,1)S(1)}, u32[]{:S(2)}, u32[]{:S(2)}) async-start(bf16[4352,2,128]{2,1,0:T(2,128)(2,1)} %bitcast.48), calls=%async_computation | async-start | bytes 4456448 | tf_op jit(solution)/shard_map/all_to_all | solution.py:641
  20.5 2.1 %constant_dynamic-slice_fusion.12 = (bf16[2,1,4,4,8,8,128]{6,5,4,3,2,1,0:T(8,128)(2,1)}, bf16[2,1,4,4,8,8,128]{6,5,4,3,2,1,0:T(8,128)(2,1)S(1)}) fusion(bf16[2,2,4,4,8,8,128]{6,5,4,3,2,1,0:T(8,128)(2,1)} %bitcast.50, s32[]{:T(128)S(6)} %select_n.63, s32[]{:T(128)S(6)} %select_n.62), kind=kLoop, calls=%fused_computation.69 | loop fusion | bytes 2097160 | tf_op jit(solution)/shard_map/dynamic_slice | solution.py:601
  22.6 2.1 %collective-permute-start = (bf16[2,1,4,4,8,8,128]{6,5,4,3,2,1,0:T(8,128)(2,1)}, bf16[2,1,4,4,8,8,128]{6,5,4,3,2,1,0:T(8,128)(2,1)S(1)}, u32[]{:S(2)}, u32[]{:S(2)}) collective-permute-start(bf16[2,1,4,4,8,8,128]{6,5,4,3,2,1,0:T(8,128)(2,1)} %get-tuple-element.118), channel_id=1, source_target_pairs={{0,1},{1,0},{2,3},{3,2},{4,5},{5,4},{6,7},{7,6},{8,9},{9,8},{10,11... | collective-permute-start | bytes 1572872 | tf_op jit(solution)/shard_map/ppermute | solution.py:612
  24.7 1.7 collective-permute-done
  26.6 0.1 fusion.9
  26.7 0.1 copy_bitcast_fusion.2
  26.8 0.1 copy_bitcast_fusion.4
  26.9 0.1 collective-permute-start.1
  27.0 2.0 collective-permute-start.2
  29.1 1.8 collective-permute-start.3
  30.9 2.0 collective-permute-start.5
  32.9 0.6 collective-permute-done.1
  33.5 1.2 collective-permute-start.6
  34.7 4.8 %collective-permute-done.2 = bf16[2,1,4,8,8,128]{5,4,2,1,0,3:T(8,128)(2,1)S(1)} collective-permute-done((bf16[2,1,4,8,8,128]{5,4,2,1,0,3:T(8,128)(2,1)S(1)}, bf16[2,1,4,8,8,128]{5,4,2,1,0,3:T(8,128)(2,1)S(1)}, u32[]{:S(2)}, u32[]{:S(2)}) %collective-permute-start.2) | collective-permute-done | bytes 131104 | tf_op jit(solution)/shard_map/ppermute | solution.py:612
  39.5 3.4 %collective-permute-done.3 = bf16[2,1,4,8,8,128]{5,4,2,1,0,3:T(8,128)(2,1)S(1)} collective-permute-done((bf16[2,1,4,8,8,128]{5,4,2,1,0,3:T(8,128)(2,1)S(1)}, bf16[2,1,4,8,8,128]{5,4,2,1,0,3:T(8,128)(2,1)S(1)}, u32[]{:S(2)}, u32[]{:S(2)}) %collective-permute-start.3) | collective-permute-done | bytes 131104 | tf_op jit(solution)/shard_map/ppermute | solution.py:612
  42.9 3.2 %collective-permute-done.6 = bf16[2,4,1,8,8,128]{5,4,2,1,0,3:T(8,128)(2,1)S(1)} collective-permute-done((bf16[2,4,1,8,8,128]{5,4,2,1,0,3:T(8,128)(2,1)S(1)}, bf16[2,4,1,8,8,128]{5,4,2,1,0,3:T(8,128)(2,1)S(1)}, u32[]{:S(2)}, u32[]{:S(2)}) %collective-permute-start.6) | collective-permute-done | bytes 131104 | tf_op jit(solution)/shard_map/ppermute | solution.py:612
  46.4 0.1 constant_dynamic-slice_fusion
  46.6 0.1 collective-permute-start.10
  46.7 3.3 %collective-permute-start.11 = (bf16[2,4,1,8,8,128]{5,4,2,1,0,3:T(8,128)(2,1)S(1)}, bf16[2,4,1,8,8,128]{5,4,2,1,0,3:T(8,128)(2,1)S(1)}, u32[]{:S(2)}, u32[]{:S(2)}) collective-permute-start(bf16[2,4,1,8,8,128]{5,4,2,1,0,3:T(8,128)(2,1)S(1)} %get-tuple-element.78), channel_id=1, source_target_pairs={{0,128},{8,136},{16,144},{24,152},{32,160},{40,168},{48,176},{56,1... | collective-permute-start | bytes 393224 | tf_op jit(solution)/shard_map/ppermute | solution.py:612
  50.0 0.5 collective-permute-start.12
  50.5 1.2 collective-permute-start.7
  51.7 1.6 collective-permute-start.8
  53.3 1.1 collective-permute-start.9
  54.4 4.7 %collective-permute-done.11 = bf16[2,4,1,8,8,128]{5,4,2,1,0,3:T(8,128)(2,1)S(1)} collective-permute-done((bf16[2,4,1,8,8,128]{5,4,2,1,0,3:T(8,128)(2,1)S(1)}, bf16[2,4,1,8,8,128]{5,4,2,1,0,3:T(8,128)(2,1)S(1)}, u32[]{:S(2)}, u32[]{:S(2)}) %collective-permute-start.11) | collective-permute-done | bytes 131104 | tf_op jit(solution)/shard_map/ppermute | solution.py:612
  59.1 3.8 %collective-permute-done.12 = bf16[2,4,1,8,8,128]{5,4,2,1,0,3:T(8,128)(2,1)S(1)} collective-permute-done((bf16[2,4,1,8,8,128]{5,4,2,1,0,3:T(8,128)(2,1)S(1)}, bf16[2,4,1,8,8,128]{5,4,2,1,0,3:T(8,128)(2,1)S(1)}, u32[]{:S(2)}, u32[]{:S(2)}) %collective-permute-start.12) | collective-permute-done | bytes 131104 | tf_op jit(solution)/shard_map/ppermute | solution.py:612
  63.0 1.1 maximum_bitcast_fusion.1
  64.1 0.1 maximum_bitcast_fusion
  64.2 0.8 fusion.1
  65.0 11.6 %all-to-all-done = bf16[4352,2,128]{2,1,0:T(2,128)(2,1)S(1)} async-done(((bf16[4352,2,128]{2,1,0:T(2,128)(2,1)}), bf16[4352,2,128]{2,1,0:T(2,128)(2,1)S(1)}, u32[]{:S(2)}, u32[]{:S(2)}) %all-to-all-start) | async-done | bytes 2228256 | tf_op jit(solution)/shard_map/all_to_all | solution.py:641
  76.6 11.5 %attend_first.1 = (bf16[6144,128]{1,0:T(8,128)(2,1)}, f32[1024,128]{1,0:T(8,128)S(1)}, f32[8,128]{1,0:T(8,128)S(1)}) custom-call(bf16[8704,128]{1,0:T(8,128)(2,1)S(1)} %bitcast.46), custom_call_target="tpu_custom_call" | custom-call | flops 3221225472 | bytes 8388608 | tf_op jit(solution)/shard_map/attend_first/pallas_call | solution.py:481
  88.1 6.4 %all-to-all-start.1 = ((bf16[1536,4,128]{2,1,0:T(4,128)(2,1)}), bf16[1536,4,128]{2,1,0:T(4,128)(2,1)S(1)}, u32[]{:S(2)}, u32[]{:S(2)}) async-start(bf16[1536,4,128]{2,1,0:T(4,128)(2,1)} %bitcast.49), calls=%async_computation.1 | async-start | bytes 3145728 | tf_op jit(solution)/shard_map/all_to_all | solution.py:658
  94.6 2.8 %collective-permute-start.14 = (bf16[512,128]{1,0:T(8,128)(2,1)}, bf16[512,128]{1,0:T(8,128)(2,1)S(1)}, u32[]{:S(2)}, u32[]{:S(2)}) collective-permute-start(bf16[512,128]{1,0:T(8,128)(2,1)} %bitcast.15), channel_id=1, source_target_pairs={{0,16},{8,24},{16,0},{24,8},{32,48},{40,56},{48,32},{56,40},{64,80... | collective-permute-start | bytes 393224 | tf_op jit(solution)/shard_map/ppermute | solution.py:612
  97.3 1.3 collective-permute-start.15
  98.6 0.7 fusion.13
  99.3 4.9 %collective-permute-start.16 = (bf16[512,128]{1,0:T(8,128)(2,1)S(1)}, bf16[512,128]{1,0:T(8,128)(2,1)S(1)}, u32[]{:S(2)}, u32[]{:S(2)}) collective-permute-start(bf16[512,128]{1,0:T(8,128)(2,1)S(1)} %bitcast.56), channel_id=1, source_target_pairs={{0,32},{8,40},{16,48},{24,56},{32,0},{40,8},{48,16},{56,24},{64,96... | collective-permute-start | bytes 393224 | tf_op jit(solution)/shard_map/ppermute | solution.py:612
  104.2 3.8 %collective-permute-start.18 = (bf16[512,128]{1,0:T(8,128)(2,1)S(1)}, bf16[512,128]{1,0:T(8,128)(2,1)S(1)}, u32[]{:S(2)}, u32[]{:S(2)}) collective-permute-start(bf16[512,128]{1,0:T(8,128)(2,1)S(1)} %bitcast.52), channel_id=1, source_target_pairs={{0,48},{8,56},{16,32},{24,40},{32,16},{40,24},{48,0},{56,8},{64,11... | collective-permute-start | bytes 393224 | tf_op jit(solution)/shard_map/ppermute | solution.py:612
  108.0 35.7 %collective-permute-done.14.refs_2_ = bf16[512,128]{1,0:T(8,128)(2,1)S(1)} collective-permute-done((bf16[512,128]{1,0:T(8,128)(2,1)}, bf16[512,128]{1,0:T(8,128)(2,1)S(1)}, u32[]{:S(2)}, u32[]{:S(2)}) %collective-permute-start.14) | collective-permute-done | bytes 131104 | tf_op jit(solution)/shard_map/ppermute | solution.py:612
  143.7 1.8 collective-permute-start.19
  145.6 4.4 %collective-permute-start.13 = (bf16[512,128]{1,0:T(8,128)(2,1)S(1)}, bf16[512,128]{1,0:T(8,128)(2,1)S(1)}, u32[]{:S(2)}, u32[]{:S(2)}) collective-permute-start(bf16[512,128]{1,0:T(8,128)(2,1)S(1)} %bitcast.54), channel_id=1, source_target_pairs={{0,8},{8,0},{16,24},{24,16},{32,40},{40,32},{48,56},{56,48},{64,72... | collective-permute-start | bytes 393224 | tf_op jit(solution)/shard_map/ppermute | solution.py:653
  150.0 0.1 pad_add_fusion.here_ref
  150.8 0.7 broadcast_in_dim.19
  151.5 0.6 broadcast_in_dim.21
  152.2 3.2 %collective-permute-done.17.refs_5_ = bf16[512,128]{1,0:T(8,128)(2,1)S(1)} collective-permute-done((bf16[512,128]{1,0:T(8,128)(2,1)S(1)}, bf16[512,128]{1,0:T(8,128)(2,1)S(1)}, u32[]{:S(2)}, u32[]{:S(2)}) %collective-permute-start.17) | collective-permute-done | bytes 131104 | tf_op jit(solution)/shard_map/ppermute | solution.py:612
  155.4 2.9 %collective-permute-done.19.refs_7_ = bf16[512,128]{1,0:T(8,128)(2,1)S(1)} collective-permute-done((bf16[512,128]{1,0:T(8,128)(2,1)S(1)}, bf16[512,128]{1,0:T(8,128)(2,1)S(1)}, u32[]{:S(2)}, u32[]{:S(2)}) %collective-permute-start.19) | collective-permute-done | bytes 131104 | tf_op jit(solution)/shard_map/ppermute | solution.py:612
  158.4 7.3 %attend_last.1 = bf16[3584,128]{1,0:T(8,128)(2,1)} custom-call(s32[4]{0:T(128)S(1)} %pad_add_fusion.here_ref, f32[1024,128]{1,0:T(8,128)S(1)} %get-tuple-element.94.lab_ref, f32[8,128]{1,0:T(8,128)S(1)} %get-tuple-element.95.sums_ref, f32[1,384]{1,0:T(1,128)S(1)} %reshape_maximum_fusion.factor_ref, bf16[512,128]{1,0:T(8,128)(2,1)S(1)} %bitcast.47, ...), custom_call_target="tpu_custom_call" | custom-call | flops 1610612736 | bytes 8388608 | tf_op jit(solution)/shard_map/attend_last/pallas_call | solution.py:502
  165.7 37.0 %all_to_all.15 = bf16[1792,2,128]{2,1,0:T(2,128)(2,1)S(1)} all-to-all(bf16[1792,2,128]{2,1,0:T(2,128)(2,1)} %bitcast.51), channel_id=1, replica_groups=mesh['dp'=32,'seq'=8] {'dp','seq'}, dimensions={0} | all-to-all | bytes 1835008 | tf_op jit(solution)/shard_map/all_to_all | solution.py:663
  202.8 2.5 %unpack.1 = (bf16[128,3072]{1,0:T(8,128)(2,1)}, bf16[128,3072]{1,0:T(8,128)(2,1)}, bf16[128,3072]{1,0:T(8,128)(2,1)}, f32[1,2]{1,0:T(1,128)}) custom-call(s32[1]{0:T(128)} %bitcast.here_ref, bf16[6144,128]{1,0:T(8,128)(2,1)S(1)} %bitcast.44, bf16[3584,128]{1,0:T(8,128)(2,1)S(1)} %bitcast.45), custom_call_target="tpu_custom_call" | custom-call | tf_op jit(solution)/shard_map/unpack/pallas_call | solution.py:586
  (37 shorter events, 0.6 us)
Async XLA Ops:
  4.8 71.8 %all-to-all-start = ((bf16[4352,2,128]{2,1,0:T(2,128)(2,1)}), bf16[4352,2,128]{2,1,0:T(2,128)(2,1)S(1)}, u32[]{:S(2)}, u32[]{:S(2)}) async-start(bf16[4352,2,128]{2,1,0:T(2,128)(2,1)} %bitcast.48), calls=%async_computation | async-start | bytes 4456448 | tf_op jit(solution)/shard_map/all_to_all | solution.py:641
  22.6 3.9 %collective-permute-start = (bf16[2,1,4,4,8,8,128]{6,5,4,3,2,1,0:T(8,128)(2,1)}, bf16[2,1,4,4,8,8,128]{6,5,4,3,2,1,0:T(8,128)(2,1)S(1)}, u32[]{:S(2)}, u32[]{:S(2)}) collective-permute-start(bf16[2,1,4,4,8,8,128]{6,5,4,3,2,1,0:T(8,128)(2,1)} %get-tuple-element.118), channel_id=1, source_target_pairs={{0,1},{1,0},{2,3},{3,2},{4,5},{5,4},{6,7},{7,6},{8,9},{9,8},{10,11... | collective-permute-start | bytes 1572872 | tf_op jit(solution)/shard_map/ppermute | solution.py:612
  26.9 6.6 %collective-permute-start.1 = (bf16[2,1,4,8,8,128]{5,4,2,1,0,3:T(8,128)(2,1)S(1)}, bf16[2,1,4,8,8,128]{5,4,2,1,0,3:T(8,128)(2,1)S(1)}, u32[]{:S(2)}, u32[]{:S(2)}) collective-permute-start(bf16[2,1,4,8,8,128]{5,4,2,1,0,3:T(8,128)(2,1)S(1)} %get-tuple-element.57), channel_id=1, source_target_pairs={{0,2},{1,3},{2,0},{3,1},{4,6},{5,7},{6,4},{7,5},{8,10},{9,11},{10,... | collective-permute-start | bytes 393224 | tf_op jit(solution)/shard_map/ppermute | solution.py:612
  27.0 12.5 %collective-permute-start.2 = (bf16[2,1,4,8,8,128]{5,4,2,1,0,3:T(8,128)(2,1)S(1)}, bf16[2,1,4,8,8,128]{5,4,2,1,0,3:T(8,128)(2,1)S(1)}, u32[]{:S(2)}, u32[]{:S(2)}) collective-permute-start(bf16[2,1,4,8,8,128]{5,4,2,1,0,3:T(8,128)(2,1)S(1)} %get-tuple-element.58), channel_id=1, source_target_pairs={{0,4},{1,5},{2,6},{3,7},{4,0},{5,1},{6,2},{7,3},{8,12},{9,13},{10,... | collective-permute-start | bytes 393224 | tf_op jit(solution)/shard_map/ppermute | solution.py:612
  29.1 13.9 %collective-permute-start.3 = (bf16[2,1,4,8,8,128]{5,4,2,1,0,3:T(8,128)(2,1)S(1)}, bf16[2,1,4,8,8,128]{5,4,2,1,0,3:T(8,128)(2,1)S(1)}, u32[]{:S(2)}, u32[]{:S(2)}) collective-permute-start(bf16[2,1,4,8,8,128]{5,4,2,1,0,3:T(8,128)(2,1)S(1)} %get-tuple-element.59), channel_id=1, source_target_pairs={{0,6},{1,7},{2,4},{3,5},{4,2},{5,3},{6,0},{7,1},{8,14},{9,15},{10,... | collective-permute-start | bytes 393224 | tf_op jit(solution)/shard_map/ppermute | solution.py:612
  30.9 12.1 %collective-permute-start.4 = (bf16[2,4,1,8,8,128]{5,4,2,1,0,3:T(8,128)(2,1)S(1)}, bf16[2,4,1,8,8,128]{5,4,2,1,0,3:T(8,128)(2,1)S(1)}, u32[]{:S(2)}, u32[]{:S(2)}) collective-permute-start(bf16[2,4,1,8,8,128]{5,4,2,1,0,3:T(8,128)(2,1)S(1)} %get-tuple-element.61), channel_id=1, source_target_pairs={{0,64},{8,72},{16,80},{24,88},{32,96},{40,104},{48,112},{56,120},{... | collective-permute-start | bytes 393224 | tf_op jit(solution)/shard_map/ppermute | solution.py:612
  30.9 12.1 %collective-permute-start.5 = (bf16[2,4,1,8,8,128]{5,4,2,1,0,3:T(8,128)(2,1)S(1)}, bf16[2,4,1,8,8,128]{5,4,2,1,0,3:T(8,128)(2,1)S(1)}, u32[]{:S(2)}, u32[]{:S(2)}) collective-permute-start(bf16[2,4,1,8,8,128]{5,4,2,1,0,3:T(8,128)(2,1)S(1)} %get-tuple-element.62), channel_id=1, source_target_pairs={{0,128},{8,136},{16,144},{24,152},{32,160},{40,168},{48,176},{56,1... | collective-permute-start | bytes 393224 | tf_op jit(solution)/shard_map/ppermute | solution.py:612
  33.5 12.7 %collective-permute-start.6 = (bf16[2,4,1,8,8,128]{5,4,2,1,0,3:T(8,128)(2,1)S(1)}, bf16[2,4,1,8,8,128]{5,4,2,1,0,3:T(8,128)(2,1)S(1)}, u32[]{:S(2)}, u32[]{:S(2)}) collective-permute-start(bf16[2,4,1,8,8,128]{5,4,2,1,0,3:T(8,128)(2,1)S(1)} %get-tuple-element.63), channel_id=1, source_target_pairs={{0,192},{8,200},{16,208},{24,216},{32,224},{40,232},{48,240},{56,2... | collective-permute-start | bytes 393224 | tf_op jit(solution)/shard_map/ppermute | solution.py:612
  46.6 6.7 %collective-permute-start.10 = (bf16[2,4,1,8,8,128]{5,4,2,1,0,3:T(8,128)(2,1)S(1)}, bf16[2,4,1,8,8,128]{5,4,2,1,0,3:T(8,128)(2,1)S(1)}, u32[]{:S(2)}, u32[]{:S(2)}) collective-permute-start(bf16[2,4,1,8,8,128]{5,4,2,1,0,3:T(8,128)(2,1)S(1)} %get-tuple-element.77), channel_id=1, source_target_pairs={{0,64},{8,72},{16,80},{24,88},{32,96},{40,104},{48,112},{56,120},{... | collective-permute-start | bytes 393224 | tf_op jit(solution)/shard_map/ppermute | solution.py:612
  46.7 12.4 %collective-permute-start.11 = (bf16[2,4,1,8,8,128]{5,4,2,1,0,3:T(8,128)(2,1)S(1)}, bf16[2,4,1,8,8,128]{5,4,2,1,0,3:T(8,128)(2,1)S(1)}, u32[]{:S(2)}, u32[]{:S(2)}) collective-permute-start(bf16[2,4,1,8,8,128]{5,4,2,1,0,3:T(8,128)(2,1)S(1)} %get-tuple-element.78), channel_id=1, source_target_pairs={{0,128},{8,136},{16,144},{24,152},{32,160},{40,168},{48,176},{56,1... | collective-permute-start | bytes 393224 | tf_op jit(solution)/shard_map/ppermute | solution.py:612
  50.0 12.9 %collective-permute-start.12 = (bf16[2,4,1,8,8,128]{5,4,2,1,0,3:T(8,128)(2,1)S(1)}, bf16[2,4,1,8,8,128]{5,4,2,1,0,3:T(8,128)(2,1)S(1)}, u32[]{:S(2)}, u32[]{:S(2)}) collective-permute-start(bf16[2,4,1,8,8,128]{5,4,2,1,0,3:T(8,128)(2,1)S(1)} %get-tuple-element.79), channel_id=1, source_target_pairs={{0,192},{8,200},{16,208},{24,216},{32,224},{40,232},{48,240},{56,2... | collective-permute-start | bytes 393224 | tf_op jit(solution)/shard_map/ppermute | solution.py:612
  50.5 12.4 %collective-permute-start.7 = (bf16[2,1,4,8,8,128]{5,4,2,1,0,3:T(8,128)(2,1)S(1)}, bf16[2,1,4,8,8,128]{5,4,2,1,0,3:T(8,128)(2,1)}, u32[]{:S(2)}, u32[]{:S(2)}) collective-permute-start(bf16[2,1,4,8,8,128]{5,4,2,1,0,3:T(8,128)(2,1)S(1)} %get-tuple-element.73), channel_id=1, source_target_pairs={{0,2},{1,3},{2,0},{3,1},{4,6},{5,7},{6,4},{7,5},{8,10},{9,11},{10,... | collective-permute-start | bytes 393224 | tf_op jit(solution)/shard_map/ppermute | solution.py:612
  51.7 11.2 %collective-permute-start.8 = (bf16[2,1,4,8,8,128]{5,4,2,1,0,3:T(8,128)(2,1)S(1)}, bf16[2,1,4,8,8,128]{5,4,2,1,0,3:T(8,128)(2,1)}, u32[]{:S(2)}, u32[]{:S(2)}) collective-permute-start(bf16[2,1,4,8,8,128]{5,4,2,1,0,3:T(8,128)(2,1)S(1)} %get-tuple-element.74), channel_id=1, source_target_pairs={{0,4},{1,5},{2,6},{3,7},{4,0},{5,1},{6,2},{7,3},{8,12},{9,13},{10,... | collective-permute-start | bytes 393224 | tf_op jit(solution)/shard_map/ppermute | solution.py:612
  53.3 9.7 %collective-permute-start.9 = (bf16[2,1,4,8,8,128]{5,4,2,1,0,3:T(8,128)(2,1)S(1)}, bf16[2,1,4,8,8,128]{5,4,2,1,0,3:T(8,128)(2,1)}, u32[]{:S(2)}, u32[]{:S(2)}) collective-permute-start(bf16[2,1,4,8,8,128]{5,4,2,1,0,3:T(8,128)(2,1)S(1)} %get-tuple-element.75), channel_id=1, source_target_pairs={{0,6},{1,7},{2,4},{3,5},{4,2},{5,3},{6,0},{7,1},{8,14},{9,15},{10,... | collective-permute-start | bytes 393224 | tf_op jit(solution)/shard_map/ppermute | solution.py:612
  88.1 10.5 %copy-start = (f32[1,2]{1,0:T(1,128)S(1)}, f32[1,2]{1,0:T(1,128)}, u32[]{:S(2)}) copy-start(f32[1,2]{1,0:T(1,128)} %param.13) | copy-start | bytes 28
  88.1 10.5 %copy-start.1 = (f32[1,2]{1,0:T(1,128)S(1)}, f32[1,2]{1,0:T(1,128)}, u32[]{:S(2)}) copy-start(f32[1,2]{1,0:T(1,128)} %param.14) | copy-start | bytes 28
  88.1 77.6 %all-to-all-start.1 = ((bf16[1536,4,128]{2,1,0:T(4,128)(2,1)}), bf16[1536,4,128]{2,1,0:T(4,128)(2,1)S(1)}, u32[]{:S(2)}, u32[]{:S(2)}) async-start(bf16[1536,4,128]{2,1,0:T(4,128)(2,1)} %bitcast.49), calls=%async_computation.1 | async-start | bytes 3145728 | tf_op jit(solution)/shard_map/all_to_all | solution.py:658
  94.6 49.2 %collective-permute-start.14 = (bf16[512,128]{1,0:T(8,128)(2,1)}, bf16[512,128]{1,0:T(8,128)(2,1)S(1)}, u32[]{:S(2)}, u32[]{:S(2)}) collective-permute-start(bf16[512,128]{1,0:T(8,128)(2,1)} %bitcast.15), channel_id=1, source_target_pairs={{0,16},{8,24},{16,0},{24,8},{32,48},{40,56},{48,32},{56,40},{64,80... | collective-permute-start | bytes 393224 | tf_op jit(solution)/shard_map/ppermute | solution.py:612
  97.3 48.2 %collective-permute-start.15 = (bf16[512,128]{1,0:T(8,128)(2,1)}, bf16[512,128]{1,0:T(8,128)(2,1)S(1)}, u32[]{:S(2)}, u32[]{:S(2)}) collective-permute-start(bf16[512,128]{1,0:T(8,128)(2,1)} %bitcast.16), channel_id=1, source_target_pairs={{0,24},{8,16},{16,8},{24,0},{32,56},{40,48},{48,40},{56,32},{64,88... | collective-permute-start | bytes 393224 | tf_op jit(solution)/shard_map/ppermute | solution.py:612
  99.3 52.9 %collective-permute-start.16 = (bf16[512,128]{1,0:T(8,128)(2,1)S(1)}, bf16[512,128]{1,0:T(8,128)(2,1)S(1)}, u32[]{:S(2)}, u32[]{:S(2)}) collective-permute-start(bf16[512,128]{1,0:T(8,128)(2,1)S(1)} %bitcast.56), channel_id=1, source_target_pairs={{0,32},{8,40},{16,48},{24,56},{32,0},{40,8},{48,16},{56,24},{64,96... | collective-permute-start | bytes 393224 | tf_op jit(solution)/shard_map/ppermute | solution.py:612
  104.2 51.3 %collective-permute-start.17 = (bf16[512,128]{1,0:T(8,128)(2,1)S(1)}, bf16[512,128]{1,0:T(8,128)(2,1)S(1)}, u32[]{:S(2)}, u32[]{:S(2)}) collective-permute-start(bf16[512,128]{1,0:T(8,128)(2,1)S(1)} %bitcast.53), channel_id=1, source_target_pairs={{0,40},{8,32},{16,56},{24,48},{32,8},{40,0},{48,24},{56,16},{64,10... | collective-permute-start | bytes 393224 | tf_op jit(solution)/shard_map/ppermute | solution.py:612
  104.2 51.3 %collective-permute-start.18 = (bf16[512,128]{1,0:T(8,128)(2,1)S(1)}, bf16[512,128]{1,0:T(8,128)(2,1)S(1)}, u32[]{:S(2)}, u32[]{:S(2)}) collective-permute-start(bf16[512,128]{1,0:T(8,128)(2,1)S(1)} %bitcast.52), channel_id=1, source_target_pairs={{0,48},{8,56},{16,32},{24,40},{32,16},{40,24},{48,0},{56,8},{64,11... | collective-permute-start | bytes 393224 | tf_op jit(solution)/shard_map/ppermute | solution.py:612
  143.7 14.6 %collective-permute-start.19 = (bf16[512,128]{1,0:T(8,128)(2,1)S(1)}, bf16[512,128]{1,0:T(8,128)(2,1)S(1)}, u32[]{:S(2)}, u32[]{:S(2)}) collective-permute-start(bf16[512,128]{1,0:T(8,128)(2,1)S(1)} %bitcast.55), channel_id=1, source_target_pairs={{0,56},{8,48},{16,40},{24,32},{32,24},{40,16},{48,8},{56,0},{64,12... | collective-permute-start | bytes 393224 | tf_op jit(solution)/shard_map/ppermute | solution.py:612
  145.6 12.8 %collective-permute-start.13 = (bf16[512,128]{1,0:T(8,128)(2,1)S(1)}, bf16[512,128]{1,0:T(8,128)(2,1)S(1)}, u32[]{:S(2)}, u32[]{:S(2)}) collective-permute-start(bf16[512,128]{1,0:T(8,128)(2,1)S(1)} %bitcast.54), channel_id=1, source_target_pairs={{0,8},{8,0},{16,24},{24,16},{32,40},{40,32},{48,56},{56,48},{64,72... | collective-permute-start | bytes 393224 | tf_op jit(solution)/shard_map/ppermute | solution.py:653
